TPU v7x, 128 devices: a whole 4x4x4 slice. The times are simulated.
128 devices in a mesh: fsdp: 16 (over y, x), expert: 8 (over z, core).
Axes of the slice: x: 4, y: 4, z: 4, core: 2. Of those that a mesh axis runs over, the one named last changes fastest.
Arguments:
- hidden_in: bfloat16 [8, 2048, 2048], P('expert', 'fsdp'), may hold values from -6 to 6
- cotangent: bfloat16 [8, 2048, 2048], P('expert', 'fsdp'), may hold values from -6 to 6
- segments: int32 [8, 2048], P('expert'), may hold values from 0 to 128, as said below
- routes: int32 [8, 2048, 2], P('expert', 'fsdp'), may hold values from 0 to 7, all different within a row; in each aligned block of 128 rows (0 to 127, 128 to 255, ..., all dimensions but the last counted through in order) at most 42 rows name the same one
- attn_gain: bfloat16 [2048], P('fsdp'), may hold values from 0.099609375 to 1.8984375
- w_query: bfloat16 [2048, 2048], P('fsdp'), may hold values from -0.125 to 0.125
- w_key: bfloat16 [2048, 512], P('fsdp'), may hold values from -0.125 to 0.125
- w_value: bfloat16 [2048, 512], P('fsdp'), may hold values from -0.125 to 0.125
- w_out: bfloat16 [2048, 2048], P('fsdp'), may hold values from -0.5 to 0.5
- ffn_gain: bfloat16 [2048], P('fsdp'), may hold values from 0.099609375 to 1.8984375
- w_router: bfloat16 [2048, 8], P('fsdp'), may hold values from -0.0625 to 0.0625
- shared_gate: bfloat16 [2048, 2816], P('fsdp'), may hold values from -0.125 to 0.125
- shared_up: bfloat16 [2048, 2816], P('fsdp'), may hold values from -0.125 to 0.125
- shared_down: bfloat16 [2816, 2048], P('fsdp'), may hold values from -0.109375 to 0.109375
- expert_gate: bfloat16 [2048, 8, 1408], P('fsdp', 'expert'), may hold values from -0.125 to 0.125
- expert_up: bfloat16 [2048, 8, 1408], P('fsdp', 'expert'), may hold values from -0.125 to 0.125
- expert_down: bfloat16 [1408, 8, 2048], P('fsdp', 'expert'), may hold values from -0.15625 to 0.15625
Outputs:
- layer_out: bfloat16 [8, 2048, 2048], P('expert', 'fsdp')
- grad_input: bfloat16 [8, 2048, 2048], P('expert', 'fsdp')
- grad_attn_gain: float32 [2048], P('fsdp')
- grad_w_query: float32 [2048, 2048], P('fsdp')
- grad_w_key: float32 [2048, 512], P('fsdp')
- grad_w_value: float32 [2048, 512], P('fsdp')
- grad_w_out: float32 [2048, 2048], P('fsdp')
- grad_ffn_gain: float32 [2048], P('fsdp')
- grad_w_router: float32 [2048, 8], P('fsdp')
- grad_shared_gate: float32 [2048, 2816], P('fsdp')
- grad_shared_up: float32 [2048, 2816], P('fsdp')
- grad_shared_down: float32 [2816, 2048], P('fsdp')
- grad_expert_gate: float32 [2048, 8, 1408], P('fsdp', 'expert')
- grad_expert_up: float32 [2048, 8, 1408], P('fsdp', 'expert')
- grad_expert_down: float32 [1408, 8, 2048], P('fsdp', 'expert')
Inputs may be any that keep to these rules, and one draw needn't show every extreme that they name: `segments`: in each sequence the document numbers start at 0 and rise by 0 or 1 from one token to the next; the last token's number is 128. `routes`: each token names 2 different experts; the tokens of one device name no expert more than 42 times.
All inputs are finite; a program needn't handle non-finite values.
Results may differ from a plain program's by a relative error of at most 0.025.
Values may be sent and summed in bfloat16 or wider, within the bound.
No kernel may reach another device: no remote copies, remote signals or barrier semaphores. Data moves between devices by JAX's collectives and lax.ppermute only.
A program may use at most 320 MiB of HBM per device.

v0:
```python
import jax
import jax.numpy as jnp
from jax import lax
from jax.experimental import pallas as pl
from jax.experimental.pallas import tpu as pltpu
from jax.sharding import PartitionSpec as P

D = 2048
H = 16
KV = 4
HD = 128
FF = 1408
SH = 2816
TOPK = 2
TOK = 128
LENGTH = 2048
SEQS = 8
EXPERTS = 8
FSDP = 16
ALL = SEQS * TOK
CAP = 42
SLOTS = SEQS * CAP
SH_ROWS = SH // FSDP
SH_PART = SH_ROWS // EXPERTS
SH_PAD = 24
SH_OWN = FSDP * SH_PAD
QBLOCK = 256

eps_norm = 1e-06
rope_base = 600000.0
masked_fill = -1e30
low = jnp.bfloat16
wide = jnp.float32


def shift_pairs(step):
    return [(z * 2 + c, ((z + step) % 4) * 2 + c) for z in range(4) for c in range(2)]


core_pairs = [(z * 2 + c, z * 2 + 1 - c) for z in range(4) for c in range(2)]


def move_z(block, step):
    return lax.ppermute(block, "expert", shift_pairs(step))


def swap_core(block):
    return lax.ppermute(block, "expert", core_pairs)


def together(*values):
    return lax.optimization_barrier(values)


TOP = TOK // 2


def first_pieces(block):
    return move_z(block, 1), move_z(block, -1)


def other_pieces(block, below, above):
    upper, lower = move_z(below[:TOP], 1), move_z(above[TOP:], -1)
    mine = [block, above, upper, lower, below]
    return mine + [swap_core(piece) for piece in mine]


def gather_pieces(block):
    return other_pieces(block, *first_pieces(block))


PIECES = [(4 * side + block, start) for side in (0, 1) for block, start in ((0, 0), (1, 0), (2, 0), (2, TOP), (3, 0))]


def load_pieces(refs, rows_ref, extra_ref, sems):
    copies = []
    for index, (ref, (block, start)) in enumerate(zip(refs, PIECES)):
        count = min(ref.shape[0], TOK - start)
        copies.append(
            pltpu.make_async_copy(
                ref.at[pl.ds(0, count), :], rows_ref.at[pl.ds(block * TOK + start, count), :], sems.at[2 * index]
            )
        )
        if extra_ref is not None and ref.shape[0] > count:
            copies.append(
                pltpu.make_async_copy(
                    ref.at[pl.ds(count, 16), :], extra_ref.at[pl.ds(block * 16, 16), :], sems.at[2 * index + 1]
                )
            )
    for copy in copies:
        copy.start()
    return copies


def scatter_start(mine, received):
    chip = mine.reshape(4, TOK, -1).astype(wide) + received.reshape(4, TOK, -1).astype(wide)
    from_below = move_z(chip[2, :TOP].astype(low), 1)
    from_above = move_z(chip[2, TOP:].astype(low), -1)
    to_above = jnp.concatenate([chip[1, :TOP] + from_below.astype(wide), chip[1, TOP:]], axis=0)
    to_below = jnp.concatenate([chip[3, :TOP], chip[3, TOP:] + from_above.astype(wide)], axis=0)
    return chip[0], to_above.astype(low), to_below.astype(low)


def scatter_end(own, first, second):
    return own + first.astype(wide) + second.astype(wide)


def scatter_rows(mine, other):
    own, to_above, to_below = scatter_start(mine, swap_core(other))
    return scatter_end(own, move_z(to_above, 1), move_z(to_below, -1))


def exchange(mine, other):
    got = swap_core(other)
    chip = jnp.stack([mine[1:], got[1:]], axis=1)
    return mine[0], got[0], *[move_z(chip[step - 1], step) for step in (1, 2, 3)]


def source_owners(expert):
    return jnp.stack([((expert // 2 - index // 2) % 4) * 2 + ((expert % 2) ^ (index % 2)) for index in range(EXPERTS)])


def relative_owner(expert, block):
    return ((expert // 2 + block % 4) % 4) * 2 + ((expert % 2) ^ (block // 4))


def pack_tiles(block):
    rows, columns = block.shape[0] // 8, block.shape[1] // 128
    tiles = block.reshape(rows, 8, columns, 128).transpose(2, 1, 0, 3)
    return tiles.reshape(columns * 8, rows * 128)


def unpack_tiles(block, count):
    rows, columns = block.shape[1] // 128, block.shape[0] // (8 * count)
    tiles = block.reshape(count, columns, 8, rows, 128).transpose(0, 3, 2, 1, 4)
    return tiles.reshape(count * rows * 8, columns * 128)


def product(left, right, contract):
    return lax.dot_general(left, right, (contract, ((), ())), preferred_element_type=wide)


def mm(left, right):
    return product(left, right, ((1,), (0,)))


def mm_t(left, right):
    return product(left, right, ((1,), (1,)))


def t_mm(left, right):
    return product(left, right, ((0,), (0,)))


def segment_columns(seg_blocks_ref):
    return seg_blocks_ref[...].T


def block_scores(qkv_ref, seg_row_ref, columns, start, reach):
    query = qkv_ref[pl.ds(start, QBLOCK), 0:HD]
    key = qkv_ref[pl.ds(0, reach), HD : 2 * HD]
    scores = mm_t(query, key) * HD ** (-0.5)
    query_pos = start + lax.broadcasted_iota(jnp.int32, (QBLOCK, reach), 0)
    key_pos = lax.broadcasted_iota(jnp.int32, (QBLOCK, reach), 1)
    block = start // TOK
    column = jnp.concatenate([columns[:, block : block + 1], columns[:, block + 1 : block + 2]], axis=0)
    same = column == seg_row_ref[:, pl.ds(0, reach)]
    return jnp.where(same & (query_pos >= key_pos), scores, masked_fill)


def attend_kernel(qkv_ref, seg_row_ref, seg_blocks_ref, mixed_ref, total_ref):
    columns = segment_columns(seg_blocks_ref)
    for block in range(LENGTH // QBLOCK):
        start, reach = block * QBLOCK, (block + 1) * QBLOCK
        scores = block_scores(qkv_ref, seg_row_ref, columns, start, reach)
        largest = jnp.max(scores, axis=-1, keepdims=True)
        exponent = jnp.exp(scores - largest)
        totals = jnp.sum(exponent, axis=-1, keepdims=True)
        probs_low = (exponent * (1.0 / totals)).astype(low)
        value = qkv_ref[pl.ds(0, reach), 2 * HD : 3 * HD]
        mixed_ref[pl.ds(start, QBLOCK), :] = mm(probs_low, value).astype(low)
        total_ref[pl.ds(start, QBLOCK), :] = largest + jnp.log(totals)


def attend_back_kernel(
    qkv_ref, grad_ref, total_ref, seg_row_ref, seg_blocks_ref, cos_ref, sin_ref, out_ref, small_ref, key_acc, value_acc
):
    columns = segment_columns(seg_blocks_ref)
    key_acc[...] = jnp.zeros_like(key_acc)
    value_acc[...] = jnp.zeros_like(value_acc)

    def turn_back(value, rows):
        return value * cos_ref[rows, :] + pltpu.roll(value, HD // 2, 1) * sin_ref[rows, :]

    for block in range(LENGTH // QBLOCK):
        start, reach = block * QBLOCK, (block + 1) * QBLOCK
        rows, span = pl.ds(start, QBLOCK), pl.ds(0, reach)
        scores = block_scores(qkv_ref, seg_row_ref, columns, start, reach)
        probs = jnp.exp(scores - total_ref[rows, :])
        tall = [pl.ds((start // TOK + part) * TALL, TOK) for part in range(QBLOCK // TOK)]
        grad = jnp.concatenate([grad_ref[part, :] for part in tall], axis=0)
        grad_probs = mm_t(grad, qkv_ref[span, 2 * HD : 3 * HD])
        inner = jnp.sum(probs * grad_probs, axis=-1, keepdims=True)
        grad_scores = (probs * (grad_probs - inner)).astype(low)
        scale = HD ** (-0.5)
        grad_query = mm(grad_scores, qkv_ref[span, HD : 2 * HD]) * scale
        out_ref[rows, 0:HD] = turn_back(grad_query, rows).astype(low)
        key_acc[span, :] += t_mm(grad_scores, qkv_ref[rows, 0:HD]) * scale
        value_acc[span, :] += t_mm(probs.astype(low), grad)
    for block in range(LENGTH // QBLOCK):
        rows = pl.ds(block * QBLOCK, QBLOCK)
        out_ref[rows, HD : 2 * HD] = turn_back(key_acc[rows, :], rows).astype(low)
        out_ref[rows, 2 * HD : 3 * HD] = value_acc[rows, :].astype(low)
    small = grad_ref[pl.ds(TOK, 16), :].astype(wide)
    for index in range(1, FSDP):
        small = small + grad_ref[pl.ds(index * TALL + TOK, 16), :].astype(wide)
    small_ref[...] = small


vmem = pl.BlockSpec(memory_space=pltpu.VMEM)
smem = pl.BlockSpec(memory_space=pltpu.SMEM)
anywhere = pl.BlockSpec(memory_space=pl.ANY)
kernel_params = pltpu.CompilerParams(vmem_limit_bytes=48 * 1024 * 1024)


def attend(qkv, seg_row, seg_blocks):
    return pl.pallas_call(
        attend_kernel,
        out_shape=(
            jax.ShapeDtypeStruct((LENGTH, HD), low),
            jax.ShapeDtypeStruct((LENGTH, 1), wide),
        ),
        in_specs=[vmem] * 3,
        out_specs=(vmem, vmem),
        compiler_params=kernel_params,
        cost_estimate=pl.CostEstimate(
            flops=2 * LENGTH * LENGTH * HD, bytes_accessed=4 * LENGTH * HD * 2, transcendentals=LENGTH * LENGTH // 2
        ),
        name="attend",
    )(qkv, seg_row, seg_blocks)


def attend_back(qkv, grad, total, seg_row, seg_blocks, cos_all, sin_all):
    return pl.pallas_call(
        attend_back_kernel,
        out_shape=(jax.ShapeDtypeStruct((LENGTH, 3 * HD), low), jax.ShapeDtypeStruct((16, TOK), wide)),
        in_specs=[vmem] * 7,
        out_specs=(vmem, vmem),
        scratch_shapes=[pltpu.VMEM((LENGTH, HD), wide), pltpu.VMEM((LENGTH, HD), wide)],
        compiler_params=kernel_params,
        cost_estimate=pl.CostEstimate(
            flops=5 * LENGTH * LENGTH * HD, bytes_accessed=8 * LENGTH * HD * 2, transcendentals=LENGTH * LENGTH // 2
        ),
        name="attend_back",
    )(qkv, grad, total, seg_row, seg_blocks, cos_all, sin_all)


ROWS = 256
FF_TILES = [(start, min(256, FF - start)) for start in range(0, FF, 256)]


def params(mebibytes):
    return pltpu.CompilerParams(vmem_limit_bytes=mebibytes * 1024 * 1024)


def cost(flops, moved, special=0):
    return pl.CostEstimate(flops=int(flops), bytes_accessed=int(moved), transcendentals=int(special))


def project_kernel(*refs):
    pieces, (attn_ref, cos_ref, sin_ref) = refs[:10], refs[10:13]
    normed_ref, sent_ref, factor_ref, gains_ref, ids_ref, hidden, sems = refs[13:]
    copies = load_pieces(pieces, hidden, ids_ref, sems)
    pick = lax.broadcasted_iota(jnp.int32, (16, TOK), 0) == lax.broadcasted_iota(jnp.int32, (16, TOK), 1)
    gains_ref[...] = mm_t(pick.astype(wide).astype(low), attn_ref[:, 768:896])
    for copy in copies:
        copy.wait()
    gain = gains_ref[0:1, :]

    @pl.loop(0, ALL // ROWS)
    def step(index):
        rows = pl.ds(index * ROWS, ROWS)
        values = hidden[rows, :].astype(wide)
        factor = lax.rsqrt(jnp.mean(values * values, axis=-1, keepdims=True) + eps_norm)
        factor_ref[rows, :] = factor
        normed = (values * factor * gain).astype(low)
        normed_ref[rows, :] = normed
        raw = mm(normed, attn_ref[:, 0:512])

        def turn(value):
            return (value * cos_ref[...] + pltpu.roll(value, HD // 2, 1) * sin_ref[...]).astype(low)

        key = turn(raw[:, 2 * HD : 3 * HD])
        value = raw[:, 3 * HD :].astype(low)
        for head in range(2):
            query = turn(raw[:, head * HD : (head + 1) * HD])
            for part in range(2):
                place = pl.ds(index * 4 * TOK + (2 * part + head) * TOK, TOK)
                within = slice(part * TOK, (part + 1) * TOK)
                sent_ref[place, 0:HD] = query[within]
                sent_ref[place, HD : 2 * HD] = key[within]
                sent_ref[place, 2 * HD : 3 * HD] = value[within]


def project(pieces, attn_all, cos_two, sin_two):
    return pl.pallas_call(
        project_kernel,
        out_shape=(
            jax.ShapeDtypeStruct((ALL, D), low),
            jax.ShapeDtypeStruct((LENGTH, 3 * HD), low),
            jax.ShapeDtypeStruct((ALL, 1), wide),
            jax.ShapeDtypeStruct((16, D), wide),
            jax.ShapeDtypeStruct((SEQS * 16, D), low),
        ),
        in_specs=[anywhere] * 10 + [vmem] * 3,
        out_specs=tuple([vmem] * 5),
        scratch_shapes=[pltpu.VMEM((ALL, D), low), pltpu.SemaphoreType.DMA((20,))],
        compiler_params=params(40),
        cost_estimate=cost(2.2e9, 16e6),
        name="project",
    )(*pieces, attn_all, cos_two, sin_two)


TALL = TOK + 16


def mix_back_kernel(place_ref, *refs):
    pieces, weight_ref, mixed_ref, small_ref = refs[:10], refs[10], refs[11], refs[12]
    sent_ref, mine_ref, other_ref, grad_ref, sems = refs[13:]
    for index in range(FSDP):
        sent_ref[pl.ds(index * TALL + TOK, 16), :] = small_ref[:, index * TOK : (index + 1) * TOK]
    for copy in load_pieces(pieces, grad_ref, None, sems):
        copy.wait()
    for index in range(ALL // ROWS):
        grad = mm_t(grad_ref[pl.ds(index * ROWS, ROWS), :], weight_ref[...]).astype(low)
        for part in range(2):
            for head in range(2):
                place = pl.ds((index * 4 + 2 * part + head) * TALL, TOK)
                sent_ref[place, :] = grad[part * TOK : (part + 1) * TOK, head * HD : (head + 1) * HD]
    for index in range(EXPERTS):
        columns = pl.ds(pl.multiple_of(place_ref[index] * 256, 256), 256)
        target = mine_ref if index < 4 else other_ref
        target[index % 4] = t_mm(mixed_ref[...], grad_ref[:, columns]).astype(low)


def mix_back(owners, pieces, weight, mixed, small):
    blocks = jax.ShapeDtypeStruct((4, 256, 256), low)
    return pl.pallas_call(
        mix_back_kernel,
        out_shape=(jax.ShapeDtypeStruct((FSDP * TALL, HD), low), blocks, blocks),
        in_specs=[smem] + [anywhere] * 10 + [vmem] * 3,
        out_specs=(vmem, vmem, vmem),
        scratch_shapes=[pltpu.VMEM((ALL, D), low), pltpu.SemaphoreType.DMA((20,))],
        compiler_params=params(60),
        cost_estimate=cost(2.2e9, 10e6),
        name="mix_back",
    )(owners, *pieces, weight, mixed, small)


def collect_kernel(core_ref, grads_ref, query_ref, mine_ref, other_ref):
    first = core_ref[0] == 0

    @pl.loop(0, SEQS)
    def step(index):
        rows = pl.ds(index * TOK, TOK)
        swapped = pl.ds(((index + SEQS // 2) % SEQS) * TOK, TOK)
        one = grads_ref[pl.ds(index * 2 * TOK, TOK), :]
        two = grads_ref[pl.ds(index * 2 * TOK + TOK, TOK), :]
        query_ref[rows, 0:HD] = one[:, :HD]
        query_ref[rows, HD : 2 * HD] = two[:, :HD]
        total = one[:, HD:].astype(wide) + two[:, HD:].astype(wide)
        lower = jnp.concatenate([total[:, : HD // 2], total[:, HD : HD + HD // 2]], axis=1)
        upper = jnp.concatenate([total[:, HD // 2 : HD], total[:, HD + HD // 2 :]], axis=1)
        mine_ref[rows, :] = jnp.where(first, lower, upper)
        other_ref[swapped, :] = jnp.where(first, upper, lower).astype(low)


def collect(core, grads):
    return pl.pallas_call(
        collect_kernel,
        out_shape=(
            jax.ShapeDtypeStruct((ALL, 2 * HD), low),
            jax.ShapeDtypeStruct((ALL, HD), wide),
            jax.ShapeDtypeStruct((ALL, HD), low),
        ),
        in_specs=[smem, vmem],
        out_specs=(vmem, vmem, vmem),
        compiler_params=params(32),
        cost_estimate=cost(1e6, 4e6),
        name="collect",
    )(core, grads)


def qkv_weights_kernel(place_ref, normed_ref, query_ref, mine_ref, got_ref, *refs):
    parts, (out_ref, grad_ref) = refs[:5], refs[5:]
    grad_ref[:, 0 : 2 * HD] = query_ref[...]
    grad_ref[:, 2 * HD : 3 * HD] = (mine_ref[...] + got_ref[...].astype(wide)).astype(low)
    for index in range(EXPERTS):
        step, side = index // 2, index % 2
        rows = pl.ds(pl.multiple_of(place_ref[index] * 256, 256), 256)
        out_ref[rows, 3 * HD : 3 * HD + 256] = parts[step + 1][side] if step else parts[side][...]
    for index in range(D // ROWS):
        rows = pl.ds(index * ROWS, ROWS)
        out_ref[rows, 0 : 3 * HD] = t_mm(normed_ref[:, rows], grad_ref[...]).astype(low)


def qkv_weights(places, normed, query, mine, got, parts):
    return pl.pallas_call(
        qkv_weights_kernel,
        out_shape=(jax.ShapeDtypeStruct((D, 3 * HD + 256), low), jax.ShapeDtypeStruct((ALL, 3 * HD), low)),
        in_specs=[smem] + [vmem] * 9,
        out_specs=(vmem, vmem),
        compiler_params=params(40),
        cost_estimate=cost(1.6e9, 10e6),
        name="qkv_weights",
    )(places, normed, query, mine, got, *parts)


def finish_kernel(shards_ref, query_ref, key_ref, value_ref, out_ref, gain_ref):
    gain = jnp.zeros((TOK, TOK), wide)
    for source in range(EXPERTS):
        query_ref[:, source * 256 : (source + 1) * 256] = shards_ref[source, :, 0:256].astype(wide)
        out_ref[:, source * 256 : (source + 1) * 256] = shards_ref[source, :, 384:640].astype(wide)
        gain = gain + shards_ref[source, :, 640:768].astype(wide)
    for pair in range(KV):
        one = shards_ref[2 * pair, :, 256:384].astype(wide)
        two = shards_ref[2 * pair + 1, :, 256:384].astype(wide)
        columns = slice(pair * HD, (pair + 1) * HD)
        key_ref[:, columns] = jnp.concatenate([one[:, : HD // 2], two[:, : HD // 2]], axis=1)
        value_ref[:, columns] = jnp.concatenate([one[:, HD // 2 :], two[:, HD // 2 :]], axis=1)
    gain_ref[...] = gain


def finish(shards):
    widths = (H * HD, KV * HD, KV * HD, H * HD, TOK)
    return pl.pallas_call(
        finish_kernel,
        out_shape=tuple(jax.ShapeDtypeStruct((TOK, width), wide) for width in widths),
        in_specs=[vmem],
        out_specs=tuple([vmem] * 5),
        compiler_params=params(32),
        cost_estimate=cost(1e6, 4e6),
        name="finish",
    )(shards)


def finish_dense_kernel(shards_ref, spread_ref, spread_rows_ref, gate_ref, up_ref, down_ref, left, rows_in):
    width = SH_OWN // 2
    for source in range(EXPERTS):
        for part in range(4):
            left[part * TOK : (part + 1) * TOK, source * width : (source + 1) * width] = shards_ref[
                source, :, part * width : (part + 1) * width
            ]
        packed = shards_ref[source, :, 2 * SH_OWN : 3 * SH_OWN].astype(wide)
        rows_in[source * SH_PAD : (source + 1) * SH_PAD, :] = pack_rows(packed)
    for start in range(0, SH // 2, 256):
        count = min(256, SH // 2 - start)
        both = mm(left[...], spread_ref[:, start : start + count])
        for part in range(4):
            target = gate_ref if part < 2 else up_ref
            begin = (part % 2) * (SH // 2) + start
            target[:, begin : begin + count] = both[part * TOK : (part + 1) * TOK]
    down_ref[...] = mm(spread_rows_ref[...], rows_in[...].astype(low))


def finish_dense(shards, spread, spread_rows):
    shapes = [(TOK, SH), (TOK, SH), (SH_ROWS, D)]
    return pl.pallas_call(
        finish_dense_kernel,
        out_shape=tuple(jax.ShapeDtypeStruct(shape, wide) for shape in shapes),
        in_specs=[vmem] * 3,
        out_specs=tuple([vmem] * 3),
        scratch_shapes=[
            pltpu.VMEM((4 * TOK, EXPERTS * SH_OWN // 2), low),
            pltpu.VMEM((EXPERTS * SH_PAD, D), wide),
        ],
        compiler_params=params(40),
        cost_estimate=cost(2.2e9, 12e6),
        name="finish_dense",
    )(shards, spread, spread_rows)


def halves(value):
    upper = value.astype(low)
    return upper, (value - upper.astype(wide)).astype(low)


def silu_parts(gate_value):
    sig = 1.0 / (1.0 + jnp.exp(-gate_value))
    return sig, gate_value * sig


def swiglu_back(sig, act, up_value, grad):
    return (grad * up_value * (sig + act * (1.0 - sig))).astype(low), (grad * act).astype(low)


def pack_rows(block):
    count, width = block.shape[0] // 8, block.shape[1] // 128
    return jnp.concatenate(
        [
            jnp.concatenate(
                [block[8 * i : 8 * i + 8, 128 * j : 128 * j + 128] for i in range(count)], axis=1
            )
            for j in range(width)
        ],
        axis=0,
    )


def slab(buffer, out_ref, sems, step, start):
    target = out_ref.at[pl.ds(step * ROWS, ROWS), pl.ds(start, buffer.shape[2])]
    return pltpu.make_async_copy(buffer.at[step % 2], target, sems.at[step % 2])


def send_slabs(tokens_ref, grad_ref, down_rows, out_ref, buffer, sems, start):
    width = grad_ref.shape[1]
    count = width // 2 // FSDP
    for step in range(D // ROWS):
        slot = step % 2
        if step >= 2:
            slab(buffer, out_ref, sems, step - 2, start).wait()
        buffer[slot, :, 0:width] = t_mm(tokens_ref[:, pl.ds(step * ROWS, ROWS)], grad_ref[...]).astype(low)
        down = down_rows(step)
        for part in range(2):
            packed = pack_rows(down[part * count : (part + 1) * count]).astype(low)
            buffer[slot, part * TOK : (part + 1) * TOK, width:] = packed
        slab(buffer, out_ref, sems, step, start).start()
    for step in (D // ROWS - 2, D // ROWS - 1):
        slab(buffer, out_ref, sems, step, start).wait()


def ffn_kernel(*refs):
    expert_ref, slots_hbm, slots_t_hbm, routes_ref, router_hbm = refs[:5]
    pieces, cot_pieces, pack_ref = refs[5:15], refs[15:25], refs[25]
    grad_mine, grad_other, gates_ref = refs[26:29]
    outs = refs[29:37]
    normed_ref, cot_ref, grad_ref = refs[37:40]
    kept = refs[40:48]
    hidden_s, grad_s, incoming, hidden_e, gated, grad_rows, grad_e, w_down_s = kept
    w_in_s, w_in, w_down, slots_ref, slots_t_ref = refs[48:53]
    raw, gate_parts, grad_in, piece_sems, cot_sems, sems, out_sems = refs[53:]
    base = 3 * SH_OWN
    half_d = D // 2

    def stage_shared(part):
        return pltpu.make_async_copy(
            pack_ref.at[pl.ds(part * half_d, half_d), pl.ds(2 * SH_OWN, SH_OWN)],
            grad_ref.at[:, pl.ds(FF + part * SH_OWN, SH_OWN)],
            sems.at[part],
        )

    def stage_down(part):
        return pltpu.make_async_copy(
            pack_ref.at[pl.ds(part * half_d, half_d), pl.ds(base + 2 * FF, FF)],
            grad_ref.at[:, pl.ds(0, FF)],
            sems.at[2 + part],
        )

    def unpack(target, pair, row, start, width):
        count = 2 * width // FSDP
        both = [
            pack_rows(grad_ref[row + part * TOK : row + (part + 1) * TOK, start : start + width].astype(wide))
            for part in range(2)
        ]
        target[pair * count : (pair + 1) * count, :] = jnp.concatenate(both, axis=0).astype(low)

    copies = [
        pltpu.make_async_copy(router_hbm, w_in_s.at[:, pl.ds(2 * SH_OWN, 128)], sems.at[4]),
        pltpu.make_async_copy(pack_ref.at[:, pl.ds(0, 2 * SH_OWN)], w_in_s.at[:, pl.ds(0, 2 * SH_OWN)], sems.at[5]),
        pltpu.make_async_copy(slots_hbm, slots_ref, sems.at[6]),
        pltpu.make_async_copy(pack_ref.at[:, pl.ds(base, 2 * FF)], w_in, sems.at[7]),
        pltpu.make_async_copy(slots_t_hbm, slots_t_ref, sems.at[8]),
    ]
    stage_shared(0).start()
    stage_shared(1).start()
    copies[0].start()
    copies[1].start()
    piece_copies = load_pieces(pieces, normed_ref, None, piece_sems)
    cot_copies = load_pieces(cot_pieces, cot_ref, None, cot_sems)
    stage_down(0).start()
    for copy in copies[2:]:
        copy.start()

    def send(index):
        copy = pltpu.make_async_copy(kept[index], outs[index], out_sems.at[index])
        copy.start()
        return copy

    expert = expert_ref[0]
    lane = lax.broadcasted_iota(jnp.int32, (ROWS, 128), 1)
    for part in range(2):
        stage_shared(part).wait()
        for pair in range(4):
            unpack(w_down_s, part * 4 + pair, pair * 2 * TOK, FF + part * SH_OWN, SH_OWN)
    for copy in piece_copies + cot_copies + copies[:2]:
        copy.wait()
    stage_down(0).wait()
    for step in range(ALL // ROWS):
        unpack(w_down, step, step * 2 * TOK, 0, FF)
        rows = pl.ds(step * ROWS, ROWS)
        both = mm(normed_ref[rows, :], w_in_s[...])
        sig, act = silu_parts(both[:, :SH_OWN])
        up = both[:, SH_OWN : 2 * SH_OWN]
        hidden_s[rows, :] = (act * up).astype(low)
        grad_hidden = mm_t(cot_ref[rows, :], w_down_s[...])
        grad_gate, grad_up = swiglu_back(sig, act, up, grad_hidden)
        grad_s[rows, 0:SH_OWN] = grad_gate
        grad_s[rows, SH_OWN : 2 * SH_OWN] = grad_up
        logits = both[:, 2 * SH_OWN :]
        first, second = routes_ref[rows, 0:1], routes_ref[rows, 1:2]
        chosen_first = jnp.sum(jnp.where(lane == first + 2, logits, 0.0), axis=1, keepdims=True)
        chosen_second = jnp.sum(jnp.where(lane == second + 2, logits, 0.0), axis=1, keepdims=True)
        gate_first = 1.0 / (1.0 + jnp.exp(chosen_second - chosen_first))
        gate_second = 1.0 / (1.0 + jnp.exp(chosen_first - chosen_second))
        here = jnp.where(first == expert, gate_first, 0.0) + jnp.where(second == expert, gate_second, 0.0)
        upper, lower = halves(here)
        parts = jnp.where(lane == 0, upper.astype(wide), 0.0) + jnp.where(lane == 1, lower.astype(wide), 0.0)
        gate_parts[rows, :] = parts.astype(low)
        if step == 0:
            both_gates = jnp.where(lane == 0, gate_first, 0.0) + jnp.where(lane == 1, gate_second, 0.0)
            gates_ref[...] = both_gates[:TOK]
    stage_down(1).start()
    sent = [send(0), send(1), send(7)]
    copies[2].wait()
    for step in range(D // ROWS):
        columns = pl.ds(step * ROWS, ROWS)
        incoming[:, columns] = mm(slots_ref[...], normed_ref[:, columns]).astype(low)
        grad_rows[:, columns] = mm(slots_ref[...], cot_ref[:, columns]).astype(low)
    slot_parts = mm(slots_ref[...], gate_parts[...])
    slot_gate = slot_parts[:, 0:1] + slot_parts[:, 1:2]
    sent.append(send(2))
    copies[3].wait()
    stage_down(1).wait()
    for step in range(4):
        unpack(w_down, 4 + step, step * 2 * TOK, 0, FF)
    for step in range(2 * FF // ROWS):
        columns = pl.ds(step * ROWS, ROWS)
        raw[:, columns] = mm(incoming[...], w_in[:, columns])
    for start, width in FF_TILES:
        gate, up = raw[:, start : start + width], raw[:, FF + start : FF + start + width]
        hidden_e[:, start : start + width] = (silu_parts(gate)[1] * up).astype(low)
    sent.append(send(3))
    slot_grad = jnp.zeros((SLOTS, 1), wide)
    for step in range(D // ROWS):
        columns = pl.ds(step * ROWS, ROWS)
        rows = mm(hidden_e[...], w_down[:, columns]).astype(low).astype(wide)
        cot = grad_rows[:, columns].astype(wide)
        gated[:, columns] = (rows * slot_gate).astype(low)
        grad_rows[:, columns] = (cot * slot_gate).astype(low)
        slot_grad = slot_grad + jnp.sum(rows * cot, axis=1, keepdims=True)
    sent += [send(4), send(5)]
    for start, width in FF_TILES:
        grad_hidden = mm_t(grad_rows[...], w_down[pl.ds(start, width), :])
        sig, act = silu_parts(raw[:, start : start + width])
        grad_gate, grad_up = swiglu_back(sig, act, raw[:, FF + start : FF + start + width], grad_hidden)
        grad_e[:, start : start + width] = grad_gate
        grad_e[:, FF + start : FF + start + width] = grad_up
    sent.append(send(6))
    for step in range(D // ROWS):
        columns = pl.ds(step * ROWS, ROWS)
        grad_in[:, columns] = mm_t(grad_e[...], w_in[columns, :]).astype(low)
    upper, lower = halves(slot_grad)
    slot_lane = lax.broadcasted_iota(jnp.int32, (SLOTS, 128), 1)
    slot_parts = (
        jnp.where(slot_lane == expert, upper.astype(wide), 0.0)
        + jnp.where(slot_lane == expert + 8, lower.astype(wide), 0.0)
    ).astype(low)
    copies[4].wait()
    half = ALL // 2
    for side, target in ((1, grad_other), (0, grad_mine)):
        for step in range(half // ROWS):
            rows = pl.ds(side * half + step * ROWS, ROWS)
            for tile in range(D // 512):
                columns = pl.ds(tile * 512, 512)
                grad_ref[rows, columns] = (
                    mm_t(grad_s[rows, :], w_in_s[columns, 0 : 2 * SH_OWN])
                    + mm(slots_t_ref[rows, :], grad_in[:, columns])
                ).astype(low)
            grad_ref[rows, D : D + 128] = mm(slots_t_ref[rows, :], slot_parts).astype(low)
        copy = pltpu.make_async_copy(grad_ref.at[pl.ds(side * half, half), :], target, sems.at[9 + side])
        copy.start()
        sent.append(copy)
    for copy in sent:
        copy.wait()


def ffn(expert, slots, slots_t, routes, router, pieces, cot_pieces, pack):
    kept = [(ALL, SH_OWN), (ALL, 2 * SH_OWN), (SLOTS, D), (SLOTS, FF), (SLOTS, D), (SLOTS, D), (SLOTS, 2 * FF)]
    kept.append((SH_OWN, D))
    grads = [(ALL // 2, D + 128)] * 2
    return pl.pallas_call(
        ffn_kernel,
        out_shape=tuple(
            [jax.ShapeDtypeStruct(shape, low) for shape in grads]
            + [jax.ShapeDtypeStruct((TOK, 128), wide)]
            + [jax.ShapeDtypeStruct(shape, low) for shape in kept]
        ),
        in_specs=[smem, anywhere, anywhere, vmem] + [anywhere] * 22,
        out_specs=tuple([anywhere] * 2 + [vmem] + [anywhere] * 8),
        scratch_shapes=[pltpu.VMEM((ALL, D), low), pltpu.VMEM((ALL, D), low), pltpu.VMEM((ALL, D + 128), low)]
        + [pltpu.VMEM(shape, low) for shape in kept]
        + [
            pltpu.VMEM((D, 2 * SH_OWN + 128), low),
            pltpu.VMEM((D, 2 * FF), low),
            pltpu.VMEM((FF, D), low),
            pltpu.VMEM((SLOTS, ALL), low),
            pltpu.VMEM((ALL, SLOTS), low),
            pltpu.VMEM((SLOTS, 2 * FF), wide),
            pltpu.VMEM((ALL, 128), low),
            pltpu.VMEM((SLOTS, D), low),
            pltpu.SemaphoreType.DMA((20,)),
            pltpu.SemaphoreType.DMA((20,)),
            pltpu.SemaphoreType.DMA((11,)),
            pltpu.SemaphoreType.DMA((8,)),
        ],
        compiler_params=params(60),
        cost_estimate=cost(27e9, 50e6, 1e6),
        name="ffn",
    )(expert, slots, slots_t, routes, router, *pieces, *cot_pieces, pack)


def shared_weights_kernel(*refs):
    pieces, cot_pieces, hidden_ref, grad_ref = refs[:10], refs[10:20], refs[20], refs[21]
    out_ref, normed_ref, cot_ref, buffer, down, piece_sems, cot_sems, sems = refs[22:]
    cot_copies = load_pieces(cot_pieces, cot_ref, None, cot_sems)
    copies = load_pieces(pieces, normed_ref, None, piece_sems)
    for copy in cot_copies:
        copy.wait()
    for tile in range(D // ROWS):
        part = pl.ds(tile * ROWS, ROWS)
        down[:, part] = t_mm(hidden_ref[...], cot_ref[:, part])
    for copy in copies:
        copy.wait()
    count = 2 * SH_PAD
    send_slabs(
        normed_ref, grad_ref, lambda step: down[step * count : (step + 1) * count, :], out_ref, buffer, sems, 0
    )


def shared_weights(pieces, cot_pieces, hidden, grad):
    return pl.pallas_call(
        shared_weights_kernel,
        out_shape=jax.ShapeDtypeStruct((D, 3 * SH_OWN + 3 * FF), low),
        in_specs=[anywhere] * 20 + [vmem] * 2,
        out_specs=anywhere,
        scratch_shapes=[
            pltpu.VMEM((ALL, D), low),
            pltpu.VMEM((ALL, D), low),
            pltpu.VMEM((2, ROWS, 3 * SH_OWN), low),
            pltpu.VMEM((SH_OWN, D), wide),
            pltpu.SemaphoreType.DMA((20,)),
            pltpu.SemaphoreType.DMA((20,)),
            pltpu.SemaphoreType.DMA((2,)),
        ],
        compiler_params=params(60),
        cost_estimate=cost(5e9, 18e6),
        name="shared_weights",
    )(*pieces, *cot_pieces, hidden, grad)


def expert_weights_kernel(_, incoming_ref, hidden_ref, grad_rows_ref, grad_ref, out_ref, buffer, sems):
    def down_rows(step):
        count = 2 * FF // FSDP
        return t_mm(hidden_ref[:, step * count : (step + 1) * count], grad_rows_ref[...])

    send_slabs(incoming_ref, grad_ref, down_rows, out_ref, buffer, sems, 3 * SH_OWN)


def expert_weights(*operands):
    return pl.pallas_call(
        expert_weights_kernel,
        out_shape=jax.ShapeDtypeStruct((D, 3 * SH_OWN + 3 * FF), low),
        in_specs=[anywhere] + [vmem] * 4,
        out_specs=anywhere,
        scratch_shapes=[pltpu.VMEM((2, ROWS, 3 * FF), low), pltpu.SemaphoreType.DMA((2,))],
        input_output_aliases={0: 0},
        compiler_params=params(48),
        cost_estimate=cost(6e9, 24e6),
        name="expert_weights",
    )(*operands)


def out_rows_kernel(place_ref, *refs):
    parts, out_ref = refs[:5], refs[5]
    for index in range(EXPERTS):
        step, side = index // 2, index % 2
        columns = pl.ds(pl.multiple_of(place_ref[index] * 256, 256), 256)
        out_ref[:, columns] = parts[step + 1][side] if step else parts[side][...]


def out_rows(places, parts):
    return pl.pallas_call(
        out_rows_kernel,
        out_shape=jax.ShapeDtypeStruct((256, D), low),
        in_specs=[smem] + [vmem] * 5,
        out_specs=vmem,
        compiler_params=params(32),
        cost_estimate=cost(0, 2e6),
        name="out_rows",
    )(places, *parts)


def back_two_kernel(
    own_ref, first_ref, second_ref, middle_ref, cot_ref, gains_ref, gates_ref, routes_ref, block_ref, grad_ref, total_ref, logits_ref
):
    total = own_ref[...] + first_ref[...].astype(wide) + second_ref[...].astype(wide)
    lane = lax.broadcasted_iota(jnp.int32, (TOK, 128), 1)
    extra = total[:, D:]
    first, second = routes_ref[:, 0:1], routes_ref[:, 1:2]

    def taken(route):
        return jnp.sum(jnp.where((lane == route) | (lane == route + 8), extra, 0.0), axis=1, keepdims=True)

    gate_first, gate_second = gates_ref[:, 0:1], gates_ref[:, 1:2]
    taken_first, taken_second = taken(first), taken(second)
    inner = gate_first * taken_first + gate_second * taken_second
    chosen_first, chosen_second = gate_first * (taken_first - inner), gate_second * (taken_second - inner)
    logits = jnp.where(lane == first, chosen_first, 0.0) + jnp.where(lane == second, chosen_second, 0.0)
    grad = total[:, :D]
    for index in range(EXPERTS):
        grad = grad + logits[:, index : index + 1] * gains_ref[2 + index : 3 + index, :]
    middle = middle_ref[...]
    factor = lax.rsqrt(jnp.mean(middle * middle, axis=-1, keepdims=True) + eps_norm)
    scaled = grad * gains_ref[1:2, :]
    mean = jnp.mean(scaled * middle, axis=-1, keepdims=True)
    result = cot_ref[...].astype(wide) + factor * scaled - middle * (factor * factor * factor * mean)
    grad_ref[...] = result
    block_ref[...] = result.astype(low)
    total_ref[...] = grad
    logits_ref[...] = logits


def back_two(*operands):
    return pl.pallas_call(
        back_two_kernel,
        out_shape=(
            jax.ShapeDtypeStruct((TOK, D), low),
            jax.ShapeDtypeStruct((TOK, D), wide),
            jax.ShapeDtypeStruct((TOK, D), wide),
            jax.ShapeDtypeStruct((TOK, 128), wide),
        ),
        in_specs=[vmem] * 8,
        out_specs=(vmem, vmem, vmem, vmem),
        compiler_params=params(32),
        cost_estimate=cost(1e7, 6e6),
        name="back_two",
    )(*operands)


def small_rows_kernel(total_ref, logits_ref, middle_ref, gains_ref, out_ref):
    middle = middle_ref[...]
    factor = lax.rsqrt(jnp.mean(middle * middle, axis=-1, keepdims=True) + eps_norm)
    gain_upper, gain_lower = halves(jnp.sum(total_ref[...] * middle * factor, axis=0, keepdims=True))
    normed = (middle * factor * gains_ref[1:2, :]).astype(low)
    logit_upper, logit_lower = halves(logits_ref[...].T[0:EXPERTS, :])
    router = mm(logit_upper, normed) + mm(logit_lower, normed)
    small = [gain_upper.astype(wide), gain_lower.astype(wide), router, jnp.zeros((6, D), wide)]
    out_ref[...] = jnp.concatenate(small, axis=0).astype(low)


def small_rows(*operands):
    return pl.pallas_call(
        small_rows_kernel,
        out_shape=jax.ShapeDtypeStruct((16, D), low),
        in_specs=[vmem] * 4,
        out_specs=vmem,
        compiler_params=params(32),
        cost_estimate=cost(1e7, 3e6),
        name="small_rows",
    )(*operands)


def norm_factor(values):
    return lax.rsqrt(jnp.mean(values * values, axis=-1, keepdims=True) + eps_norm)


def norm_back(values, factor, gain, grad):
    scaled = grad * gain
    inner = jnp.mean(scaled * values, axis=-1, keepdims=True)
    return factor * scaled - values * (factor * factor * factor * inner)


def per_device(
    hidden_in,
    cotangent,
    segments,
    routes,
    attn_gain,
    w_query,
    w_key,
    w_value,
    w_out,
    ffn_gain,
    w_router,
    shared_gate,
    shared_up,
    shared_down,
    expert_gate,
    expert_up,
    expert_down,
):
    expert = lax.axis_index("expert")
    z, core = expert // 2, expert % 2
    place = lax.axis_index("fsdp")

    misc = jnp.concatenate(
        [attn_gain[:, None], ffn_gain[:, None], w_router, jnp.zeros((TOK, 118), low)], axis=1
    )
    attn_pack = jnp.concatenate(
        [
            lax.dynamic_slice_in_dim(w_query, 256 * expert, 256, 1),
            lax.dynamic_slice_in_dim(w_key, HD * z, HD, 1),
            lax.dynamic_slice_in_dim(w_value, HD * z, HD, 1),
            lax.dynamic_slice_in_dim(w_out, 256 * expert, 256, 1),
            misc,
        ],
        axis=1,
    )
    attn_all = lax.all_gather(attn_pack, "fsdp", axis=0, tiled=True)
    half_in, half_out = SH // 2, SH_OWN // 2
    sel_column = jnp.arange(half_out)
    picked = SH_ROWS * (sel_column // SH_PAD) + SH_PART * expert + sel_column % SH_PAD
    picked = jnp.where(sel_column % SH_PAD < SH_PART, picked, -1)
    select = (jnp.arange(half_in)[:, None] == picked[None, :]).astype(low)
    own_shared = mm(
        jnp.concatenate(
            [shared_gate[:, :half_in], shared_gate[:, half_in:], shared_up[:, :half_in], shared_up[:, half_in:]],
            axis=0,
        ),
        select,
    ).astype(low)
    own_down = jnp.pad(
        lax.dynamic_slice_in_dim(shared_down, SH_PART * expert, SH_PART, 0),
        ((0, SH_PAD - SH_PART), (0, 0)),
    )
    ffn_pack = jnp.concatenate(
        [
            own_shared[:TOK],
            own_shared[TOK : 2 * TOK],
            own_shared[2 * TOK : 3 * TOK],
            own_shared[3 * TOK :],
            pack_tiles(own_down),
            expert_gate[:, 0],
            expert_up[:, 0],
            pack_tiles(expert_down[:, 0]),
        ],
        axis=1,
    )
    ffn_all = lax.all_gather(ffn_pack, "fsdp", axis=0, tiled=True)

    ids = jnp.concatenate(
        [
            segments.astype(low),
            jnp.pad(routes[0].reshape(1, TOK * TOPK), ((0, 0), (0, LENGTH - TOK * TOPK))).astype(low),
            jnp.zeros((14, LENGTH), low),
        ],
        axis=0,
    )
    hidden_pieces = gather_pieces(jnp.concatenate([hidden_in[0], ids], axis=0))
    cot_block, *hidden_pieces = together(cotangent[0], *hidden_pieces)
    cot_pieces = gather_pieces(cot_block)

    inverse_freq = rope_base ** (-jnp.arange(HD // 2, dtype=wide) * 2.0 / HD)
    angles = jnp.arange(LENGTH).astype(wide)[:, None] * inverse_freq[None, :]
    cosine, sine = jnp.cos(angles), jnp.sin(angles)
    cos_all = jnp.concatenate([cosine, cosine], axis=1)
    sin_back = jnp.concatenate([sine, -sine], axis=1)
    cos_own = lax.dynamic_slice_in_dim(cos_all, place * TOK, TOK, 0)
    sin_own = -lax.dynamic_slice_in_dim(sin_back, place * TOK, TOK, 0)
    cos_two, sin_two = jnp.concatenate([cos_own, cos_own]), jnp.concatenate([sin_own, sin_own])
    put_row = jnp.arange(SH_PAD * EXPERTS * FSDP // 2)
    source, within = put_row // half_out, put_row % half_out
    target = SH_ROWS * (within // SH_PAD) + SH_PART * source + within % SH_PAD
    target = jnp.where(within % SH_PAD < SH_PART, target, -1)
    spread = (target[:, None] == jnp.arange(half_in)[None, :]).astype(low)
    put_row = jnp.arange(EXPERTS * SH_PAD)
    target = SH_PART * (put_row // SH_PAD) + put_row % SH_PAD
    target = jnp.where(put_row % SH_PAD < SH_PART, target, -1)
    spread_rows = (jnp.arange(SH_ROWS)[:, None] == target[None, :]).astype(low)
    attn_all, cos_two, sin_two, cos_all, sin_back, spread, spread_rows = together(
        attn_all, cos_two, sin_two, cos_all, sin_back, spread, spread_rows
    )
    normed_one, sent, factor_one, gains, ids_all = project(hidden_pieces, attn_all, cos_two, sin_two)
    qkv = lax.all_to_all(sent, "fsdp", split_axis=0, concat_axis=0, tiled=True)

    ids_all = ids_all.reshape(SEQS, 16, D)
    seg_row = lax.dynamic_slice_in_dim(ids_all[:, 0].astype(wide), place // 2, 1, 0)
    seg_blocks = jnp.pad(seg_row.reshape(FSDP, TOK), ((0, TOK - FSDP), (0, 0)))
    route_all = ids_all[:, 1, : TOK * TOPK].astype(jnp.int32).reshape(ALL, TOPK)
    hit = jnp.any(route_all == expert, axis=1).astype(wide)
    order = jnp.arange(ALL)
    rank = mm(hit.astype(low)[None, :], (order[:, None] < order[None, :]).astype(low))
    slot_bool = (rank.astype(jnp.int32) == jnp.arange(SLOTS)[:, None]) & (hit > 0.5)[None, :]
    slots = slot_bool.astype(low)
    slots_t = slot_bool.T.astype(low)
    out_columns = attn_all[:, 512:768].reshape(EXPERTS, 256, 256)
    owners = jnp.stack([relative_owner(expert, block) for block in range(EXPERTS)])
    out_blocks = [lax.dynamic_index_in_dim(out_columns, owners[block], 0) for block in range(EXPERTS)]
    out_mine, out_other = jnp.concatenate(out_blocks[:4]), jnp.concatenate(out_blocks[4:])
    out_mine, out_other, _ = together(out_mine, out_other, sent)
    w_out_own = out_rows(source_owners(expert), exchange(out_mine, out_other))
    router = attn_all[:, 768:896]
    is_first = core == 0
    kv_weight = attn_all[:, 256:512].reshape(D, 2, 2, HD // 2)
    kv_weight = jnp.where(is_first, kv_weight[:, :, 0], kv_weight[:, :, 1]).reshape(D, HD)
    qkv_weight = jnp.concatenate([attn_all[:, :256], kv_weight], axis=1)
    route_own = route_all[:TOK]
    qkv, seg_row, seg_blocks, route_all, slots, slots_t, w_out_own, router, qkv_weight, route_own, *cot_pieces = together(
        qkv, seg_row, seg_blocks, route_all, slots, slots_t, w_out_own, router, qkv_weight, route_own, *cot_pieces
    )
    mixed_head, log_total = attend(qkv, seg_row, seg_blocks)
    mixed = (
        lax.all_to_all(mixed_head, "fsdp", split_axis=0, concat_axis=0, tiled=True)
        .reshape(SEQS, 2, TOK, HD)
        .transpose(0, 2, 1, 3)
        .reshape(ALL, 2 * HD)
    )
    own_hidden = hidden_in[0].astype(wide)
    half = ALL // 2
    middle = own_hidden + scatter_rows(
        mm(mixed[:half], w_out_own).astype(low), mm(mixed[half:], w_out_own).astype(low)
    )
    factor_two = norm_factor(middle)
    gain_one, gain_two = gains[0:1], gains[1:2]
    normed_block = (middle * factor_two * gain_two).astype(low)

    base = 3 * SH_OWN
    normed_pieces = gather_pieces(normed_block)
    (
        grad_mine,
        grad_other,
        gates,
        hidden_shared,
        grad_shared,
        incoming,
        hidden_expert,
        gated_rows,
        grad_rows,
        grad_expert,
        shared_down_w,
    ) = ffn(expert[None], slots, slots_t, route_all, router, normed_pieces, cot_pieces, ffn_all)
    received = swap_core(grad_other)
    ffn_grads = shared_weights(normed_pieces, cot_pieces, hidden_shared, grad_shared)
    received, ffn_grads = together(received, ffn_grads)
    own_grad, to_above, to_below = scatter_start(grad_mine, received)
    to_above, to_below, ffn_grads = together(to_above, to_below, ffn_grads)
    from_below, from_above = move_z(to_above, 1), move_z(to_below, -1)
    ffn_grads = expert_weights(ffn_grads, incoming, hidden_expert, grad_rows, grad_expert)
    from_below, from_above, ffn_grads = together(from_below, from_above, ffn_grads)
    ffn_sums = lax.psum_scatter(ffn_grads, "fsdp", scatter_dimension=0, tiled=True)
    back_block, grad_middle, grad_two, grad_logits = back_two(
        own_grad, from_below, from_above, middle, cotangent[0], gains, gates, route_own
    )
    back_block, hidden_shared, gated_rows = together(back_block, hidden_shared, gated_rows)
    below, above = first_pieces(back_block)
    small = small_rows(grad_two, grad_logits, middle, gains)
    result_other = (mm(hidden_shared[half:], shared_down_w) + mm(slots_t[half:], gated_rows)).astype(low)
    result_mine = (mm(hidden_shared[:half], shared_down_w) + mm(slots_t[:half], gated_rows)).astype(low)
    below, above, result_other, result_mine, small = together(below, above, result_other, result_mine, small)
    back_pieces = other_pieces(back_block, below, above)

    sent_back, out_mine, out_other = mix_back(owners, back_pieces, w_out_own, mixed, small)
    grad_head = lax.all_to_all(sent_back, "fsdp", split_axis=0, concat_axis=0, tiled=True)
    grads_head, small_sums = attend_back(qkv, grad_head, log_total, seg_row, seg_blocks, cos_all, sin_back)
    grads_qkv = lax.all_to_all(grads_head, "fsdp", split_axis=0, concat_axis=0, tiled=True)
    result_other, result_mine, _ = together(result_other, result_mine, sent_back)
    result_got = swap_core(result_other)
    result_got, out_mine, out_other = together(result_got, out_mine, out_other)
    out_parts = exchange(out_mine, out_other)
    result_own, to_above, to_below = scatter_start(result_mine, result_got)
    result_own = scatter_end(result_own, move_z(to_above, 1), move_z(to_below, -1))
    layer_out = (middle + result_own).astype(low)
    grads_qkv, layer_out, *out_parts = together(grads_qkv, layer_out, *out_parts)

    grad_query, kv_mine, kv_other = collect(core[None], grads_qkv)
    attn_grads, grad_qkv = qkv_weights(
        source_owners(expert), normed_one, grad_query, kv_mine, swap_core(kv_other), out_parts
    )
    attn_parts = lax.all_to_all(attn_grads, "fsdp", split_axis=0, concat_axis=0, tiled=True)

    grad_normed_other = mm_t(grad_qkv[half:], qkv_weight).astype(low)
    grad_normed_mine = mm_t(grad_qkv[:half], qkv_weight).astype(low)
    own_grad_one, to_above, to_below = scatter_start(grad_normed_mine, swap_core(grad_normed_other))
    attn_parts, to_above, to_below = together(attn_parts, to_above, to_below)
    own_grad_one = scatter_end(own_grad_one, move_z(to_above, 1), move_z(to_below, -1))
    grad_input = (grad_middle + norm_back(own_hidden, factor_one[:TOK], gain_one, own_grad_one)).astype(low)
    attn_sums = jnp.sum(attn_parts.reshape(FSDP, TOK, 3 * HD + 256).astype(wide), axis=0)

    own_weight = lax.dynamic_slice_in_dim(qkv_weight, place * TOK, TOK, 0)
    gain_part = jnp.sum(attn_sums[:, : 3 * HD] * own_weight.astype(wide), axis=1, keepdims=True)
    gain_upper, gain_lower = halves(gain_part / attn_gain.astype(wide)[:, None])
    small = [gain_upper, gain_lower, small_sums.T.astype(low), jnp.zeros((TOK, 110), low)]
    shards = jnp.concatenate([attn_sums.astype(low), *small], axis=1)

    ffn_sums, _ = together(ffn_sums, to_above)
    shared_shards = lax.all_gather(ffn_sums[:, :base], "expert", axis=0)
    shared_shards, shards = together(shared_shards, shards)
    attn_shards = lax.all_gather(shards, "expert", axis=0)
    grad_shared_gate, grad_shared_up, grad_shared_down = finish_dense(shared_shards, spread, spread_rows)
    grad_w_query, grad_w_key, grad_w_value, grad_w_out, small = finish(attn_shards)
    grad_expert_gate = ffn_sums[:, base : base + FF].astype(wide)[:, None]
    grad_expert_up = ffn_sums[:, base + FF : base + 2 * FF].astype(wide)[:, None]
    grad_expert_down = unpack_tiles(ffn_sums[:, base + 2 * FF :], 1).astype(wide)[:, None]
    return (
        layer_out[None],
        grad_input[None],
        small[:, 0] + small[:, 1],
        grad_w_query,
        grad_w_key,
        grad_w_value,
        grad_w_out,
        small[:, 2] + small[:, 3],
        small[:, 4 : 4 + EXPERTS],
        grad_shared_gate,
        grad_shared_up,
        grad_shared_down,
        grad_expert_gate,
        grad_expert_up,
        grad_expert_down,
    )


def solution(mesh):
    in_specs = (
        P("expert", "fsdp", None),
        P("expert", "fsdp", None),
        P("expert", None),
        P("expert", "fsdp", None),
        P("fsdp"),
        P("fsdp", None),
        P("fsdp", None),
        P("fsdp", None),
        P("fsdp", None),
        P("fsdp"),
        P("fsdp", None),
        P("fsdp", None),
        P("fsdp", None),
        P("fsdp", None),
        P("fsdp", "expert", None),
        P("fsdp", "expert", None),
        P("fsdp", "expert", None),
    )
    out_specs = (
        P("expert", "fsdp", None),
        P("expert", "fsdp", None),
        P("fsdp"),
        P("fsdp", None),
        P("fsdp", None),
        P("fsdp", None),
        P("fsdp", None),
        P("fsdp"),
        P("fsdp", None),
        P("fsdp", None),
        P("fsdp", None),
        P("fsdp", None),
        P("fsdp", "expert", None),
        P("fsdp", "expert", None),
        P("fsdp", "expert", None),
    )
    return jax.shard_map(
        per_device, mesh=mesh, in_specs=in_specs, out_specs=out_specs, check_vma=False
    )
```

profile of v0, /device:TPU:0, one launch (start us, length us, event | category | flops | bytes accessed | tf_op | source)
XLA Modules:
  0.0 592.4 jit_solution(12563338502661848752)
XLA Ops:
  16.3 4.2 collective-permute-start
  23.3 13.2 %collective-permute-done.1.refs_4_ = bf16[144,2048]{1,0:T(8,128)(2,1)S(1)} collective-permute-done((bf16[144,2048]{1,0:T(8,128)(2,1)S(1)}, bf16[144,2048]{1,0:T(8,128)(2,1)S(1)}, u32[]{:S(2)}, u32[]{:S(2)}) %collective-permute-start.1) | collective-permute-done | bytes 589856 | tf_op jit(solution)/shard_map/ppermute | solution.py:44
  37.9 3.2 collective-permute-start.3
  41.7 5.7 multiply_sine_fusion
  55.8 3.9 pad_maximum_fusion.1
  59.6 10.4 %collective-permute-done.14.refs_19_.refs_14_ = bf16[128,2048]{1,0:T(8,128)(2,1)} collective-permute-done((bf16[128,2048]{1,0:T(8,128)(2,1)S(1)}, bf16[128,2048]{1,0:T(8,128)(2,1)}, u32[]{:S(2)}, u32[]{:S(2)}) %collective-permute-start.14) | collective-permute-done | bytes 524320 | tf_op jit(solution)/shard_map/ppermute | solution.py:44
  73.4 3.2 collective-permute-start.16
  83.9 8.5 %project.1 = (bf16[1024,2048]{1,0:T(8,128)(2,1)}, bf16[2048,384]{1,0:T(8,128)(2,1)}, f32[1024,1]{1,0:T(8,128)S(1)}, f32[16,2048]{1,0:T(8,128)S(1)}, bf16[128,2048]{1,0:T(8,128)(2,1)S(1)}) custom-call(bf16[144,2048]{1,0:T(8,128)(2,1)S(1)} %fusion.31.refs_0_, bf16[144,2048]{1,0:T(8,128)(2,1)S(1)} %collective-permute-done.refs_1_, ...), custom_call_target="tpu_custom_call" | custom-call | flops 2200000000 | bytes 16000000 | tf_op jit(solution)/shard_map/project/pallas_call | solution.py:306
  94.6 7.0 %all-to-all-start = ((bf16[16,128,384]{2,1,0:T(8,128)(2,1)}), bf16[16,128,384]{2,1,0:T(8,128)(2,1)}, u32[]{:S(2)}, u32[]{:S(2)}) async-start(bf16[16,128,384]{2,1,0:T(8,128)(2,1)} %bitcast.4), calls=%async_computation | async-start | bytes 3145728 | tf_op jit(solution)/shard_map/all_to_all | solution.py:984
  125.4 9.6 %collective-permute-done.10.refs_2_ = bf16[2,256,256]{2,1,0:T(8,128)(2,1)S(1)} collective-permute-done((bf16[2,256,256]{2,1,0:T(8,128)(2,1)S(1)}, bf16[2,256,256]{2,1,0:T(8,128)(2,1)S(1)}, u32[]{:S(2)}, u32[]{:S(2)}) %collective-permute-start.10) | collective-permute-done | bytes 262176 | tf_op jit(solution)/shard_map/ppermute | solution.py:44
  144.3 8.3 %attend.1 = (bf16[2048,128]{1,0:T(8,128)(2,1)S(1)}, f32[2048,1]{1,0:T(8,128)S(1)}) custom-call(bf16[2048,384]{1,0:T(8,128)(2,1)} %bitcast.5.qkv_ref, f32[1,2048]{1,0:T(1,128)S(1)} %fusion.119.seg_row_ref, f32[128,128]{1,0:T(8,128)S(1)} %pad.14.seg_blocks_ref), custom_call_target="tpu_custom_call" | custom-call | flops 1073741824 | bytes 2097152 | tf_op jit(solution)/shard_map/attend/pallas_call | solution.py:227
  152.6 25.3 %all_to_all.56 = bf16[16,128,128]{2,1,0:T(8,128)(2,1)S(1)} all-to-all(bf16[16,128,128]{2,1,0:T(8,128)(2,1)S(1)} %bitcast.240), channel_id=1, replica_groups=mesh['fsdp'=16,'expert'=8] {'fsdp'}, dimensions={0} | all-to-all | bytes 1048576 | tf_op jit(solution)/shard_map/all_to_all | solution.py:1013
  180.6 3.1 collective-permute-done.22
  188.2 6.3 %collective-permute-done.23 = bf16[64,2048]{1,0:T(8,128)(2,1)S(1)} collective-permute-done((bf16[64,2048]{1,0:T(8,128)(2,1)S(1)}, bf16[64,2048]{1,0:T(8,128)(2,1)S(1)}, u32[]{:S(2)}, u32[]{:S(2)}) %collective-permute-start.23) | collective-permute-done | bytes 262176 | tf_op jit(solution)/shard_map/ppermute | solution.py:44
  197.8 10.3 %collective-permute-done.26 = bf16[128,2048]{1,0:T(8,128)(2,1)S(1)} collective-permute-done((bf16[128,2048]{1,0:T(8,128)(2,1)S(1)}, bf16[128,2048]{1,0:T(8,128)(2,1)S(1)}, u32[]{:S(2)}, u32[]{:S(2)}) %collective-permute-start.26) | collective-permute-done | bytes 524320 | tf_op jit(solution)/shard_map/ppermute | solution.py:44
  208.1 3.5 collective-permute-done.24
  212.3 3.2 collective-permute-start.27
  215.5 9.8 %collective-permute-done.28.refs_9_.refs_4_ = bf16[128,2048]{1,0:T(8,128)(2,1)S(1)} collective-permute-done((bf16[128,2048]{1,0:T(8,128)(2,1)S(1)}, bf16[128,2048]{1,0:T(8,128)(2,1)S(1)}, u32[]{:S(2)}, u32[]{:S(2)}) %collective-permute-start.28) | collective-permute-done | bytes 524320 | tf_op jit(solution)/shard_map/ppermute | solution.py:44
  225.6 3.2 collective-permute-start.30
  229.0 4.0 collective-permute-done.29.refs_7_.refs_2_
  238.2 42.9 %ffn.1 = (bf16[512,2176]{1,0:T(8,128)(2,1)}, bf16[512,2176]{1,0:T(8,128)(2,1)}, f32[128,128]{1,0:T(8,128)}, bf16[1024,384]{1,0:T(8,128)(2,1)}, bf16[1024,768]{1,...) custom-call(s32[1]{0:T(128)} %bitcast.35.refs_0_, ...), custom_call_target="tpu_custom_call" | custom-call | flops 27000000512 | bytes 50000000 | tf_op jit(solution)/shard_map/ffn/pallas_call | solution.py:691
  281.7 14.4 %shared_weights.1._ = bf16[2048,5376]{1,0:T(8,128)(2,1)} custom-call(bf16[128,2048]{1,0:T(8,128)(2,1)} %copy-done.59, bf16[128,2048]{1,0:T(8,128)(2,1)} %copy-done.65, bf16[64,2048]{1,0:T(8,128)(2,1)} %copy-done.74, bf16[64,2048]{1,0:T(8,128)(2,1)} %copy-done.75, bf16[128,2048]{1,0:T(8,128)(2,1)} %copy-done.64, bf16[128,2048]{1,0:T(8,128)(2,1)} %copy-done.68, ...), custom_call_target="tpu_custom_call" | custom-call | flops 5000000000 | bytes 18000000 | tf_op jit(solution)/shard_map/shared_weights/pallas_call | solution.py:741
  299.2 3.8 collective-permute-start.38
  302.9 6.1 %collective-permute-done.38 = bf16[64,2176]{1,0:T(8,128)(2,1)S(1)} collective-permute-done((bf16[64,2176]{1,0:T(8,128)(2,1)S(1)}, bf16[64,2176]{1,0:T(8,128)(2,1)S(1)}, u32[]{:S(2)}, u32[]{:S(2)}) %collective-permute-start.38) | collective-permute-done | bytes 278560 | tf_op jit(solution)/shard_map/ppermute | solution.py:44
  309.0 3.4 collective-permute-done.37
  314.2 3.4 collective-permute-start.40
  317.6 12.7 %expert_weights.1 = bf16[2048,5376]{1,0:T(8,128)(2,1)} custom-call(bf16[2048,5376]{1,0:T(8,128)(2,1)} %shared_weights.1._, bf16[336,2048]{1,0:T(8,128)(2,1)S(1)} %copy-done.10, bf16[336,1408]{1,0:T(8,128)(2,1)S(1)} %copy-done.15, bf16[336,2048]{1,0:T(8,128)(2,1)S(1)} %copy-done.11, bf16[336,2816]{1,0:T(8,128)(2,1)S(1)} %copy-done.7), custom_call_target="tpu_custom_call", output_to_operand_aliasing={{}: (0, {})} | custom-call | flops 6000000000 | bytes 24000000 | tf_op jit(solution)/shard_map/expert_weights/pallas_call | solution.py:770
  335.2 3.2 collective-permute-start.42
  351.0 3.3 collective-permute-start.44
  354.4 3.9 collective-permute-done.43.refs_2_
  362.5 7.4 %mix_back.1 = (bf16[2304,128]{1,0:T(8,128)(2,1)}, bf16[4,256,256]{2,1,0:T(8,128)(2,1)}, bf16[4,256,256]{2,1,0:T(8,128)(2,1)}) custom-call(s32[8]{0:T(128)} %stack.95.place_ref, bf16[128,2048]{1,0:T(8,128)(2,1)} %get-tuple-element.186.refs_0_, bf16[128,2048]{1,0:T(8,128)(2,1)} %collective-permute-done.42.refs_1_, ...), custom_call_target="tpu_custom_call" | custom-call | flops 2200000000 | bytes 10000000 | tf_op jit(solution)/shard_map/mix_back/pallas_call | solution.py:348
  370.3 23.7 %all_to_all.57 = bf16[16,144,128]{2,1,0:T(8,128)(2,1)S(1)} all-to-all(bf16[16,144,128]{2,1,0:T(8,128)(2,1)} %bitcast.263), channel_id=1, replica_groups=mesh['fsdp'=16,'expert'=8] {'fsdp'}, dimensions={0} | all-to-all | bytes 1179648 | tf_op jit(solution)/shard_map/all_to_all | solution.py:1063
  396.5 10.5 %attend_back.1 = (bf16[2048,384]{1,0:T(8,128)(2,1)S(1)}, f32[16,128]{1,0:T(8,128)S(1)}) custom-call(bf16[2048,384]{1,0:T(8,128)(2,1)} %bitcast.5.qkv_ref, bf16[2304,128]{1,0:T(8,128)(2,1)S(1)} %bitcast.239, f32[2048,1]{1,0:T(8,128)S(1)} %copy-done.46, f32[1,2048]{1,0:T(1,128)S(1)} %fusion.119.seg_row_ref, f32[128,128]{1,0:T(8,128)S(1)} %copy-done.41, ...), custom_call_target="tpu_custom_call" | custom-call | flops 2684354560 | bytes 4194304 | tf_op jit(solution)/shard_map/attend_back/pallas_call | solution.py:244
  408.1 3.7 all-to-all-start.3
  411.9 3.2 convert_add_fusion.2
  419.7 5.5 collective-permute-done.51
  425.4 3.1 collective-permute-start.54
  430.0 4.4 collective-permute-start.57
  435.1 11.4 %collective-permute-done.54 = bf16[128,2048]{1,0:T(8,128)(2,1)S(1)} collective-permute-done((bf16[128,2048]{1,0:T(8,128)(2,1)S(1)}, bf16[128,2048]{1,0:T(8,128)(2,1)S(1)}, u32[]{:S(2)}, u32[]{:S(2)}) %collective-permute-start.54) | collective-permute-done | bytes 524320 | tf_op jit(solution)/shard_map/ppermute | solution.py:44
  449.1 4.1 collective-permute-done.56.refs_2_
  462.3 5.0 qkv_weights.1
  470.1 6.6 %all-to-all-start.4 = ((bf16[16,128,640]{2,1,0:T(8,128)(2,1)}), bf16[16,128,640]{2,1,0:T(8,128)(2,1)}, u32[]{:S(2)}, u32[]{:S(2)}) async-start(bf16[16,128,640]{2,1,0:T(8,128)(2,1)} %bitcast.83), calls=%async_computation.4 | async-start | bytes 5242880 | tf_op jit(solution)/shard_map/all_to_all | solution.py:1079
  483.0 6.2 %collective-permute-done.62 = bf16[64,2048]{1,0:T(8,128)(2,1)S(1)} collective-permute-done((bf16[64,2048]{1,0:T(8,128)(2,1)S(1)}, bf16[64,2048]{1,0:T(8,128)(2,1)S(1)}, u32[]{:S(2)}, u32[]{:S(2)}) %collective-permute-start.62) | collective-permute-done | bytes 262176 | tf_op jit(solution)/shard_map/ppermute | solution.py:44
  491.5 31.9 %all-to-all-done.4 = bf16[16,128,640]{2,1,0:T(8,128)(2,1)} async-done(((bf16[16,128,640]{2,1,0:T(8,128)(2,1)}), bf16[16,128,640]{2,1,0:T(8,128)(2,1)}, u32[]{:S(2)}, u32[]{:S(2)}) %all-to-all-start.4) | async-done | bytes 2621472 | tf_op jit(solution)/shard_map/all_to_all | solution.py:1079
  529.7 18.8 %all-gather.11.cloned.1.call-done = bf16[1024,1152]{1,0:T(8,128)(2,1)} async-done(((bf16[128,1152]{1,0:T(8,128)(2,1)}), bf16[1024,1152]{1,0:T(8,128)(2,1)}) %all-gather.11.cloned.1.call-update) | async-done | bytes 2359312 | tf_op jit(solution)/shard_map/all_gather | solution.py:1096
  550.9 12.8 %collective-permute-done.64 = bf16[128,2048]{1,0:T(8,128)(2,1)S(1)} collective-permute-done((bf16[128,2048]{1,0:T(8,128)(2,1)}, bf16[128,2048]{1,0:T(8,128)(2,1)S(1)}, u32[]{:S(2)}, u32[]{:S(2)}) %collective-permute-start.64) | collective-permute-done | bytes 524320 | tf_op jit(solution)/shard_map/ppermute | solution.py:44
  563.7 3.2 collective-permute-done.63
  576.5 4.6 finish_dense.1
  (431 shorter events, 167.6 us)
Async XLA Ops:
  7.2 69.4 %all-gather.7.cloned.1.call-start = ((), (), s32[]{:S(2)}) async-start(), calls=%async_computation.6 | async-start | bytes 3899392 | tf_op jit(solution)/shard_map/all_gather | solution.py:919
  12.3 225.9 %all-gather.9.cloned.1.call-start = ((), (), s32[]{:S(2)}) async-start(), calls=%async_computation.7 | async-start | bytes 23396352 | tf_op jit(solution)/shard_map/all_gather | solution.py:949
  16.3 20.9 %collective-permute-start = (bf16[144,2048]{1,0:T(8,128)(2,1)S(1)}, bf16[144,2048]{1,0:T(8,128)(2,1)S(1)}, u32[]{:S(2)}, u32[]{:S(2)}) collective-permute-start(bf16[144,2048]{1,0:T(8,128)(2,1)S(1)} %fusion.31.refs_0_), channel_id=1, source_target_pairs={{0,6},{1,7},{2,0},{3,1},{4,2},{5,3},{6,4},{7,5},{8,14},{9,15},{10,... | collective-permute-start | bytes 1769480 | tf_op jit(solution)/shard_map/ppermute | solution.py:44
  20.5 16.0 %collective-permute-start.1 = (bf16[144,2048]{1,0:T(8,128)(2,1)S(1)}, bf16[144,2048]{1,0:T(8,128)(2,1)S(1)}, u32[]{:S(2)}, u32[]{:S(2)}) collective-permute-start(bf16[144,2048]{1,0:T(8,128)(2,1)S(1)} %fusion.31.refs_0_), channel_id=1, source_target_pairs={{0,2},{1,3},{2,4},{3,5},{4,6},{5,7},{6,0},{7,1},{8,10},{9,11},{10,... | collective-permute-start | bytes 1769480 | tf_op jit(solution)/shard_map/ppermute | solution.py:44
  20.5 29.2 %collective-permute-start.4 = (bf16[144,2048]{1,0:T(8,128)(2,1)S(1)}, bf16[144,2048]{1,0:T(8,128)(2,1)S(1)}, u32[]{:S(2)}, u32[]{:S(2)}) collective-permute-start(bf16[144,2048]{1,0:T(8,128)(2,1)S(1)} %fusion.31.refs_0_), channel_id=1, source_target_pairs={{0,1},{1,0},{2,3},{3,2},{4,5},{5,4},{6,7},{7,6},{8,9},{9,8},{10,11... | collective-permute-start | bytes 1769480 | tf_op jit(solution)/shard_map/ppermute | solution.py:48
  37.2 10.2 %collective-permute-start.2 = (bf16[64,2048]{1,0:T(8,128)(2,1)}, bf16[64,2048]{1,0:T(8,128)(2,1)}, u32[]{:S(2)}, u32[]{:S(2)}) collective-permute-start(bf16[64,2048]{1,0:T(8,128)(2,1)} %slice.391), channel_id=1, source_target_pairs={{0,2},{1,3},{2,4},{3,5},{4,6},{5,7},{6,0},{7,1},{8,10},{9,11},{10,... | collective-permute-start | bytes 786440 | tf_op jit(solution)/shard_map/ppermute | solution.py:44
  41.2 10.0 %collective-permute-start.5 = (bf16[144,2048]{1,0:T(8,128)(2,1)S(1)}, bf16[144,2048]{1,0:T(8,128)(2,1)}, u32[]{:S(2)}, u32[]{:S(2)}) collective-permute-start(bf16[144,2048]{1,0:T(8,128)(2,1)S(1)} %collective-permute-done.refs_1_), channel_id=1, source_target_pairs={{0,1},{1,0},{2,3},{3,2},{4,5},{5,4},{6,7},{7,6},{8,9},{9,8},{10,11... | collective-permute-start | bytes 1769480 | tf_op jit(solution)/shard_map/ppermute | solution.py:48
  41.2 10.0 %collective-permute-start.8 = (bf16[144,2048]{1,0:T(8,128)(2,1)S(1)}, bf16[144,2048]{1,0:T(8,128)(2,1)}, u32[]{:S(2)}, u32[]{:S(2)}) collective-permute-start(bf16[144,2048]{1,0:T(8,128)(2,1)S(1)} %collective-permute-done.1.refs_4_), channel_id=1, source_target_pairs={{0,1},{1,0},{2,3},{3,2},{4,5},{5,4},{6,7},{7,6},{8,9},{9,8},{10,11... | collective-permute-start | bytes 1769480 | tf_op jit(solution)/shard_map/ppermute | solution.py:48
  51.9 19.8 %collective-permute-start.13 = (bf16[128,2048]{1,0:T(8,128)(2,1)S(1)}, bf16[128,2048]{1,0:T(8,128)(2,1)}, u32[]{:S(2)}, u32[]{:S(2)}) collective-permute-start(bf16[128,2048]{1,0:T(8,128)(2,1)S(1)} %bitcast.233), channel_id=1, source_target_pairs={{0,6},{1,7},{2,0},{3,1},{4,2},{5,3},{6,4},{7,5},{8,14},{9,15},{10,... | collective-permute-start | bytes 1572872 | tf_op jit(solution)/shard_map/ppermute | solution.py:44
  54.8 15.2 %collective-permute-start.14 = (bf16[128,2048]{1,0:T(8,128)(2,1)S(1)}, bf16[128,2048]{1,0:T(8,128)(2,1)}, u32[]{:S(2)}, u32[]{:S(2)}) collective-permute-start(bf16[128,2048]{1,0:T(8,128)(2,1)S(1)} %bitcast.234), channel_id=1, source_target_pairs={{0,2},{1,3},{2,4},{3,5},{4,6},{5,7},{6,0},{7,1},{8,10},{9,11},{10,... | collective-permute-start | bytes 1572872 | tf_op jit(solution)/shard_map/ppermute | solution.py:44
  71.7 53.1 %collective-permute-start.15 = (bf16[64,2048]{1,0:T(8,128)(2,1)}, bf16[64,2048]{1,0:T(8,128)(2,1)}, u32[]{:S(2)}, u32[]{:S(2)}) collective-permute-start(bf16[64,2048]{1,0:T(8,128)(2,1)} %slice.404), channel_id=1, source_target_pairs={{0,2},{1,3},{2,4},{3,5},{4,6},{5,7},{6,0},{7,1},{8,10},{9,11},{10,... | collective-permute-start | bytes 786440 | tf_op jit(solution)/shard_map/ppermute | solution.py:44
  73.4 51.5 %collective-permute-start.16 = (bf16[64,2048]{1,0:T(8,128)(2,1)}, bf16[64,2048]{1,0:T(8,128)(2,1)}, u32[]{:S(2)}, u32[]{:S(2)}) collective-permute-start(bf16[64,2048]{1,0:T(8,128)(2,1)} %slice.405), channel_id=1, source_target_pairs={{0,6},{1,7},{2,0},{3,1},{4,2},{5,3},{6,4},{7,5},{8,14},{9,15},{10,... | collective-permute-start | bytes 786440 | tf_op jit(solution)/shard_map/ppermute | solution.py:44
  94.6 49.6 %all-to-all-start = ((bf16[16,128,384]{2,1,0:T(8,128)(2,1)}), bf16[16,128,384]{2,1,0:T(8,128)(2,1)}, u32[]{:S(2)}, u32[]{:S(2)}) async-start(bf16[16,128,384]{2,1,0:T(8,128)(2,1)} %bitcast.4), calls=%async_computation | async-start | bytes 3145728 | tf_op jit(solution)/shard_map/all_to_all | solution.py:984
  101.6 421.8 %reduce-scatter.2.cloned.1.call-start = ((), (), s32[]{:S(2)}) async-start(), calls=%async_computation.8 | async-start | bytes 23396352 | tf_op jit(solution)/shard_map/reduce_scatter | solution.py:1050
  107.9 10.3 %collective-permute-start.9 = (bf16[4,256,256]{2,1,0:T(8,128)(2,1)}, bf16[4,256,256]{2,1,0:T(8,128)(2,1)}, u32[]{:S(2)}, u32[]{:S(2)}) collective-permute-start(bf16[4,256,256]{2,1,0:T(8,128)(2,1)} %pad_maximum_fusion.6), channel_id=1, source_target_pairs={{0,1},{1,0},{2,3},{3,2},{4,5},{5,4},{6,7},{7,6},{8,9},{9,8},{10,11... | collective-permute-start | bytes 1572872 | tf_op jit(solution)/shard_map/ppermute | solution.py:48
  119.4 15.6 %collective-permute-start.10 = (bf16[2,256,256]{2,1,0:T(8,128)(2,1)S(1)}, bf16[2,256,256]{2,1,0:T(8,128)(2,1)S(1)}, u32[]{:S(2)}, u32[]{:S(2)}) collective-permute-start(bf16[2,256,256]{2,1,0:T(8,128)(2,1)S(1)} %get-tuple-element.353), channel_id=1, source_target_pairs={{0,2},{1,3},{2,4},{3,5},{4,6},{5,7},{6,0},{7,1},{8,10},{9,11},{10,... | collective-permute-start | bytes 786440 | tf_op jit(solution)/shard_map/ppermute | solution.py:44
  121.4 13.6 %collective-permute-start.11 = (bf16[2,256,256]{2,1,0:T(8,128)(2,1)S(1)}, bf16[2,256,256]{2,1,0:T(8,128)(2,1)S(1)}, u32[]{:S(2)}, u32[]{:S(2)}) collective-permute-start(bf16[2,256,256]{2,1,0:T(8,128)(2,1)S(1)} %get-tuple-element.354), channel_id=1, source_target_pairs={{0,4},{1,5},{2,6},{3,7},{4,0},{5,1},{6,2},{7,3},{8,12},{9,13},{10,... | collective-permute-start | bytes 786440 | tf_op jit(solution)/shard_map/ppermute | solution.py:44
  122.8 14.7 %collective-permute-start.12 = (bf16[2,256,256]{2,1,0:T(8,128)(2,1)S(1)}, bf16[2,256,256]{2,1,0:T(8,128)(2,1)S(1)}, u32[]{:S(2)}, u32[]{:S(2)}) collective-permute-start(bf16[2,256,256]{2,1,0:T(8,128)(2,1)S(1)} %get-tuple-element.352), channel_id=1, source_target_pairs={{0,6},{1,7},{2,0},{3,1},{4,2},{5,3},{6,4},{7,5},{8,14},{9,15},{10,... | collective-permute-start | bytes 786440 | tf_op jit(solution)/shard_map/ppermute | solution.py:44
  124.8 19.5 %collective-permute-start.17 = (bf16[128,2048]{1,0:T(8,128)(2,1)S(1)}, bf16[128,2048]{1,0:T(8,128)(2,1)}, u32[]{:S(2)}, u32[]{:S(2)}) collective-permute-start(bf16[128,2048]{1,0:T(8,128)(2,1)S(1)} %bitcast.235), channel_id=1, source_target_pairs={{0,1},{1,0},{2,3},{3,2},{4,5},{5,4},{6,7},{7,6},{8,9},{9,8},{10,11... | collective-permute-start | bytes 1572872 | tf_op jit(solution)/shard_map/ppermute | solution.py:48
  124.9 19.4 %collective-permute-start.18 = (bf16[128,2048]{1,0:T(8,128)(2,1)}, bf16[128,2048]{1,0:T(8,128)(2,1)}, u32[]{:S(2)}, u32[]{:S(2)}) collective-permute-start(bf16[128,2048]{1,0:T(8,128)(2,1)} %collective-permute-done.13.refs_16_.refs_11_), channel_id=1, source_target_pairs={{0,1},{1,0},{2,3},{3,2},{4,5},{5,4},{6,7},{7,6},{8,9},{9,8},{10,11... | collective-permute-start | bytes 1572872 | tf_op jit(solution)/shard_map/ppermute | solution.py:48
  184.9 9.6 %collective-permute-start.23 = (bf16[64,2048]{1,0:T(8,128)(2,1)S(1)}, bf16[64,2048]{1,0:T(8,128)(2,1)S(1)}, u32[]{:S(2)}, u32[]{:S(2)}) collective-permute-start(bf16[64,2048]{1,0:T(8,128)(2,1)S(1)} %get-tuple-element.334), channel_id=1, source_target_pairs={{0,2},{1,3},{2,4},{3,5},{4,6},{5,7},{6,0},{7,1},{8,10},{9,11},{10,... | collective-permute-start | bytes 786440 | tf_op jit(solution)/shard_map/ppermute | solution.py:44
  194.6 13.5 %collective-permute-start.26 = (bf16[128,2048]{1,0:T(8,128)(2,1)S(1)}, bf16[128,2048]{1,0:T(8,128)(2,1)S(1)}, u32[]{:S(2)}, u32[]{:S(2)}) collective-permute-start(bf16[128,2048]{1,0:T(8,128)(2,1)S(1)} %pad_maximum_fusion.8), channel_id=1, source_target_pairs={{0,6},{1,7},{2,0},{3,1},{4,2},{5,3},{6,4},{7,5},{8,14},{9,15},{10,... | collective-permute-start | bytes 1572872 | tf_op jit(solution)/shard_map/ppermute | solution.py:44
  197.7 13.9 %collective-permute-start.24 = (bf16[128,2048]{1,0:T(8,128)(2,1)S(1)}, bf16[128,2048]{1,0:T(8,128)(2,1)S(1)}, u32[]{:S(2)}, u32[]{:S(2)}) collective-permute-start(bf16[128,2048]{1,0:T(8,128)(2,1)S(1)} %pad_maximum_fusion.7), channel_id=1, source_target_pairs={{0,2},{1,3},{2,4},{3,5},{4,6},{5,7},{6,0},{7,1},{8,10},{9,11},{10,... | collective-permute-start | bytes 1572872 | tf_op jit(solution)/shard_map/ppermute | solution.py:44
  212.2 13.1 %collective-permute-start.28 = (bf16[128,2048]{1,0:T(8,128)(2,1)S(1)}, bf16[128,2048]{1,0:T(8,128)(2,1)S(1)}, u32[]{:S(2)}, u32[]{:S(2)}) collective-permute-start(bf16[128,2048]{1,0:T(8,128)(2,1)S(1)} %multiply_convert_fusion.refs_5_.refs_0_), channel_id=1, source_target_pairs={{0,2},{1,3},{2,4},{3,5},{4,6},{5,7},{6,0},{7,1},{8,10},{9,11},{10,... | collective-permute-start | bytes 1572872 | tf_op jit(solution)/shard_map/ppermute | solution.py:44
  212.3 13.1 %collective-permute-start.27 = (bf16[128,2048]{1,0:T(8,128)(2,1)S(1)}, bf16[128,2048]{1,0:T(8,128)(2,1)S(1)}, u32[]{:S(2)}, u32[]{:S(2)}) collective-permute-start(bf16[128,2048]{1,0:T(8,128)(2,1)S(1)} %multiply_convert_fusion.refs_5_.refs_0_), channel_id=1, source_target_pairs={{0,6},{1,7},{2,0},{3,1},{4,2},{5,3},{6,4},{7,5},{8,14},{9,15},{10,... | collective-permute-start | bytes 1572872 | tf_op jit(solution)/shard_map/ppermute | solution.py:44
  215.5 19.6 %collective-permute-start.31 = (bf16[128,2048]{1,0:T(8,128)(2,1)S(1)}, bf16[128,2048]{1,0:T(8,128)(2,1)S(1)}, u32[]{:S(2)}, u32[]{:S(2)}) collective-permute-start(bf16[128,2048]{1,0:T(8,128)(2,1)S(1)} %multiply_convert_fusion.refs_5_.refs_0_), channel_id=1, source_target_pairs={{0,1},{1,0},{2,3},{3,2},{4,5},{5,4},{6,7},{7,6},{8,9},{9,8},{10,11... | collective-permute-start | bytes 1572872 | tf_op jit(solution)/shard_map/ppermute | solution.py:48
  225.5 9.7 %collective-permute-start.32 = (bf16[128,2048]{1,0:T(8,128)(2,1)S(1)}, bf16[128,2048]{1,0:T(8,128)(2,1)S(1)}, u32[]{:S(2)}, u32[]{:S(2)}) collective-permute-start(bf16[128,2048]{1,0:T(8,128)(2,1)S(1)} %collective-permute-done.27.refs_6_.refs_1_), channel_id=1, source_target_pairs={{0,1},{1,0},{2,3},{3,2},{4,5},{5,4},{6,7},{7,6},{8,9},{9,8},{10,11... | collective-permute-start | bytes 1572872 | tf_op jit(solution)/shard_map/ppermute | solution.py:48
  281.1 14.9 %collective-permute-start.36 = (bf16[512,2176]{1,0:T(8,128)(2,1)}, bf16[512,2176]{1,0:T(8,128)(2,1)}, u32[]{:S(2)}, u32[]{:S(2)}) collective-permute-start(bf16[512,2176]{1,0:T(8,128)(2,1)} %get-tuple-element.168), channel_id=1, source_target_pairs={{0,1},{1,0},{2,3},{3,2},{4,5},{5,4},{6,7},{7,6},{8,9},{9,8},{10,11... | collective-permute-start | bytes 6684680 | tf_op jit(solution)/shard_map/ppermute | solution.py:48
  299.2 9.9 %collective-permute-start.38 = (bf16[64,2176]{1,0:T(8,128)(2,1)S(1)}, bf16[64,2176]{1,0:T(8,128)(2,1)S(1)}, u32[]{:S(2)}, u32[]{:S(2)}) collective-permute-start(bf16[64,2176]{1,0:T(8,128)(2,1)S(1)} %get-tuple-element.323), channel_id=1, source_target_pairs={{0,6},{1,7},{2,0},{3,1},{4,2},{5,3},{6,4},{7,5},{8,14},{9,15},{10,... | collective-permute-start | bytes 835592 | tf_op jit(solution)/shard_map/ppermute | solution.py:44
  314.2 16.1 %collective-permute-start.39 = (bf16[128,2176]{1,0:T(8,128)(2,1)}, bf16[128,2176]{1,0:T(8,128)(2,1)S(1)}, u32[]{:S(2)}, u32[]{:S(2)}) collective-permute-start(bf16[128,2176]{1,0:T(8,128)(2,1)} %pad_maximum_fusion.3), channel_id=1, source_target_pairs={{0,2},{1,3},{2,4},{3,5},{4,6},{5,7},{6,0},{7,1},{8,10},{9,11},{10,... | collective-permute-start | bytes 1671176 | tf_op jit(solution)/shard_map/ppermute | solution.py:44
  314.2 16.1 %collective-permute-start.40 = (bf16[128,2176]{1,0:T(8,128)(2,1)}, bf16[128,2176]{1,0:T(8,128)(2,1)S(1)}, u32[]{:S(2)}, u32[]{:S(2)}) collective-permute-start(bf16[128,2176]{1,0:T(8,128)(2,1)} %pad_maximum_fusion.4), channel_id=1, source_target_pairs={{0,6},{1,7},{2,0},{3,1},{4,2},{5,3},{6,4},{7,5},{8,14},{9,15},{10,... | collective-permute-start | bytes 1671176 | tf_op jit(solution)/shard_map/ppermute | solution.py:44
  335.2 13.7 %collective-permute-start.41 = (bf16[128,2048]{1,0:T(8,128)(2,1)}, bf16[128,2048]{1,0:T(8,128)(2,1)}, u32[]{:S(2)}, u32[]{:S(2)}) collective-permute-start(bf16[128,2048]{1,0:T(8,128)(2,1)} %get-tuple-element.186.refs_0_), channel_id=1, source_target_pairs={{0,2},{1,3},{2,4},{3,5},{4,6},{5,7},{6,0},{7,1},{8,10},{9,11},{10,... | collective-permute-start | bytes 1572872 | tf_op jit(solution)/shard_map/ppermute | solution.py:44
  335.2 13.7 %collective-permute-start.42 = (bf16[128,2048]{1,0:T(8,128)(2,1)}, bf16[128,2048]{1,0:T(8,128)(2,1)}, u32[]{:S(2)}, u32[]{:S(2)}) collective-permute-start(bf16[128,2048]{1,0:T(8,128)(2,1)} %get-tuple-element.186.refs_0_), channel_id=1, source_target_pairs={{0,6},{1,7},{2,0},{3,1},{4,2},{5,3},{6,4},{7,5},{8,14},{9,15},{10,... | collective-permute-start | bytes 1572872 | tf_op jit(solution)/shard_map/ppermute | solution.py:44
  338.4 24.1 %collective-permute-start.45 = (bf16[128,2048]{1,0:T(8,128)(2,1)}, bf16[128,2048]{1,0:T(8,128)(2,1)}, u32[]{:S(2)}, u32[]{:S(2)}) collective-permute-start(bf16[128,2048]{1,0:T(8,128)(2,1)} %get-tuple-element.186.refs_0_), channel_id=1, source_target_pairs={{0,1},{1,0},{2,3},{3,2},{4,5},{5,4},{6,7},{7,6},{8,9},{9,8},{10,11... | collective-permute-start | bytes 1572872 | tf_op jit(solution)/shard_map/ppermute | solution.py:48
  350.9 11.6 %collective-permute-start.46 = (bf16[128,2048]{1,0:T(8,128)(2,1)}, bf16[128,2048]{1,0:T(8,128)(2,1)}, u32[]{:S(2)}, u32[]{:S(2)}) collective-permute-start(bf16[128,2048]{1,0:T(8,128)(2,1)} %collective-permute-done.42.refs_1_), channel_id=1, source_target_pairs={{0,1},{1,0},{2,3},{3,2},{4,5},{5,4},{6,7},{7,6},{8,9},{9,8},{10,11... | collective-permute-start | bytes 1572872 | tf_op jit(solution)/shard_map/ppermute | solution.py:48
  369.9 42.0 %collective-permute-start.50 = (bf16[512,2048]{1,0:T(8,128)(2,1)}, bf16[512,2048]{1,0:T(8,128)(2,1)}, u32[]{:S(2)}, u32[]{:S(2)}) collective-permute-start(bf16[512,2048]{1,0:T(8,128)(2,1)} %add_convert_fusion.1), channel_id=1, source_target_pairs={{0,1},{1,0},{2,3},{3,2},{4,5},{5,4},{6,7},{7,6},{8,9},{9,8},{10,11... | collective-permute-start | bytes 6291464 | tf_op jit(solution)/shard_map/ppermute | solution.py:48
  408.1 41.0 %all-to-all-start.3 = ((bf16[16,128,384]{2,1,0:T(8,128)(2,1)}), bf16[16,128,384]{2,1,0:T(8,128)(2,1)S(1)}, u32[]{:S(2)}, u32[]{:S(2)}) async-start(bf16[16,128,384]{2,1,0:T(8,128)(2,1)} %bitcast.237), calls=%async_computation.3 | async-start | bytes 3145728 | tf_op jit(solution)/shard_map/all_to_all | solution.py:1065
  415.6 9.7 %collective-permute-start.51 = (bf16[64,2048]{1,0:T(8,128)(2,1)S(1)}, bf16[64,2048]{1,0:T(8,128)(2,1)S(1)}, u32[]{:S(2)}, u32[]{:S(2)}) collective-permute-start(bf16[64,2048]{1,0:T(8,128)(2,1)S(1)} %get-tuple-element.330), channel_id=1, source_target_pairs={{0,2},{1,3},{2,4},{3,5},{4,6},{5,7},{6,0},{7,1},{8,10},{9,11},{10,... | collective-permute-start | bytes 786440 | tf_op jit(solution)/shard_map/ppermute | solution.py:44
  425.4 21.1 %collective-permute-start.54 = (bf16[128,2048]{1,0:T(8,128)(2,1)S(1)}, bf16[128,2048]{1,0:T(8,128)(2,1)S(1)}, u32[]{:S(2)}, u32[]{:S(2)}) collective-permute-start(bf16[128,2048]{1,0:T(8,128)(2,1)S(1)} %pad_maximum_fusion.10), channel_id=1, source_target_pairs={{0,6},{1,7},{2,0},{3,1},{4,2},{5,3},{6,4},{7,5},{8,14},{9,15},{10,... | collective-permute-start | bytes 1572872 | tf_op jit(solution)/shard_map/ppermute | solution.py:44
  428.6 18.0 %collective-permute-start.52 = (bf16[128,2048]{1,0:T(8,128)(2,1)S(1)}, bf16[128,2048]{1,0:T(8,128)(2,1)S(1)}, u32[]{:S(2)}, u32[]{:S(2)}) collective-permute-start(bf16[128,2048]{1,0:T(8,128)(2,1)S(1)} %pad_maximum_fusion.9), channel_id=1, source_target_pairs={{0,2},{1,3},{2,4},{3,5},{4,6},{5,7},{6,0},{7,1},{8,10},{9,11},{10,... | collective-permute-start | bytes 1572872 | tf_op jit(solution)/shard_map/ppermute | solution.py:44
  429.8 23.5 %collective-permute-start.56 = (bf16[2,256,256]{2,1,0:T(8,128)(2,1)}, bf16[2,256,256]{2,1,0:T(8,128)(2,1)S(1)}, u32[]{:S(2)}, u32[]{:S(2)}) collective-permute-start(bf16[2,256,256]{2,1,0:T(8,128)(2,1)} %get-tuple-element.350), channel_id=1, source_target_pairs={{0,2},{1,3},{2,4},{3,5},{4,6},{5,7},{6,0},{7,1},{8,10},{9,11},{10,... | collective-permute-start | bytes 786440 | tf_op jit(solution)/shard_map/ppermute | solution.py:44
  430.0 24.0 %collective-permute-start.57 = (bf16[2,256,256]{2,1,0:T(8,128)(2,1)}, bf16[2,256,256]{2,1,0:T(8,128)(2,1)S(1)}, u32[]{:S(2)}, u32[]{:S(2)}) collective-permute-start(bf16[2,256,256]{2,1,0:T(8,128)(2,1)} %get-tuple-element.351), channel_id=1, source_target_pairs={{0,4},{1,5},{2,6},{3,7},{4,0},{5,1},{6,2},{7,3},{8,12},{9,13},{10,... | collective-permute-start | bytes 786440 | tf_op jit(solution)/shard_map/ppermute | solution.py:44
  434.4 20.2 %collective-permute-start.58 = (bf16[2,256,256]{2,1,0:T(8,128)(2,1)}, bf16[2,256,256]{2,1,0:T(8,128)(2,1)}, u32[]{:S(2)}, u32[]{:S(2)}) collective-permute-start(bf16[2,256,256]{2,1,0:T(8,128)(2,1)} %get-tuple-element.349), channel_id=1, source_target_pairs={{0,6},{1,7},{2,0},{3,1},{4,2},{5,3},{6,4},{7,5},{8,14},{9,15},{10,... | collective-permute-start | bytes 786440 | tf_op jit(solution)/shard_map/ppermute | solution.py:44
  470.1 53.3 %all-to-all-start.4 = ((bf16[16,128,640]{2,1,0:T(8,128)(2,1)}), bf16[16,128,640]{2,1,0:T(8,128)(2,1)}, u32[]{:S(2)}, u32[]{:S(2)}) async-start(bf16[16,128,640]{2,1,0:T(8,128)(2,1)} %bitcast.83), calls=%async_computation.4 | async-start | bytes 5242880 | tf_op jit(solution)/shard_map/all_to_all | solution.py:1079
  476.7 71.9 %all-gather.11.cloned.1.call-start = ((), (), s32[]{:S(2)}) async-start(), calls=%async_computation.9 | async-start | bytes 2654208 | tf_op jit(solution)/shard_map/all_gather | solution.py:1096
  525.1 56.0 %all-gather.13.cloned.1.call-start = ((), (), s32[]{:S(2)}) async-start(), calls=%async_computation.10 | async-start | bytes 1769472 | tf_op jit(solution)/shard_map/all_gather | solution.py:1098
  548.6 15.1 %collective-permute-start.64 = (bf16[128,2048]{1,0:T(8,128)(2,1)}, bf16[128,2048]{1,0:T(8,128)(2,1)S(1)}, u32[]{:S(2)}, u32[]{:S(2)}) collective-permute-start(bf16[128,2048]{1,0:T(8,128)(2,1)} %pad_maximum_fusion.12), channel_id=1, source_target_pairs={{0,6},{1,7},{2,0},{3,1},{4,2},{5,3},{6,4},{7,5},{8,14},{9,15},{10,... | collective-permute-start | bytes 1572872 | tf_op jit(solution)/shard_map/ppermute | solution.py:44
  550.3 16.5 %collective-permute-start.63 = (bf16[128,2048]{1,0:T(8,128)(2,1)S(1)}, bf16[128,2048]{1,0:T(8,128)(2,1)S(1)}, u32[]{:S(2)}, u32[]{:S(2)}) collective-permute-start(bf16[128,2048]{1,0:T(8,128)(2,1)S(1)} %pad_maximum_fusion.11), channel_id=1, source_target_pairs={{0,2},{1,3},{2,4},{3,5},{4,6},{5,7},{6,0},{7,1},{8,10},{9,11},{10,... | collective-permute-start | bytes 1572872 | tf_op jit(solution)/shard_map/ppermute | solution.py:44
  (109 other events, 714.3 us)
Sparse Core Ops, SparseCore 0:
  12.4 51.9 all-gather.6
  67.2 159.2 all-gather.8
  331.3 171.7 reduce-scatter.1
  525.2 23.2 all-gather.10
  550.8 25.6 all-gather.12
where the time goes:
time: 603 us; the launch traced here: 592 us
  waiting for transfers between devices  190 us (32%)
  Pallas kernels  120 us (20%)
  starting transfers between devices  82.8 us (14%)
  local copies, waits for them, and re-layouts  71.9 us (12%)
  blocking collectives  48.9 us (8%)
  other arithmetic  48.7 us (8%)
  between operations  15.7 us (3%)
  matrix products  14.1 us (2%)
    ppermute x38, waiting for transfers between devices, move_z(): return lax.ppermute(block, 'expert', shift_pairs(step))  133 us
    ppermute x38, starting transfers between devices, move_z(): return lax.ppermute(block, 'expert', shift_pairs(step))  60.1 us
    pallas_call x1, Pallas kernels, ffn(): pl.pallas_call(ffn_kernel, out_shape=tuple([jax.ShapeDtypeStruct(shape, l...  42.9 us
    unnamed x173, local copies, waits for them, and re-layouts  35.7 us
    all_to_all x1, waiting for transfers between devices, per_device(): lax.all_to_all(attn_grads, 'fsdp', split_axis=0, concat_axis=0, tiled=True)  31.9 us
    all_to_all x1, blocking collectives, per_device(): lax.all_to_all(mixed_head, 'fsdp', split_axis=0, concat_axis=0, tiled=True)  25.3 us
    all_to_all x1, blocking collectives, per_device(): lax.all_to_all(sent_back, 'fsdp', split_axis=0, concat_axis=0, tiled=True)  23.7 us
    all_gather x1, waiting for transfers between devices, per_device(): shared_shards = lax.all_gather(ffn_sums[:, :base], 'expert', axis=0)  18.8 us
  transfers between devices with their start and end apart: 73, of which 27 were waited for; matrix products, arithmetic and copies ran while one was open for 15% of the time, Pallas kernels for 13%

commit v1 on v0

--- a/solution.py
+++ b/solution.py
@@ -507,38 +507,39 @@
     )
 
 
-def slab(buffer, out_ref, sems, step, start):
-    target = out_ref.at[pl.ds(step * ROWS, ROWS), pl.ds(start, buffer.shape[2])]
-    return pltpu.make_async_copy(buffer.at[step % 2], target, sems.at[step % 2])
+def slab(buffer, out_ref, sems, step, start, width):
+    target = out_ref.at[pl.ds(step * ROWS, ROWS), pl.ds(start, width)]
+    return pltpu.make_async_copy(buffer.at[step % 2, :, pl.ds(0, width)], target, sems.at[step % 2])
 
 
 def send_slabs(tokens_ref, grad_ref, down_rows, out_ref, buffer, sems, start):
     width = grad_ref.shape[1]
     count = width // 2 // FSDP
+    place = (start, width + width // 2)
     for step in range(D // ROWS):
         slot = step % 2
         if step >= 2:
-            slab(buffer, out_ref, sems, step - 2, start).wait()
+            slab(buffer, out_ref, sems, step - 2, *place).wait()
         buffer[slot, :, 0:width] = t_mm(tokens_ref[:, pl.ds(step * ROWS, ROWS)], grad_ref[...]).astype(low)
         down = down_rows(step)
         for part in range(2):
             packed = pack_rows(down[part * count : (part + 1) * count]).astype(low)
-            buffer[slot, part * TOK : (part + 1) * TOK, width:] = packed
-        slab(buffer, out_ref, sems, step, start).start()
+            buffer[slot, part * TOK : (part + 1) * TOK, width : width + width // 2] = packed
+        slab(buffer, out_ref, sems, step, *place).start()
     for step in (D // ROWS - 2, D // ROWS - 1):
-        slab(buffer, out_ref, sems, step, start).wait()
+        slab(buffer, out_ref, sems, step, *place).wait()
 
 
 def ffn_kernel(*refs):
     expert_ref, slots_hbm, slots_t_hbm, routes_ref, router_hbm = refs[:5]
     pieces, cot_pieces, pack_ref = refs[5:15], refs[15:25], refs[25]
-    grad_mine, grad_other, gates_ref = refs[26:29]
-    outs = refs[29:37]
-    normed_ref, cot_ref, grad_ref = refs[37:40]
-    kept = refs[40:48]
+    grad_mine, grad_other, gates_ref, out_ref = refs[26:30]
+    outs = refs[30:33]
+    normed_ref, cot_ref, grad_ref = refs[33:36]
+    kept = refs[36:44]
     hidden_s, grad_s, incoming, hidden_e, gated, grad_rows, grad_e, w_down_s = kept
-    w_in_s, w_in, w_down, slots_ref, slots_t_ref = refs[48:53]
-    raw, gate_parts, grad_in, piece_sems, cot_sems, sems, out_sems = refs[53:]
+    w_in_s, w_in, w_down, slots_ref, slots_t_ref = refs[44:49]
+    raw, gate_parts, grad_in, buffer, piece_sems, cot_sems, sems, out_sems, slab_sems = refs[49:]
     base = 3 * SH_OWN
     half_d = D // 2
 
@@ -581,8 +582,8 @@
     for copy in copies[2:]:
         copy.start()
 
-    def send(index):
-        copy = pltpu.make_async_copy(kept[index], outs[index], out_sems.at[index])
+    def send(index, source):
+        copy = pltpu.make_async_copy(source, outs[index], out_sems.at[index])
         copy.start()
         return copy
 
@@ -620,7 +621,8 @@
             both_gates = jnp.where(lane == 0, gate_first, 0.0) + jnp.where(lane == 1, gate_second, 0.0)
             gates_ref[...] = both_gates[:TOK]
     stage_down(1).start()
-    sent = [send(0), send(1), send(7)]
+    sent = [send(0, hidden_s)]
+    down_copy = send(1, w_down_s)
     copies[2].wait()
     for step in range(D // ROWS):
         columns = pl.ds(step * ROWS, ROWS)
@@ -628,7 +630,6 @@
         grad_rows[:, columns] = mm(slots_ref[...], cot_ref[:, columns]).astype(low)
     slot_parts = mm(slots_ref[...], gate_parts[...])
     slot_gate = slot_parts[:, 0:1] + slot_parts[:, 1:2]
-    sent.append(send(2))
     copies[3].wait()
     stage_down(1).wait()
     for step in range(4):
@@ -639,7 +640,6 @@
     for start, width in FF_TILES:
         gate, up = raw[:, start : start + width], raw[:, FF + start : FF + start + width]
         hidden_e[:, start : start + width] = (silu_parts(gate)[1] * up).astype(low)
-    sent.append(send(3))
     slot_grad = jnp.zeros((SLOTS, 1), wide)
     for step in range(D // ROWS):
         columns = pl.ds(step * ROWS, ROWS)
@@ -648,14 +648,13 @@
         gated[:, columns] = (rows * slot_gate).astype(low)
         grad_rows[:, columns] = (cot * slot_gate).astype(low)
         slot_grad = slot_grad + jnp.sum(rows * cot, axis=1, keepdims=True)
-    sent += [send(4), send(5)]
+    sent.append(send(2, gated))
     for start, width in FF_TILES:
         grad_hidden = mm_t(grad_rows[...], w_down[pl.ds(start, width), :])
         sig, act = silu_parts(raw[:, start : start + width])
         grad_gate, grad_up = swiglu_back(sig, act, raw[:, FF + start : FF + start + width], grad_hidden)
         grad_e[:, start : start + width] = grad_gate
         grad_e[:, FF + start : FF + start + width] = grad_up
-    sent.append(send(6))
     for step in range(D // ROWS):
         columns = pl.ds(step * ROWS, ROWS)
         grad_in[:, columns] = mm_t(grad_e[...], w_in[columns, :]).astype(low)
@@ -680,11 +679,27 @@
         copy = pltpu.make_async_copy(grad_ref.at[pl.ds(side * half, half), :], target, sems.at[9 + side])
         copy.start()
         sent.append(copy)
+
+    def expert_down(step):
+        count = 2 * FF // FSDP
+        return t_mm(hidden_e[:, step * count : (step + 1) * count], grad_rows[...])
+
+    def shared_down(step):
+        count = 2 * SH_PAD
+        return w_down_s[step * count : (step + 1) * count, :].astype(wide)
+
+    down_copy.wait()
+    for step in range(D // ROWS):
+        columns = pl.ds(step * ROWS, ROWS)
+        w_down_s[:, columns] = t_mm(hidden_s[...], cot_ref[:, columns]).astype(low)
+    send_slabs(incoming, grad_e, expert_down, out_ref, buffer, slab_sems, base)
+    send_slabs(normed_ref, grad_s, shared_down, out_ref, buffer, slab_sems, 0)
     for copy in sent:
         copy.wait()
 
 
 def ffn(expert, slots, slots_t, routes, router, pieces, cot_pieces, pack):
+    outs = [(D, 3 * SH_OWN + 3 * FF), (ALL, SH_OWN), (SH_OWN, D), (SLOTS, D)]
     kept = [(ALL, SH_OWN), (ALL, 2 * SH_OWN), (SLOTS, D), (SLOTS, FF), (SLOTS, D), (SLOTS, D), (SLOTS, 2 * FF)]
     kept.append((SH_OWN, D))
     grads = [(ALL // 2, D + 128)] * 2
@@ -693,10 +708,10 @@
         out_shape=tuple(
             [jax.ShapeDtypeStruct(shape, low) for shape in grads]
             + [jax.ShapeDtypeStruct((TOK, 128), wide)]
-            + [jax.ShapeDtypeStruct(shape, low) for shape in kept]
+            + [jax.ShapeDtypeStruct(shape, low) for shape in outs]
         ),
         in_specs=[smem, anywhere, anywhere, vmem] + [anywhere] * 22,
-        out_specs=tuple([anywhere] * 2 + [vmem] + [anywhere] * 8),
+        out_specs=tuple([anywhere] * 2 + [vmem] + [anywhere] * 4),
         scratch_shapes=[pltpu.VMEM((ALL, D), low), pltpu.VMEM((ALL, D), low), pltpu.VMEM((ALL, D + 128), low)]
         + [pltpu.VMEM(shape, low) for shape in kept]
         + [
@@ -708,76 +723,17 @@
             pltpu.VMEM((SLOTS, 2 * FF), wide),
             pltpu.VMEM((ALL, 128), low),
             pltpu.VMEM((SLOTS, D), low),
+            pltpu.VMEM((2, ROWS, 3 * FF), low),
             pltpu.SemaphoreType.DMA((20,)),
             pltpu.SemaphoreType.DMA((20,)),
             pltpu.SemaphoreType.DMA((11,)),
-            pltpu.SemaphoreType.DMA((8,)),
-        ],
-        compiler_params=params(60),
-        cost_estimate=cost(27e9, 50e6, 1e6),
-        name="ffn",
-    )(expert, slots, slots_t, routes, router, *pieces, *cot_pieces, pack)
-
-
-def shared_weights_kernel(*refs):
-    pieces, cot_pieces, hidden_ref, grad_ref = refs[:10], refs[10:20], refs[20], refs[21]
-    out_ref, normed_ref, cot_ref, buffer, down, piece_sems, cot_sems, sems = refs[22:]
-    cot_copies = load_pieces(cot_pieces, cot_ref, None, cot_sems)
-    copies = load_pieces(pieces, normed_ref, None, piece_sems)
-    for copy in cot_copies:
-        copy.wait()
-    for tile in range(D // ROWS):
-        part = pl.ds(tile * ROWS, ROWS)
-        down[:, part] = t_mm(hidden_ref[...], cot_ref[:, part])
-    for copy in copies:
-        copy.wait()
-    count = 2 * SH_PAD
-    send_slabs(
-        normed_ref, grad_ref, lambda step: down[step * count : (step + 1) * count, :], out_ref, buffer, sems, 0
-    )
-
-
-def shared_weights(pieces, cot_pieces, hidden, grad):
-    return pl.pallas_call(
-        shared_weights_kernel,
-        out_shape=jax.ShapeDtypeStruct((D, 3 * SH_OWN + 3 * FF), low),
-        in_specs=[anywhere] * 20 + [vmem] * 2,
-        out_specs=anywhere,
-        scratch_shapes=[
-            pltpu.VMEM((ALL, D), low),
-            pltpu.VMEM((ALL, D), low),
-            pltpu.VMEM((2, ROWS, 3 * SH_OWN), low),
-            pltpu.VMEM((SH_OWN, D), wide),
-            pltpu.SemaphoreType.DMA((20,)),
-            pltpu.SemaphoreType.DMA((20,)),
+            pltpu.SemaphoreType.DMA((3,)),
             pltpu.SemaphoreType.DMA((2,)),
         ],
         compiler_params=params(60),
-        cost_estimate=cost(5e9, 18e6),
-        name="shared_weights",
-    )(*pieces, *cot_pieces, hidden, grad)
-
-
-def expert_weights_kernel(_, incoming_ref, hidden_ref, grad_rows_ref, grad_ref, out_ref, buffer, sems):
-    def down_rows(step):
-        count = 2 * FF // FSDP
-        return t_mm(hidden_ref[:, step * count : (step + 1) * count], grad_rows_ref[...])
-
-    send_slabs(incoming_ref, grad_ref, down_rows, out_ref, buffer, sems, 3 * SH_OWN)
-
-
-def expert_weights(*operands):
-    return pl.pallas_call(
-        expert_weights_kernel,
-        out_shape=jax.ShapeDtypeStruct((D, 3 * SH_OWN + 3 * FF), low),
-        in_specs=[anywhere] + [vmem] * 4,
-        out_specs=anywhere,
-        scratch_shapes=[pltpu.VMEM((2, ROWS, 3 * FF), low), pltpu.SemaphoreType.DMA((2,))],
-        input_output_aliases={0: 0},
-        compiler_params=params(48),
-        cost_estimate=cost(6e9, 24e6),
-        name="expert_weights",
-    )(*operands)
+        cost_estimate=cost(38e9, 70e6, 1e6),
+        name="ffn",
+    )(expert, slots, slots_t, routes, router, *pieces, *cot_pieces, pack)
 
 
 def out_rows_kernel(place_ref, *refs):
@@ -958,7 +914,7 @@
     )
     hidden_pieces = gather_pieces(jnp.concatenate([hidden_in[0], ids], axis=0))
     cot_block, *hidden_pieces = together(cotangent[0], *hidden_pieces)
-    cot_pieces = gather_pieces(cot_block)
+    cot_first = first_pieces(cot_block)
 
     inverse_freq = rope_base ** (-jnp.arange(HD // 2, dtype=wide) * 2.0 / HD)
     angles = jnp.arange(LENGTH).astype(wide)[:, None] * inverse_freq[None, :]
@@ -977,10 +933,11 @@
     target = SH_PART * (put_row // SH_PAD) + put_row % SH_PAD
     target = jnp.where(put_row % SH_PAD < SH_PART, target, -1)
     spread_rows = (jnp.arange(SH_ROWS)[:, None] == target[None, :]).astype(low)
-    attn_all, cos_two, sin_two, cos_all, sin_back, spread, spread_rows = together(
-        attn_all, cos_two, sin_two, cos_all, sin_back, spread, spread_rows
-    )
+    attn_all, cos_two, sin_two, cos_all, sin_back = together(attn_all, cos_two, sin_two, cos_all, sin_back)
     normed_one, sent, factor_one, gains, ids_all = project(hidden_pieces, attn_all, cos_two, sin_two)
+
+    sent, cot_block, *cot_first = together(sent, cot_block, *cot_first)
+    cot_pieces = other_pieces(cot_block, *cot_first)
     qkv = lax.all_to_all(sent, "fsdp", split_axis=0, concat_axis=0, tiled=True)
 
     ids_all = ids_all.reshape(SEQS, 16, D)
@@ -1026,28 +983,12 @@
 
     base = 3 * SH_OWN
     normed_pieces = gather_pieces(normed_block)
-    (
-        grad_mine,
-        grad_other,
-        gates,
-        hidden_shared,
-        grad_shared,
-        incoming,
-        hidden_expert,
-        gated_rows,
-        grad_rows,
-        grad_expert,
-        shared_down_w,
-    ) = ffn(expert[None], slots, slots_t, route_all, router, normed_pieces, cot_pieces, ffn_all)
-    received = swap_core(grad_other)
-    ffn_grads = shared_weights(normed_pieces, cot_pieces, hidden_shared, grad_shared)
-    received, ffn_grads = together(received, ffn_grads)
-    own_grad, to_above, to_below = scatter_start(grad_mine, received)
-    to_above, to_below, ffn_grads = together(to_above, to_below, ffn_grads)
+    grad_mine, grad_other, gates, ffn_grads, hidden_shared, shared_down_w, gated_rows = ffn(
+        expert[None], slots, slots_t, route_all, router, normed_pieces, cot_pieces, ffn_all
+    )
+    ffn_sums = lax.psum_scatter(ffn_grads, "fsdp", scatter_dimension=0, tiled=True)
+    own_grad, to_above, to_below = scatter_start(grad_mine, swap_core(grad_other))
     from_below, from_above = move_z(to_above, 1), move_z(to_below, -1)
-    ffn_grads = expert_weights(ffn_grads, incoming, hidden_expert, grad_rows, grad_expert)
-    from_below, from_above, ffn_grads = together(from_below, from_above, ffn_grads)
-    ffn_sums = lax.psum_scatter(ffn_grads, "fsdp", scatter_dimension=0, tiled=True)
     back_block, grad_middle, grad_two, grad_logits = back_two(
         own_grad, from_below, from_above, middle, cotangent[0], gains, gates, route_own
     )
@@ -1084,6 +1025,9 @@
     attn_parts, to_above, to_below = together(attn_parts, to_above, to_below)
     own_grad_one = scatter_end(own_grad_one, move_z(to_above, 1), move_z(to_below, -1))
     grad_input = (grad_middle + norm_back(own_hidden, factor_one[:TOK], gain_one, own_grad_one)).astype(low)
+    ffn_sums, _ = together(ffn_sums, attn_grads)
+    shared_shards = lax.all_gather(ffn_sums[:, :base], "expert", axis=0)
+    attn_parts, shared_shards = together(attn_parts, shared_shards)
     attn_sums = jnp.sum(attn_parts.reshape(FSDP, TOK, 3 * HD + 256).astype(wide), axis=0)
 
     own_weight = lax.dynamic_slice_in_dim(qkv_weight, place * TOK, TOK, 0)
@@ -1092,9 +1036,6 @@
     small = [gain_upper, gain_lower, small_sums.T.astype(low), jnp.zeros((TOK, 110), low)]
     shards = jnp.concatenate([attn_sums.astype(low), *small], axis=1)
 
-    ffn_sums, _ = together(ffn_sums, to_above)
-    shared_shards = lax.all_gather(ffn_sums[:, :base], "expert", axis=0)
-    shared_shards, shards = together(shared_shards, shards)
     attn_shards = lax.all_gather(shards, "expert", axis=0)
     grad_shared_gate, grad_shared_up, grad_shared_down = finish_dense(shared_shards, spread, spread_rows)
     grad_w_query, grad_w_key, grad_w_value, grad_w_out, small = finish(attn_shards)

time: 603 us -> 566 us (0.939)
  waiting for transfers between devices: 190 us -> 174 us
  local copies, waits for them, and re-layouts: 71.9 us -> 60.3 us
    pallas_call x2 -> x0, Pallas kernels: 27.1 us -> none  [the longest x1 14.4 us: shared_weights(): pl.pallas_call(shared_weights_kernel, out_shape=jax.ShapeDtypeStruct((D,...]
    pallas_call x1, Pallas kernels: 42.9 us -> 62.8 us  [ffn(): pl.pallas_call(ffn_kernel, out_shape=tuple([jax.ShapeDtypeStruct(shape, l...]
    all_gather x1, waiting for transfers between devices: 18.8 us -> 0.01 us  [per_device(): shared_shards = lax.all_gather(ffn_sums[:, :base], 'expert', axis=0)]
    all_to_all x1, waiting for transfers between devices: 31.9 us -> 17.5 us  [per_device(): lax.all_to_all(attn_grads, 'fsdp', split_axis=0, concat_axis=0, tiled=True)]
    all_gather x1, waiting for transfers between devices: 0.01 us -> 6.64 us  [per_device(): ffn_all = lax.all_gather(ffn_pack, 'fsdp', axis=0, tiled=True)]
    unnamed x173 -> x129, local copies, waits for them, and re-layouts: 35.7 us -> 29.6 us
  transfers between devices with their start and end apart: 73 -> 73, of which waited for: 27 -> 32; matrix products, arithmetic and copies ran while one was open for 15% -> 16% of each run, Pallas kernels for 13% -> 9%
where the time goes in v1:
time: 566 us; the launch traced here: 555 us
  waiting for transfers between devices  174 us (31%)
  Pallas kernels  114 us (20%)
  starting transfers between devices  80.3 us (14%)
  local copies, waits for them, and re-layouts  60.3 us (11%)
  blocking collectives  50.1 us (9%)
  other arithmetic  46.7 us (8%)
  between operations  15.6 us (3%)
  matrix products  14 us (2%)
    ppermute x38, waiting for transfers between devices, move_z(): return lax.ppermute(block, 'expert', shift_pairs(step))  134 us
    pallas_call x1, Pallas kernels, ffn(): pl.pallas_call(ffn_kernel, out_shape=tuple([jax.ShapeDtypeStruct(shape, l...  62.8 us
    ppermute x38, starting transfers between devices, move_z(): return lax.ppermute(block, 'expert', shift_pairs(step))  61.3 us
    unnamed x129, local copies, waits for them, and re-layouts  29.6 us
    all_to_all x1, blocking collectives, per_device(): lax.all_to_all(mixed_head, 'fsdp', split_axis=0, concat_axis=0, tiled=True)  25.2 us
    all_to_all x1, blocking collectives, per_device(): lax.all_to_all(sent_back, 'fsdp', split_axis=0, concat_axis=0, tiled=True)  24.9 us
    all_to_all x1, waiting for transfers between devices, per_device(): lax.all_to_all(attn_grads, 'fsdp', split_axis=0, concat_axis=0, tiled=True)  17.5 us
    dot_general x10, matrix products, product(): lax.dot_general(left, right, (contract, ((), ())), preferred_element_type...  14 us
  transfers between devices with their start and end apart: 73, of which 32 were waited for; matrix products, arithmetic and copies ran while one was open for 16% of the time, Pallas kernels for 9%

profile of v1, /device:TPU:0, one launch (start us, length us, event | category | flops | bytes accessed | tf_op | source)
XLA Modules:
  0.0 555.1 jit_solution(9609300590783695322)
XLA Ops:
  16.3 4.2 collective-permute-start
  20.5 12.6 %collective-permute-done.refs_1_ = bf16[144,2048]{1,0:T(8,128)(2,1)S(1)} collective-permute-done((bf16[144,2048]{1,0:T(8,128)(2,1)S(1)}, bf16[144,2048]{1,0:T(8,128)(2,1)S(1)}, u32[]{:S(2)}, u32[]{:S(2)}) %collective-permute-start) | collective-permute-done | bytes 589856 | tf_op jit(solution)/shard_map/ppermute | solution.py:44
  33.1 3.8 collective-permute-start.3
  37.7 7.4 %collective-permute-done.2.refs_2_ = bf16[64,2048]{1,0:T(8,128)(2,1)} collective-permute-done((bf16[64,2048]{1,0:T(8,128)(2,1)S(1)}, bf16[64,2048]{1,0:T(8,128)(2,1)}, u32[]{:S(2)}, u32[]{:S(2)}) %collective-permute-start.2) | collective-permute-done | bytes 262176 | tf_op jit(solution)/shard_map/ppermute | solution.py:44
  45.7 5.7 %multiply_sine_fusion = (f32[2048,64]{1,0:T(8,128)}, f32[2048,64]{1,0:T(8,128)}, f32[2048,64]{1,0:T(8,128)}) fusion(f32[64]{0:T(128)S(1)} %multiply_power_fusion, f32[2048]{0:T(1024)S(1)} %iota_convert_fusion), kind=kLoop, calls=%fused_computation.24 | loop fusion | flops 262144 | bytes 1581312 | tf_op jit(solution)/shard_map/sin | solution.py:921
  54.1 3.2 collective-permute-start.10
  57.6 3.8 pad_maximum_fusion.1
  68.6 8.8 %project.1 = (bf16[1024,2048]{1,0:T(8,128)(2,1)}, bf16[2048,384]{1,0:T(8,128)(2,1)}, f32[1024,1]{1,0:T(8,128)S(1)}, f32[16,2048]{1,0:T(8,128)S(1)}, bf16[128,2048]{1,0:T(8,128)(2,1)S(1)}) custom-call(bf16[144,2048]{1,0:T(8,128)(2,1)S(1)} %fusion.31.refs_0_, bf16[144,2048]{1,0:T(8,128)(2,1)S(1)} %collective-permute-done.refs_1_, ...), custom_call_target="tpu_custom_call" | custom-call | flops 2200000000 | bytes 16000000 | tf_op jit(solution)/shard_map/project/pallas_call | solution.py:306
  79.0 4.6 all-to-all-start
  85.5 3.2 fusion.103
  112.4 4.1 collective-permute-done.12.refs_2_
  116.6 4.6 collective-permute-done.13.refs_3_
  127.3 8.3 %attend.1 = (bf16[2048,128]{1,0:T(8,128)(2,1)S(1)}, f32[2048,1]{1,0:T(8,128)S(1)}) custom-call(bf16[2048,384]{1,0:T(8,128)(2,1)} %bitcast.5.qkv_ref, f32[1,2048]{1,0:T(1,128)S(1)} %fusion.118.seg_row_ref, f32[128,128]{1,0:T(8,128)S(1)} %pad.14.seg_blocks_ref), custom_call_target="tpu_custom_call" | custom-call | flops 1073741824 | bytes 2097152 | tf_op jit(solution)/shard_map/attend/pallas_call | solution.py:227
  135.6 25.2 %all_to_all.56 = bf16[16,128,128]{2,1,0:T(8,128)(2,1)S(1)} all-to-all(bf16[16,128,128]{2,1,0:T(8,128)(2,1)S(1)} %bitcast.234), channel_id=1, replica_groups=mesh['fsdp'=16,'expert'=8] {'fsdp'}, dimensions={0} | all-to-all | bytes 1048576 | tf_op jit(solution)/shard_map/all_to_all | solution.py:970
  163.2 3.1 collective-permute-done.22
  170.8 6.3 %collective-permute-done.23 = bf16[64,2048]{1,0:T(8,128)(2,1)S(1)} collective-permute-done((bf16[64,2048]{1,0:T(8,128)(2,1)S(1)}, bf16[64,2048]{1,0:T(8,128)(2,1)S(1)}, u32[]{:S(2)}, u32[]{:S(2)}) %collective-permute-start.23) | collective-permute-done | bytes 262176 | tf_op jit(solution)/shard_map/ppermute | solution.py:44
  180.4 10.3 %collective-permute-done.26 = bf16[128,2048]{1,0:T(8,128)(2,1)S(1)} collective-permute-done((bf16[128,2048]{1,0:T(8,128)(2,1)S(1)}, bf16[128,2048]{1,0:T(8,128)(2,1)S(1)}, u32[]{:S(2)}, u32[]{:S(2)}) %collective-permute-start.26) | collective-permute-done | bytes 524320 | tf_op jit(solution)/shard_map/ppermute | solution.py:44
  190.7 3.5 collective-permute-done.24
  194.9 3.2 collective-permute-start.27
  198.2 9.8 %collective-permute-done.28.refs_9_ = bf16[128,2048]{1,0:T(8,128)(2,1)S(1)} collective-permute-done((bf16[128,2048]{1,0:T(8,128)(2,1)S(1)}, bf16[128,2048]{1,0:T(8,128)(2,1)S(1)}, u32[]{:S(2)}, u32[]{:S(2)}) %collective-permute-start.28) | collective-permute-done | bytes 524320 | tf_op jit(solution)/shard_map/ppermute | solution.py:44
  208.2 3.2 collective-permute-start.30
  211.6 4.0 collective-permute-done.29.refs_7_
  220.2 6.6 %all-gather.9.cloned.1.call-done.refs_25_ = bf16[2048,5376]{1,0:T(8,128)(2,1)} async-done(((bf16[128,5376]{1,0:T(8,128)(2,1)}), bf16[2048,5376]{1,0:T(8,128)(2,1)}) %all-gather.9.cloned.1.call-update) | async-done | bytes 22020112 | tf_op jit(solution)/shard_map/all_gather | solution.py:905
  226.9 62.8 %ffn.1 = (bf16[512,2176]{1,0:T(8,128)(2,1)}, bf16[512,2176]{1,0:T(8,128)(2,1)}, f32[128,128]{1,0:T(8,128)}, bf16[2048,5376]{1,0:T(8,128)(2,1)}, bf16[1024,384]{1...) custom-call(s32[1]{0:T(128)} %bitcast.35.refs_0_, bf16[336,1024]{1,0:T(8,128)(2,1)} %fusion.13.refs_1_, ...), custom_call_target="tpu_custom_call" | custom-call | flops 38000001024 | bytes 70000000 | tf_op jit(solution)/shard_map/ffn/pallas_call | solution.py:706
  289.8 4.5 collective-permute-done.36
  299.8 6.2 %collective-permute-done.39 = bf16[64,2176]{1,0:T(8,128)(2,1)S(1)} collective-permute-done((bf16[64,2176]{1,0:T(8,128)(2,1)S(1)}, bf16[64,2176]{1,0:T(8,128)(2,1)S(1)}, u32[]{:S(2)}, u32[]{:S(2)}) %collective-permute-start.39) | collective-permute-done | bytes 278560 | tf_op jit(solution)/shard_map/ppermute | solution.py:44
  306.0 3.4 collective-permute-done.37
  309.7 3.3 collective-permute-start.40
  313.1 11.4 %collective-permute-done.38.first_ref = bf16[128,2176]{1,0:T(8,128)(2,1)S(1)} collective-permute-done((bf16[128,2176]{1,0:T(8,128)(2,1)S(1)}, bf16[128,2176]{1,0:T(8,128)(2,1)S(1)}, u32[]{:S(2)}, u32[]{:S(2)}) %collective-permute-start.38) | collective-permute-done | bytes 557088 | tf_op jit(solution)/shard_map/ppermute | solution.py:44
  324.5 3.5 back_two.1
  328.0 3.2 collective-permute-start.42
  347.2 3.7 collective-permute-done.43.refs_2_
  356.3 7.1 %mix_back.1 = (bf16[2304,128]{1,0:T(8,128)(2,1)}, bf16[4,256,256]{2,1,0:T(8,128)(2,1)}, bf16[4,256,256]{2,1,0:T(8,128)(2,1)}) custom-call(s32[8]{0:T(128)} %stack.95.place_ref, bf16[128,2048]{1,0:T(8,128)(2,1)} %get-tuple-element.168.refs_0_, bf16[128,2048]{1,0:T(8,128)(2,1)} %collective-permute-done.42.refs_1_, ...), custom_call_target="tpu_custom_call" | custom-call | flops 2200000000 | bytes 10000000 | tf_op jit(solution)/shard_map/mix_back/pallas_call | solution.py:348
  363.9 24.9 %all_to_all.57 = bf16[16,144,128]{2,1,0:T(8,128)(2,1)S(1)} all-to-all(bf16[16,144,128]{2,1,0:T(8,128)(2,1)} %bitcast.257), channel_id=1, replica_groups=mesh['fsdp'=16,'expert'=8] {'fsdp'}, dimensions={0} | all-to-all | bytes 1179648 | tf_op jit(solution)/shard_map/all_to_all | solution.py:1004
  391.4 10.5 %attend_back.1 = (bf16[2048,384]{1,0:T(8,128)(2,1)S(1)}, f32[16,128]{1,0:T(8,128)S(1)}) custom-call(bf16[2048,384]{1,0:T(8,128)(2,1)} %bitcast.5.qkv_ref, bf16[2304,128]{1,0:T(8,128)(2,1)S(1)} %bitcast.233, f32[2048,1]{1,0:T(8,128)S(1)} %copy-done.25, f32[1,2048]{1,0:T(1,128)S(1)} %fusion.118.seg_row_ref, f32[128,128]{1,0:T(8,128)S(1)} %pad.14.seg_blocks_ref, ...), custom_call_target="tpu_custom_call" | custom-call | flops 2684354560 | bytes 4194304 | tf_op jit(solution)/shard_map/attend_back/pallas_call | solution.py:244
  403.0 3.7 all-to-all-start.3
  406.8 3.1 convert_add_fusion.2
  414.1 5.6 %collective-permute-done.51 = bf16[64,2048]{1,0:T(8,128)(2,1)S(1)} collective-permute-done((bf16[64,2048]{1,0:T(8,128)(2,1)S(1)}, bf16[64,2048]{1,0:T(8,128)(2,1)S(1)}, u32[]{:S(2)}, u32[]{:S(2)}) %collective-permute-start.51) | collective-permute-done | bytes 262176 | tf_op jit(solution)/shard_map/ppermute | solution.py:44
  419.9 3.1 collective-permute-start.54
  424.8 4.1 collective-permute-start.57
  429.6 11.4 %collective-permute-done.54 = bf16[128,2048]{1,0:T(8,128)(2,1)S(1)} collective-permute-done((bf16[128,2048]{1,0:T(8,128)(2,1)S(1)}, bf16[128,2048]{1,0:T(8,128)(2,1)S(1)}, u32[]{:S(2)}, u32[]{:S(2)}) %collective-permute-start.54) | collective-permute-done | bytes 524320 | tf_op jit(solution)/shard_map/ppermute | solution.py:44
  444.3 3.6 collective-permute-done.56.refs_2_
  456.8 5.1 qkv_weights.1
  466.3 6.5 %all-to-all-start.4 = ((bf16[16,128,640]{2,1,0:T(8,128)(2,1)}), bf16[16,128,640]{2,1,0:T(8,128)(2,1)}, u32[]{:S(2)}, u32[]{:S(2)}) async-start(bf16[16,128,640]{2,1,0:T(8,128)(2,1)} %bitcast.83), calls=%async_computation.4 | async-start | bytes 5242880 | tf_op jit(solution)/shard_map/all_to_all | solution.py:1020
  481.4 11.4 %collective-permute-done.62 = bf16[64,2048]{1,0:T(8,128)(2,1)S(1)} collective-permute-done((bf16[64,2048]{1,0:T(8,128)(2,1)S(1)}, bf16[64,2048]{1,0:T(8,128)(2,1)S(1)}, u32[]{:S(2)}, u32[]{:S(2)}) %collective-permute-start.62) | collective-permute-done | bytes 262176 | tf_op jit(solution)/shard_map/ppermute | solution.py:44
  496.5 17.5 %all-to-all-done.4 = bf16[16,128,640]{2,1,0:T(8,128)(2,1)} async-done(((bf16[16,128,640]{2,1,0:T(8,128)(2,1)}), bf16[16,128,640]{2,1,0:T(8,128)(2,1)}, u32[]{:S(2)}, u32[]{:S(2)}) %all-to-all-start.4) | async-done | bytes 2621472 | tf_op jit(solution)/shard_map/all_to_all | solution.py:1020
  522.5 4.9 collective-permute-done.64
  539.2 4.6 finish_dense.1
  (384 shorter events, 160.8 us)
Async XLA Ops:
  7.2 57.3 %all-gather.7.cloned.1.call-start = ((), (), s32[]{:S(2)}) async-start(), calls=%async_computation.6 | async-start | bytes 3899392 | tf_op jit(solution)/shard_map/all_gather | solution.py:875
  12.3 214.6 %all-gather.9.cloned.1.call-start = ((), (), s32[]{:S(2)}) async-start(), calls=%async_computation.7 | async-start | bytes 23396352 | tf_op jit(solution)/shard_map/all_gather | solution.py:905
  16.3 16.8 %collective-permute-start = (bf16[144,2048]{1,0:T(8,128)(2,1)S(1)}, bf16[144,2048]{1,0:T(8,128)(2,1)S(1)}, u32[]{:S(2)}, u32[]{:S(2)}) collective-permute-start(bf16[144,2048]{1,0:T(8,128)(2,1)S(1)} %fusion.31.refs_0_), channel_id=1, source_target_pairs={{0,6},{1,7},{2,0},{3,1},{4,2},{5,3},{6,4},{7,5},{8,14},{9,15},{10,... | collective-permute-start | bytes 1769480 | tf_op jit(solution)/shard_map/ppermute | solution.py:44
  20.5 16.4 %collective-permute-start.1 = (bf16[144,2048]{1,0:T(8,128)(2,1)S(1)}, bf16[144,2048]{1,0:T(8,128)(2,1)S(1)}, u32[]{:S(2)}, u32[]{:S(2)}) collective-permute-start(bf16[144,2048]{1,0:T(8,128)(2,1)S(1)} %fusion.31.refs_0_), channel_id=1, source_target_pairs={{0,2},{1,3},{2,4},{3,5},{4,6},{5,7},{6,0},{7,1},{8,10},{9,11},{10,... | collective-permute-start | bytes 1769480 | tf_op jit(solution)/shard_map/ppermute | solution.py:44
  33.1 12.1 %collective-permute-start.3 = (bf16[80,2048]{1,0:T(8,128)(2,1)S(1)}, bf16[80,2048]{1,0:T(8,128)(2,1)S(1)}, u32[]{:S(2)}, u32[]{:S(2)}) collective-permute-start(bf16[80,2048]{1,0:T(8,128)(2,1)S(1)} %slice.392), channel_id=1, source_target_pairs={{0,6},{1,7},{2,0},{3,1},{4,2},{5,3},{6,4},{7,5},{8,14},{9,15},{10,... | collective-permute-start | bytes 983048 | tf_op jit(solution)/shard_map/ppermute | solution.py:44
  37.0 15.5 %collective-permute-start.4 = (bf16[144,2048]{1,0:T(8,128)(2,1)S(1)}, bf16[144,2048]{1,0:T(8,128)(2,1)S(1)}, u32[]{:S(2)}, u32[]{:S(2)}) collective-permute-start(bf16[144,2048]{1,0:T(8,128)(2,1)S(1)} %fusion.31.refs_0_), channel_id=1, source_target_pairs={{0,1},{1,0},{2,3},{3,2},{4,5},{5,4},{6,7},{7,6},{8,9},{9,8},{10,11... | collective-permute-start | bytes 1769480 | tf_op jit(solution)/shard_map/ppermute | solution.py:48
  37.1 16.2 %collective-permute-start.5 = (bf16[144,2048]{1,0:T(8,128)(2,1)S(1)}, bf16[144,2048]{1,0:T(8,128)(2,1)S(1)}, u32[]{:S(2)}, u32[]{:S(2)}) collective-permute-start(bf16[144,2048]{1,0:T(8,128)(2,1)S(1)} %collective-permute-done.refs_1_), channel_id=1, source_target_pairs={{0,1},{1,0},{2,3},{3,2},{4,5},{5,4},{6,7},{7,6},{8,9},{9,8},{10,11... | collective-permute-start | bytes 1769480 | tf_op jit(solution)/shard_map/ppermute | solution.py:48
  37.6 16.4 %collective-permute-start.8 = (bf16[144,2048]{1,0:T(8,128)(2,1)S(1)}, bf16[144,2048]{1,0:T(8,128)(2,1)}, u32[]{:S(2)}, u32[]{:S(2)}) collective-permute-start(bf16[144,2048]{1,0:T(8,128)(2,1)S(1)} %collective-permute-done.1.refs_4_), channel_id=1, source_target_pairs={{0,1},{1,0},{2,3},{3,2},{4,5},{5,4},{6,7},{7,6},{8,9},{9,8},{10,11... | collective-permute-start | bytes 1769480 | tf_op jit(solution)/shard_map/ppermute | solution.py:48
  54.1 24.9 %collective-permute-start.9 = (bf16[128,2048]{1,0:T(8,128)(2,1)}, bf16[128,2048]{1,0:T(8,128)(2,1)}, u32[]{:S(2)}, u32[]{:S(2)}) collective-permute-start(bf16[128,2048]{1,0:T(8,128)(2,1)} %bitcast.refs_15_.cot_ref), channel_id=1, source_target_pairs={{0,2},{1,3},{2,4},{3,5},{4,6},{5,7},{6,0},{7,1},{8,10},{9,11},{10,... | collective-permute-start | bytes 1572872 | tf_op jit(solution)/shard_map/ppermute | solution.py:44
  54.1 24.9 %collective-permute-start.10 = (bf16[128,2048]{1,0:T(8,128)(2,1)}, bf16[128,2048]{1,0:T(8,128)(2,1)}, u32[]{:S(2)}, u32[]{:S(2)}) collective-permute-start(bf16[128,2048]{1,0:T(8,128)(2,1)} %bitcast.refs_15_.cot_ref), channel_id=1, source_target_pairs={{0,6},{1,7},{2,0},{3,1},{4,2},{5,3},{6,4},{7,5},{8,14},{9,15},{10,... | collective-permute-start | bytes 1572872 | tf_op jit(solution)/shard_map/ppermute | solution.py:44
  79.0 48.3 %all-to-all-start = ((bf16[16,128,384]{2,1,0:T(8,128)(2,1)}), bf16[16,128,384]{2,1,0:T(8,128)(2,1)}, u32[]{:S(2)}, u32[]{:S(2)}) async-start(bf16[16,128,384]{2,1,0:T(8,128)(2,1)} %bitcast.4), calls=%async_computation | async-start | bytes 3145728 | tf_op jit(solution)/shard_map/all_to_all | solution.py:941
  83.6 381.0 %reduce-scatter.2.cloned.1.call-start = ((), (), s32[]{:S(2)}) async-start(), calls=%async_computation.8 | async-start | bytes 23396352 | tf_op jit(solution)/shard_map/reduce_scatter | solution.py:989
  89.6 15.4 %collective-permute-start.11 = (bf16[4,256,256]{2,1,0:T(8,128)(2,1)}, bf16[4,256,256]{2,1,0:T(8,128)(2,1)}, u32[]{:S(2)}, u32[]{:S(2)}) collective-permute-start(bf16[4,256,256]{2,1,0:T(8,128)(2,1)} %pad_maximum_fusion.6), channel_id=1, source_target_pairs={{0,1},{1,0},{2,3},{3,2},{4,5},{5,4},{6,7},{7,6},{8,9},{9,8},{10,11... | collective-permute-start | bytes 1572872 | tf_op jit(solution)/shard_map/ppermute | solution.py:48
  98.1 13.7 %collective-permute-start.15 = (bf16[64,2048]{1,0:T(8,128)(2,1)S(1)}, bf16[64,2048]{1,0:T(8,128)(2,1)}, u32[]{:S(2)}, u32[]{:S(2)}) collective-permute-start(bf16[64,2048]{1,0:T(8,128)(2,1)S(1)} %slice.318), channel_id=1, source_target_pairs={{0,2},{1,3},{2,4},{3,5},{4,6},{5,7},{6,0},{7,1},{8,10},{9,11},{10,... | collective-permute-start | bytes 786440 | tf_op jit(solution)/shard_map/ppermute | solution.py:44
  100.7 11.3 %collective-permute-start.16 = (bf16[64,2048]{1,0:T(8,128)(2,1)S(1)}, bf16[64,2048]{1,0:T(8,128)(2,1)}, u32[]{:S(2)}, u32[]{:S(2)}) collective-permute-start(bf16[64,2048]{1,0:T(8,128)(2,1)S(1)} %slice.319), channel_id=1, source_target_pairs={{0,6},{1,7},{2,0},{3,1},{4,2},{5,3},{6,4},{7,5},{8,14},{9,15},{10,... | collective-permute-start | bytes 786440 | tf_op jit(solution)/shard_map/ppermute | solution.py:44
  106.1 10.5 %collective-permute-start.12 = (bf16[2,256,256]{2,1,0:T(8,128)(2,1)S(1)}, bf16[2,256,256]{2,1,0:T(8,128)(2,1)S(1)}, u32[]{:S(2)}, u32[]{:S(2)}) collective-permute-start(bf16[2,256,256]{2,1,0:T(8,128)(2,1)S(1)} %get-tuple-element.333), channel_id=1, source_target_pairs={{0,2},{1,3},{2,4},{3,5},{4,6},{5,7},{6,0},{7,1},{8,10},{9,11},{10,... | collective-permute-start | bytes 786440 | tf_op jit(solution)/shard_map/ppermute | solution.py:44
  107.5 13.7 %collective-permute-start.13 = (bf16[2,256,256]{2,1,0:T(8,128)(2,1)S(1)}, bf16[2,256,256]{2,1,0:T(8,128)(2,1)S(1)}, u32[]{:S(2)}, u32[]{:S(2)}) collective-permute-start(bf16[2,256,256]{2,1,0:T(8,128)(2,1)S(1)} %get-tuple-element.334), channel_id=1, source_target_pairs={{0,4},{1,5},{2,6},{3,7},{4,0},{5,1},{6,2},{7,3},{8,12},{9,13},{10,... | collective-permute-start | bytes 786440 | tf_op jit(solution)/shard_map/ppermute | solution.py:44
  110.5 12.4 %collective-permute-start.14 = (bf16[2,256,256]{2,1,0:T(8,128)(2,1)S(1)}, bf16[2,256,256]{2,1,0:T(8,128)(2,1)S(1)}, u32[]{:S(2)}, u32[]{:S(2)}) collective-permute-start(bf16[2,256,256]{2,1,0:T(8,128)(2,1)S(1)} %get-tuple-element.332), channel_id=1, source_target_pairs={{0,6},{1,7},{2,0},{3,1},{4,2},{5,3},{6,4},{7,5},{8,14},{9,15},{10,... | collective-permute-start | bytes 786440 | tf_op jit(solution)/shard_map/ppermute | solution.py:44
  111.9 15.4 %collective-permute-start.18 = (bf16[128,2048]{1,0:T(8,128)(2,1)}, bf16[128,2048]{1,0:T(8,128)(2,1)}, u32[]{:S(2)}, u32[]{:S(2)}) collective-permute-start(bf16[128,2048]{1,0:T(8,128)(2,1)} %collective-permute-done.10.refs_16_), channel_id=1, source_target_pairs={{0,1},{1,0},{2,3},{3,2},{4,5},{5,4},{6,7},{7,6},{8,9},{9,8},{10,11... | collective-permute-start | bytes 1572872 | tf_op jit(solution)/shard_map/ppermute | solution.py:48
  112.0 15.3 %collective-permute-start.21 = (bf16[128,2048]{1,0:T(8,128)(2,1)}, bf16[128,2048]{1,0:T(8,128)(2,1)}, u32[]{:S(2)}, u32[]{:S(2)}) collective-permute-start(bf16[128,2048]{1,0:T(8,128)(2,1)} %collective-permute-done.9.refs_19_), channel_id=1, source_target_pairs={{0,1},{1,0},{2,3},{3,2},{4,5},{5,4},{6,7},{7,6},{8,9},{9,8},{10,11... | collective-permute-start | bytes 1572872 | tf_op jit(solution)/shard_map/ppermute | solution.py:48
  116.6 10.6 %collective-permute-start.17 = (bf16[128,2048]{1,0:T(8,128)(2,1)}, bf16[128,2048]{1,0:T(8,128)(2,1)}, u32[]{:S(2)}, u32[]{:S(2)}) collective-permute-start(bf16[128,2048]{1,0:T(8,128)(2,1)} %bitcast.refs_15_.cot_ref), channel_id=1, source_target_pairs={{0,1},{1,0},{2,3},{3,2},{4,5},{5,4},{6,7},{7,6},{8,9},{9,8},{10,11... | collective-permute-start | bytes 1572872 | tf_op jit(solution)/shard_map/ppermute | solution.py:48
  177.3 13.5 %collective-permute-start.26 = (bf16[128,2048]{1,0:T(8,128)(2,1)S(1)}, bf16[128,2048]{1,0:T(8,128)(2,1)S(1)}, u32[]{:S(2)}, u32[]{:S(2)}) collective-permute-start(bf16[128,2048]{1,0:T(8,128)(2,1)S(1)} %pad_maximum_fusion.8), channel_id=1, source_target_pairs={{0,6},{1,7},{2,0},{3,1},{4,2},{5,3},{6,4},{7,5},{8,14},{9,15},{10,... | collective-permute-start | bytes 1572872 | tf_op jit(solution)/shard_map/ppermute | solution.py:44
  180.3 13.9 %collective-permute-start.24 = (bf16[128,2048]{1,0:T(8,128)(2,1)S(1)}, bf16[128,2048]{1,0:T(8,128)(2,1)S(1)}, u32[]{:S(2)}, u32[]{:S(2)}) collective-permute-start(bf16[128,2048]{1,0:T(8,128)(2,1)S(1)} %pad_maximum_fusion.7), channel_id=1, source_target_pairs={{0,2},{1,3},{2,4},{3,5},{4,6},{5,7},{6,0},{7,1},{8,10},{9,11},{10,... | collective-permute-start | bytes 1572872 | tf_op jit(solution)/shard_map/ppermute | solution.py:44
  194.8 13.1 %collective-permute-start.28 = (bf16[128,2048]{1,0:T(8,128)(2,1)S(1)}, bf16[128,2048]{1,0:T(8,128)(2,1)S(1)}, u32[]{:S(2)}, u32[]{:S(2)}) collective-permute-start(bf16[128,2048]{1,0:T(8,128)(2,1)S(1)} %multiply_convert_fusion.refs_5_), channel_id=1, source_target_pairs={{0,2},{1,3},{2,4},{3,5},{4,6},{5,7},{6,0},{7,1},{8,10},{9,11},{10,... | collective-permute-start | bytes 1572872 | tf_op jit(solution)/shard_map/ppermute | solution.py:44
  194.9 13.1 %collective-permute-start.27 = (bf16[128,2048]{1,0:T(8,128)(2,1)S(1)}, bf16[128,2048]{1,0:T(8,128)(2,1)S(1)}, u32[]{:S(2)}, u32[]{:S(2)}) collective-permute-start(bf16[128,2048]{1,0:T(8,128)(2,1)S(1)} %multiply_convert_fusion.refs_5_), channel_id=1, source_target_pairs={{0,6},{1,7},{2,0},{3,1},{4,2},{5,3},{6,4},{7,5},{8,14},{9,15},{10,... | collective-permute-start | bytes 1572872 | tf_op jit(solution)/shard_map/ppermute | solution.py:44
  198.2 19.9 %collective-permute-start.31 = (bf16[128,2048]{1,0:T(8,128)(2,1)S(1)}, bf16[128,2048]{1,0:T(8,128)(2,1)S(1)}, u32[]{:S(2)}, u32[]{:S(2)}) collective-permute-start(bf16[128,2048]{1,0:T(8,128)(2,1)S(1)} %multiply_convert_fusion.refs_5_), channel_id=1, source_target_pairs={{0,1},{1,0},{2,3},{3,2},{4,5},{5,4},{6,7},{7,6},{8,9},{9,8},{10,11... | collective-permute-start | bytes 1572872 | tf_op jit(solution)/shard_map/ppermute | solution.py:48
  208.1 10.0 %collective-permute-start.32 = (bf16[128,2048]{1,0:T(8,128)(2,1)S(1)}, bf16[128,2048]{1,0:T(8,128)(2,1)S(1)}, u32[]{:S(2)}, u32[]{:S(2)}) collective-permute-start(bf16[128,2048]{1,0:T(8,128)(2,1)S(1)} %collective-permute-done.27.refs_6_), channel_id=1, source_target_pairs={{0,1},{1,0},{2,3},{3,2},{4,5},{5,4},{6,7},{7,6},{8,9},{9,8},{10,11... | collective-permute-start | bytes 1572872 | tf_op jit(solution)/shard_map/ppermute | solution.py:48
  309.5 14.9 %collective-permute-start.38 = (bf16[128,2176]{1,0:T(8,128)(2,1)S(1)}, bf16[128,2176]{1,0:T(8,128)(2,1)S(1)}, u32[]{:S(2)}, u32[]{:S(2)}) collective-permute-start(bf16[128,2176]{1,0:T(8,128)(2,1)S(1)} %pad_maximum_fusion.3), channel_id=1, source_target_pairs={{0,2},{1,3},{2,4},{3,5},{4,6},{5,7},{6,0},{7,1},{8,10},{9,11},{10,... | collective-permute-start | bytes 1671176 | tf_op jit(solution)/shard_map/ppermute | solution.py:44
  309.7 14.8 %collective-permute-start.40 = (bf16[128,2176]{1,0:T(8,128)(2,1)S(1)}, bf16[128,2176]{1,0:T(8,128)(2,1)S(1)}, u32[]{:S(2)}, u32[]{:S(2)}) collective-permute-start(bf16[128,2176]{1,0:T(8,128)(2,1)S(1)} %pad_maximum_fusion.4), channel_id=1, source_target_pairs={{0,6},{1,7},{2,0},{3,1},{4,2},{5,3},{6,4},{7,5},{8,14},{9,15},{10,... | collective-permute-start | bytes 1671176 | tf_op jit(solution)/shard_map/ppermute | solution.py:44
  327.9 13.7 %collective-permute-start.41 = (bf16[128,2048]{1,0:T(8,128)(2,1)}, bf16[128,2048]{1,0:T(8,128)(2,1)}, u32[]{:S(2)}, u32[]{:S(2)}) collective-permute-start(bf16[128,2048]{1,0:T(8,128)(2,1)} %get-tuple-element.168.refs_0_), channel_id=1, source_target_pairs={{0,2},{1,3},{2,4},{3,5},{4,6},{5,7},{6,0},{7,1},{8,10},{9,11},{10,... | collective-permute-start | bytes 1572872 | tf_op jit(solution)/shard_map/ppermute | solution.py:44
  328.0 13.7 %collective-permute-start.42 = (bf16[128,2048]{1,0:T(8,128)(2,1)}, bf16[128,2048]{1,0:T(8,128)(2,1)}, u32[]{:S(2)}, u32[]{:S(2)}) collective-permute-start(bf16[128,2048]{1,0:T(8,128)(2,1)} %get-tuple-element.168.refs_0_), channel_id=1, source_target_pairs={{0,6},{1,7},{2,0},{3,1},{4,2},{5,3},{6,4},{7,5},{8,14},{9,15},{10,... | collective-permute-start | bytes 1572872 | tf_op jit(solution)/shard_map/ppermute | solution.py:44
  331.2 24.4 %collective-permute-start.45 = (bf16[128,2048]{1,0:T(8,128)(2,1)}, bf16[128,2048]{1,0:T(8,128)(2,1)}, u32[]{:S(2)}, u32[]{:S(2)}) collective-permute-start(bf16[128,2048]{1,0:T(8,128)(2,1)} %get-tuple-element.168.refs_0_), channel_id=1, source_target_pairs={{0,1},{1,0},{2,3},{3,2},{4,5},{5,4},{6,7},{7,6},{8,9},{9,8},{10,11... | collective-permute-start | bytes 1572872 | tf_op jit(solution)/shard_map/ppermute | solution.py:48
  344.6 11.0 %collective-permute-start.46 = (bf16[128,2048]{1,0:T(8,128)(2,1)}, bf16[128,2048]{1,0:T(8,128)(2,1)}, u32[]{:S(2)}, u32[]{:S(2)}) collective-permute-start(bf16[128,2048]{1,0:T(8,128)(2,1)} %collective-permute-done.42.refs_1_), channel_id=1, source_target_pairs={{0,1},{1,0},{2,3},{3,2},{4,5},{5,4},{6,7},{7,6},{8,9},{9,8},{10,11... | collective-permute-start | bytes 1572872 | tf_op jit(solution)/shard_map/ppermute | solution.py:48
  363.4 43.4 %collective-permute-start.50 = (bf16[512,2048]{1,0:T(8,128)(2,1)}, bf16[512,2048]{1,0:T(8,128)(2,1)}, u32[]{:S(2)}, u32[]{:S(2)}) collective-permute-start(bf16[512,2048]{1,0:T(8,128)(2,1)} %add_convert_fusion.1), channel_id=1, source_target_pairs={{0,1},{1,0},{2,3},{3,2},{4,5},{5,4},{6,7},{7,6},{8,9},{9,8},{10,11... | collective-permute-start | bytes 6291464 | tf_op jit(solution)/shard_map/ppermute | solution.py:48
  403.0 41.2 %all-to-all-start.3 = ((bf16[16,128,384]{2,1,0:T(8,128)(2,1)}), bf16[16,128,384]{2,1,0:T(8,128)(2,1)S(1)}, u32[]{:S(2)}, u32[]{:S(2)}) async-start(bf16[16,128,384]{2,1,0:T(8,128)(2,1)} %bitcast.231), calls=%async_computation.3 | async-start | bytes 3145728 | tf_op jit(solution)/shard_map/all_to_all | solution.py:1006
  406.8 109.4 %all-gather.11.cloned.1.call-start = ((), (), s32[]{:S(2)}) async-start(), calls=%async_computation.9 | async-start | bytes 2654208 | tf_op jit(solution)/shard_map/all_gather | solution.py:1029
  419.9 21.1 %collective-permute-start.54 = (bf16[128,2048]{1,0:T(8,128)(2,1)S(1)}, bf16[128,2048]{1,0:T(8,128)(2,1)S(1)}, u32[]{:S(2)}, u32[]{:S(2)}) collective-permute-start(bf16[128,2048]{1,0:T(8,128)(2,1)S(1)} %pad_maximum_fusion.10), channel_id=1, source_target_pairs={{0,6},{1,7},{2,0},{3,1},{4,2},{5,3},{6,4},{7,5},{8,14},{9,15},{10,... | collective-permute-start | bytes 1572872 | tf_op jit(solution)/shard_map/ppermute | solution.py:44
  423.0 18.0 %collective-permute-start.52 = (bf16[128,2048]{1,0:T(8,128)(2,1)S(1)}, bf16[128,2048]{1,0:T(8,128)(2,1)S(1)}, u32[]{:S(2)}, u32[]{:S(2)}) collective-permute-start(bf16[128,2048]{1,0:T(8,128)(2,1)S(1)} %pad_maximum_fusion.9), channel_id=1, source_target_pairs={{0,2},{1,3},{2,4},{3,5},{4,6},{5,7},{6,0},{7,1},{8,10},{9,11},{10,... | collective-permute-start | bytes 1572872 | tf_op jit(solution)/shard_map/ppermute | solution.py:44
  424.2 23.6 %collective-permute-start.56 = (bf16[2,256,256]{2,1,0:T(8,128)(2,1)}, bf16[2,256,256]{2,1,0:T(8,128)(2,1)S(1)}, u32[]{:S(2)}, u32[]{:S(2)}) collective-permute-start(bf16[2,256,256]{2,1,0:T(8,128)(2,1)} %get-tuple-element.330), channel_id=1, source_target_pairs={{0,2},{1,3},{2,4},{3,5},{4,6},{5,7},{6,0},{7,1},{8,10},{9,11},{10,... | collective-permute-start | bytes 786440 | tf_op jit(solution)/shard_map/ppermute | solution.py:44
  424.8 23.7 %collective-permute-start.57 = (bf16[2,256,256]{2,1,0:T(8,128)(2,1)}, bf16[2,256,256]{2,1,0:T(8,128)(2,1)S(1)}, u32[]{:S(2)}, u32[]{:S(2)}) collective-permute-start(bf16[2,256,256]{2,1,0:T(8,128)(2,1)} %get-tuple-element.331), channel_id=1, source_target_pairs={{0,4},{1,5},{2,6},{3,7},{4,0},{5,1},{6,2},{7,3},{8,12},{9,13},{10,... | collective-permute-start | bytes 786440 | tf_op jit(solution)/shard_map/ppermute | solution.py:44
  428.9 20.3 %collective-permute-start.58 = (bf16[2,256,256]{2,1,0:T(8,128)(2,1)}, bf16[2,256,256]{2,1,0:T(8,128)(2,1)}, u32[]{:S(2)}, u32[]{:S(2)}) collective-permute-start(bf16[2,256,256]{2,1,0:T(8,128)(2,1)} %get-tuple-element.329), channel_id=1, source_target_pairs={{0,6},{1,7},{2,0},{3,1},{4,2},{5,3},{6,4},{7,5},{8,14},{9,15},{10,... | collective-permute-start | bytes 786440 | tf_op jit(solution)/shard_map/ppermute | solution.py:44
  464.4 9.7 %collective-permute-start.60 = (bf16[512,2048]{1,0:T(8,128)(2,1)}, bf16[512,2048]{1,0:T(8,128)(2,1)}, u32[]{:S(2)}, u32[]{:S(2)}) collective-permute-start(bf16[512,2048]{1,0:T(8,128)(2,1)} %convolution_convert_fusion.2), channel_id=1, source_target_pairs={{0,1},{1,0},{2,3},{3,2},{4,5},{5,4},{6,7},{7,6},{8,9},{9,8},{10,11... | collective-permute-start | bytes 6291464 | tf_op jit(solution)/shard_map/ppermute | solution.py:48
  466.3 47.7 %all-to-all-start.4 = ((bf16[16,128,640]{2,1,0:T(8,128)(2,1)}), bf16[16,128,640]{2,1,0:T(8,128)(2,1)}, u32[]{:S(2)}, u32[]{:S(2)}) async-start(bf16[16,128,640]{2,1,0:T(8,128)(2,1)} %bitcast.83), calls=%async_computation.4 | async-start | bytes 5242880 | tf_op jit(solution)/shard_map/all_to_all | solution.py:1020
  472.8 71.0 %all-gather.13.cloned.1.call-start = ((), (), s32[]{:S(2)}) async-start(), calls=%async_computation.10 | async-start | bytes 1769472 | tf_op jit(solution)/shard_map/all_gather | solution.py:1039
  479.1 13.7 %collective-permute-start.62 = (bf16[64,2048]{1,0:T(8,128)(2,1)S(1)}, bf16[64,2048]{1,0:T(8,128)(2,1)S(1)}, u32[]{:S(2)}, u32[]{:S(2)}) collective-permute-start(bf16[64,2048]{1,0:T(8,128)(2,1)S(1)} %get-tuple-element.307), channel_id=1, source_target_pairs={{0,6},{1,7},{2,0},{3,1},{4,2},{5,3},{6,4},{7,5},{8,14},{9,15},{10,... | collective-permute-start | bytes 786440 | tf_op jit(solution)/shard_map/ppermute | solution.py:44
  479.2 14.3 %collective-permute-start.61 = (bf16[64,2048]{1,0:T(8,128)(2,1)S(1)}, bf16[64,2048]{1,0:T(8,128)(2,1)S(1)}, u32[]{:S(2)}, u32[]{:S(2)}) collective-permute-start(bf16[64,2048]{1,0:T(8,128)(2,1)S(1)} %get-tuple-element.309), channel_id=1, source_target_pairs={{0,2},{1,3},{2,4},{3,5},{4,6},{5,7},{6,0},{7,1},{8,10},{9,11},{10,... | collective-permute-start | bytes 786440 | tf_op jit(solution)/shard_map/ppermute | solution.py:44
  514.0 13.4 %collective-permute-start.64 = (bf16[128,2048]{1,0:T(8,128)(2,1)}, bf16[128,2048]{1,0:T(8,128)(2,1)}, u32[]{:S(2)}, u32[]{:S(2)}) collective-permute-start(bf16[128,2048]{1,0:T(8,128)(2,1)} %pad_maximum_fusion.12), channel_id=1, source_target_pairs={{0,6},{1,7},{2,0},{3,1},{4,2},{5,3},{6,4},{7,5},{8,14},{9,15},{10,... | collective-permute-start | bytes 1572872 | tf_op jit(solution)/shard_map/ppermute | solution.py:44
  514.0 14.8 %collective-permute-start.63 = (bf16[128,2048]{1,0:T(8,128)(2,1)}, bf16[128,2048]{1,0:T(8,128)(2,1)}, u32[]{:S(2)}, u32[]{:S(2)}) collective-permute-start(bf16[128,2048]{1,0:T(8,128)(2,1)} %pad_maximum_fusion.11), channel_id=1, source_target_pairs={{0,2},{1,3},{2,4},{3,5},{4,6},{5,7},{6,0},{7,1},{8,10},{9,11},{10,... | collective-permute-start | bytes 1572872 | tf_op jit(solution)/shard_map/ppermute | solution.py:44
  (87 other events, 544.7 us)
Sparse Core Ops, SparseCore 0:
  12.4 51.9 all-gather.6
  67.2 159.6 all-gather.8
  289.8 160.0 reduce-scatter.1
  466.4 28.2 all-gather.10
  519.7 21.4 all-gather.12

commit v2 on v1

--- a/solution.py
+++ b/solution.py
@@ -110,8 +110,7 @@
     return scatter_end(own, move_z(to_above, 1), move_z(to_below, -1))
 
 
-def exchange(mine, other):
-    got = swap_core(other)
+def exchange(mine, got):
     chip = jnp.stack([mine[1:], got[1:]], axis=1)
     return mine[0], got[0], *[move_z(chip[step - 1], step) for step in (1, 2, 3)]
 
@@ -391,29 +390,51 @@
     )(core, grads)
 
 
-def qkv_weights_kernel(place_ref, normed_ref, query_ref, mine_ref, got_ref, *refs):
-    parts, (out_ref, grad_ref) = refs[:5], refs[5:]
-    grad_ref[:, 0 : 2 * HD] = query_ref[...]
-    grad_ref[:, 2 * HD : 3 * HD] = (mine_ref[...] + got_ref[...].astype(wide)).astype(low)
+def gather_rows_kernel(place_ref, *refs):
+    parts, out_ref = refs[:5], refs[5]
     for index in range(EXPERTS):
         step, side = index // 2, index % 2
         rows = pl.ds(pl.multiple_of(place_ref[index] * 256, 256), 256)
-        out_ref[rows, 3 * HD : 3 * HD + 256] = parts[step + 1][side] if step else parts[side][...]
+        out_ref[rows, :] = parts[step + 1][side] if step else parts[side][...]
+
+
+def gather_out(places, parts):
+    return pl.pallas_call(
+        gather_rows_kernel,
+        out_shape=jax.ShapeDtypeStruct((D, 256), low),
+        in_specs=[smem] + [vmem] * 5,
+        out_specs=vmem,
+        compiler_params=params(32),
+        cost_estimate=cost(0, 2e6),
+        name="gather_out",
+    )(places, *parts)
+
+
+def qkv_weights_kernel(normed_hbm, query_ref, mine_ref, got_ref, out_ref, grad_ref, normed_ref, sems):
+    copies = []
+    for index in range(D // ROWS):
+        columns = pl.ds(index * ROWS, ROWS)
+        copies.append(pltpu.make_async_copy(normed_hbm.at[:, columns], normed_ref.at[:, columns], sems.at[index]))
+        copies[index].start()
+    grad_ref[:, 0 : 2 * HD] = query_ref[...]
+    grad_ref[:, 2 * HD : 3 * HD] = (mine_ref[...] + got_ref[...].astype(wide)).astype(low)
     for index in range(D // ROWS):
         rows = pl.ds(index * ROWS, ROWS)
-        out_ref[rows, 0 : 3 * HD] = t_mm(normed_ref[:, rows], grad_ref[...]).astype(low)
-
-
-def qkv_weights(places, normed, query, mine, got, parts):
+        copies[index].wait()
+        out_ref[rows, :] = t_mm(normed_ref[:, rows], grad_ref[...]).astype(low)
+
+
+def qkv_weights(normed, query, mine, got):
     return pl.pallas_call(
         qkv_weights_kernel,
-        out_shape=(jax.ShapeDtypeStruct((D, 3 * HD + 256), low), jax.ShapeDtypeStruct((ALL, 3 * HD), low)),
-        in_specs=[smem] + [vmem] * 9,
+        out_shape=(jax.ShapeDtypeStruct((D, 3 * HD), low), jax.ShapeDtypeStruct((ALL, 3 * HD), low)),
+        in_specs=[anywhere] + [vmem] * 3,
         out_specs=(vmem, vmem),
-        compiler_params=params(40),
-        cost_estimate=cost(1.6e9, 10e6),
+        scratch_shapes=[pltpu.VMEM((ALL, D), low), pltpu.SemaphoreType.DMA((D // ROWS,))],
+        compiler_params=params(60),
+        cost_estimate=cost(1.6e9, 8e6),
         name="qkv_weights",
-    )(places, normed, query, mine, got, *parts)
+    )(normed, query, mine, got)
 
 
 def finish_kernel(shards_ref, query_ref, key_ref, value_ref, out_ref, gain_ref):
@@ -955,7 +976,7 @@
     out_blocks = [lax.dynamic_index_in_dim(out_columns, owners[block], 0) for block in range(EXPERTS)]
     out_mine, out_other = jnp.concatenate(out_blocks[:4]), jnp.concatenate(out_blocks[4:])
     out_mine, out_other, _ = together(out_mine, out_other, sent)
-    w_out_own = out_rows(source_owners(expert), exchange(out_mine, out_other))
+    w_out_own = out_rows(source_owners(expert), exchange(out_mine, swap_core(out_other)))
     router = attn_all[:, 768:896]
     is_first = core == 0
     kv_weight = attn_all[:, 256:512].reshape(D, 2, 2, HD // 2)
@@ -1002,21 +1023,21 @@
 
     sent_back, out_mine, out_other = mix_back(owners, back_pieces, w_out_own, mixed, small)
     grad_head = lax.all_to_all(sent_back, "fsdp", split_axis=0, concat_axis=0, tiled=True)
+    result_other, out_other, _ = together(result_other, out_other, sent_back)
+    result_got, out_got = swap_core(result_other), swap_core(out_other)
+    grad_head, result_got, out_got = together(grad_head, result_got, out_got)
     grads_head, small_sums = attend_back(qkv, grad_head, log_total, seg_row, seg_blocks, cos_all, sin_back)
     grads_qkv = lax.all_to_all(grads_head, "fsdp", split_axis=0, concat_axis=0, tiled=True)
-    result_other, result_mine, _ = together(result_other, result_mine, sent_back)
-    result_got = swap_core(result_other)
-    result_got, out_mine, out_other = together(result_got, out_mine, out_other)
-    out_parts = exchange(out_mine, out_other)
+    out_grads = gather_out(source_owners(expert), exchange(out_mine, out_got))
     result_own, to_above, to_below = scatter_start(result_mine, result_got)
     result_own = scatter_end(result_own, move_z(to_above, 1), move_z(to_below, -1))
     layer_out = (middle + result_own).astype(low)
-    grads_qkv, layer_out, *out_parts = together(grads_qkv, layer_out, *out_parts)
+    grads_qkv, layer_out, out_grads = together(grads_qkv, layer_out, out_grads)
+    out_parts = lax.all_to_all(out_grads, "fsdp", split_axis=0, concat_axis=0, tiled=True)
 
     grad_query, kv_mine, kv_other = collect(core[None], grads_qkv)
-    attn_grads, grad_qkv = qkv_weights(
-        source_owners(expert), normed_one, grad_query, kv_mine, swap_core(kv_other), out_parts
-    )
+    attn_grads, grad_qkv = qkv_weights(normed_one, grad_query, kv_mine, swap_core(kv_other))
+    attn_grads, out_parts = together(attn_grads, out_parts)
     attn_parts = lax.all_to_all(attn_grads, "fsdp", split_axis=0, concat_axis=0, tiled=True)
 
     grad_normed_other = mm_t(grad_qkv[half:], qkv_weight).astype(low)
@@ -1028,13 +1049,14 @@
     ffn_sums, _ = together(ffn_sums, attn_grads)
     shared_shards = lax.all_gather(ffn_sums[:, :base], "expert", axis=0)
     attn_parts, shared_shards = together(attn_parts, shared_shards)
-    attn_sums = jnp.sum(attn_parts.reshape(FSDP, TOK, 3 * HD + 256).astype(wide), axis=0)
+    attn_sums = jnp.sum(attn_parts.reshape(FSDP, TOK, 3 * HD).astype(wide), axis=0)
+    out_sums = jnp.sum(out_parts.reshape(FSDP, TOK, 256).astype(wide), axis=0)
 
     own_weight = lax.dynamic_slice_in_dim(qkv_weight, place * TOK, TOK, 0)
-    gain_part = jnp.sum(attn_sums[:, : 3 * HD] * own_weight.astype(wide), axis=1, keepdims=True)
+    gain_part = jnp.sum(attn_sums * own_weight.astype(wide), axis=1, keepdims=True)
     gain_upper, gain_lower = halves(gain_part / attn_gain.astype(wide)[:, None])
     small = [gain_upper, gain_lower, small_sums.T.astype(low), jnp.zeros((TOK, 110), low)]
-    shards = jnp.concatenate([attn_sums.astype(low), *small], axis=1)
+    shards = jnp.concatenate([attn_sums.astype(low), out_sums.astype(low), *small], axis=1)
 
     attn_shards = lax.all_gather(shards, "expert", axis=0)
     grad_shared_gate, grad_shared_up, grad_shared_down = finish_dense(shared_shards, spread, spread_rows)

time: 566 us -> 563 us (level)
  blocking collectives: 50.1 us -> 25.3 us
  starting transfers between devices: 80.3 us -> 87.6 us
  waiting for transfers between devices: 174 us -> 181 us
    all_to_all x1 -> x0, blocking collectives: 24.9 us -> none  [per_device(): lax.all_to_all(sent_back, 'fsdp', split_axis=0, concat_axis=0, tiled=True)]
    all_to_all x0 -> x2, waiting for transfers between devices: none -> 24.8 us  [the longest x1 17.3 us: per_device(): lax.all_to_all(sent_back, 'fsdp', split_axis=0, concat_axis=0, tiled=True)]
    all_to_all x1, waiting for transfers between devices: 17.5 us -> 3.34 us  [per_device(): lax.all_to_all(attn_grads, 'fsdp', split_axis=0, concat_axis=0, tiled=True)]
    all_to_all x0 -> x2, starting transfers between devices: none -> 8.91 us  [the longest x1 5.08 us: per_device(): lax.all_to_all(sent_back, 'fsdp', split_axis=0, concat_axis=0, tiled=True)]
    unnamed x129 -> x143, local copies, waits for them, and re-layouts: 29.6 us -> 25.4 us
  transfers between devices with their start and end apart: 73 -> 75, of which waited for: 32 -> 31; matrix products, arithmetic and copies ran while one was open for 16% -> 19% of each run, Pallas kernels for 9% -> 9%
where the time goes in v2:
time: 563 us; the launch traced here: 552 us
  waiting for transfers between devices  181 us (32%)
  Pallas kernels  114 us (20%)
  starting transfers between devices  87.6 us (16%)
  local copies, waits for them, and re-layouts  62.4 us (11%)
  other arithmetic  48.6 us (9%)
  blocking collectives  25.3 us (4%)
  matrix products  17.4 us (3%)
  between operations  15.8 us (3%)
    ppermute x38, waiting for transfers between devices, move_z(): return lax.ppermute(block, 'expert', shift_pairs(step))  130 us
    pallas_call x1, Pallas kernels, ffn(): pl.pallas_call(ffn_kernel, out_shape=tuple([jax.ShapeDtypeStruct(shape, l...  62.7 us
    ppermute x38, starting transfers between devices, move_z(): return lax.ppermute(block, 'expert', shift_pairs(step))  61.2 us
    unnamed x143, local copies, waits for them, and re-layouts  25.4 us
    all_to_all x1, blocking collectives, per_device(): lax.all_to_all(mixed_head, 'fsdp', split_axis=0, concat_axis=0, tiled=True)  25.3 us
    dot_general x10, matrix products, product(): lax.dot_general(left, right, (contract, ((), ())), preferred_element_type...  17.4 us
    all_to_all x1, waiting for transfers between devices, per_device(): lax.all_to_all(sent_back, 'fsdp', split_axis=0, concat_axis=0, tiled=True)  17.3 us
  transfers between devices with their start and end apart: 75, of which 31 were waited for; matrix products, arithmetic and copies ran while one was open for 19% of the time, Pallas kernels for 9%

profile of v2, /device:TPU:0, one launch (start us, length us, event | category | flops | bytes accessed | tf_op | source)
XLA Modules:
  0.0 552.1 jit_solution(17779867557097982903)
XLA Ops:
  16.3 4.2 collective-permute-start
  20.5 12.6 %collective-permute-done.refs_1_ = bf16[144,2048]{1,0:T(8,128)(2,1)S(1)} collective-permute-done((bf16[144,2048]{1,0:T(8,128)(2,1)S(1)}, bf16[144,2048]{1,0:T(8,128)(2,1)S(1)}, u32[]{:S(2)}, u32[]{:S(2)}) %collective-permute-start) | collective-permute-done | bytes 589856 | tf_op jit(solution)/shard_map/ppermute | solution.py:44
  33.1 3.8 collective-permute-start.3
  37.7 7.4 %collective-permute-done.2.refs_2_ = bf16[64,2048]{1,0:T(8,128)(2,1)} collective-permute-done((bf16[64,2048]{1,0:T(8,128)(2,1)S(1)}, bf16[64,2048]{1,0:T(8,128)(2,1)}, u32[]{:S(2)}, u32[]{:S(2)}) %collective-permute-start.2) | collective-permute-done | bytes 262176 | tf_op jit(solution)/shard_map/ppermute | solution.py:44
  45.7 5.7 %multiply_sine_fusion = (f32[2048,64]{1,0:T(8,128)}, f32[2048,64]{1,0:T(8,128)}, f32[2048,64]{1,0:T(8,128)}) fusion(f32[64]{0:T(128)S(1)} %multiply_power_fusion, f32[2048]{0:T(1024)S(1)} %iota_convert_fusion), kind=kLoop, calls=%fused_computation.24 | loop fusion | flops 262144 | bytes 1581312 | tf_op jit(solution)/shard_map/sin | solution.py:942
  52.6 3.2 collective-permute-start.10
  56.1 4.3 pad_maximum_fusion.1
  60.4 4.1 all-gather.7.cloned.1.call-done.refs_10_
  67.5 8.6 %project.1 = (bf16[1024,2048]{1,0:T(8,128)(2,1)}, bf16[2048,384]{1,0:T(8,128)(2,1)S(1)}, f32[1024,1]{1,0:T(8,128)S(1)}, f32[16,2048]{1,0:T(8,128)S(1)}, bf16[128,2048]{1,0:T(8,128)(2,1)S(1)}) custom-call(bf16[144,2048]{1,0:T(8,128)(2,1)S(1)} %fusion.31.refs_0_, bf16[144,2048]{1,0:T(8,128)(2,1)S(1)} %collective-permute-done.refs_1_, ...), custom_call_target="tpu_custom_call" | custom-call | flops 2200000000 | bytes 16000000 | tf_op jit(solution)/shard_map/project/pallas_call | solution.py:305
  78.8 4.8 all-to-all-start
  113.5 3.2 collective-permute-done.12.refs_2_
  116.7 4.6 collective-permute-done.13.refs_3_
  130.9 6.6 %attend.1 = (bf16[2048,128]{1,0:T(8,128)(2,1)S(1)}, f32[2048,1]{1,0:T(8,128)S(1)}) custom-call(bf16[2048,384]{1,0:T(8,128)(2,1)S(1)} %bitcast.235, f32[1,2048]{1,0:T(1,128)S(1)} %fusion.117.seg_row_ref, f32[128,128]{1,0:T(8,128)S(1)} %copy-done.19), custom_call_target="tpu_custom_call" | custom-call | flops 1073741824 | bytes 2097152 | tf_op jit(solution)/shard_map/attend/pallas_call | solution.py:226
  137.4 25.3 %all_to_all.69 = bf16[16,128,128]{2,1,0:T(8,128)(2,1)S(1)} all-to-all(bf16[16,128,128]{2,1,0:T(8,128)(2,1)S(1)} %bitcast.241), channel_id=1, replica_groups=mesh['fsdp'=16,'expert'=8] {'fsdp'}, dimensions={0} | all-to-all | bytes 1048576 | tf_op jit(solution)/shard_map/all_to_all | solution.py:991
  172.7 6.3 %collective-permute-done.23 = bf16[64,2048]{1,0:T(8,128)(2,1)S(1)} collective-permute-done((bf16[64,2048]{1,0:T(8,128)(2,1)S(1)}, bf16[64,2048]{1,0:T(8,128)(2,1)S(1)}, u32[]{:S(2)}, u32[]{:S(2)}) %collective-permute-start.23) | collective-permute-done | bytes 262176 | tf_op jit(solution)/shard_map/ppermute | solution.py:44
  182.3 10.3 %collective-permute-done.26 = bf16[128,2048]{1,0:T(8,128)(2,1)S(1)} collective-permute-done((bf16[128,2048]{1,0:T(8,128)(2,1)S(1)}, bf16[128,2048]{1,0:T(8,128)(2,1)S(1)}, u32[]{:S(2)}, u32[]{:S(2)}) %collective-permute-start.26) | collective-permute-done | bytes 524320 | tf_op jit(solution)/shard_map/ppermute | solution.py:44
  192.6 3.5 collective-permute-done.24
  196.8 3.2 collective-permute-start.27
  200.1 9.8 %collective-permute-done.28.refs_9_ = bf16[128,2048]{1,0:T(8,128)(2,1)S(1)} collective-permute-done((bf16[128,2048]{1,0:T(8,128)(2,1)S(1)}, bf16[128,2048]{1,0:T(8,128)(2,1)S(1)}, u32[]{:S(2)}, u32[]{:S(2)}) %collective-permute-start.28) | collective-permute-done | bytes 524320 | tf_op jit(solution)/shard_map/ppermute | solution.py:44
  213.5 4.0 collective-permute-done.29.refs_7_
  221.6 5.2 all-gather.9.cloned.1.call-done.refs_25_
  226.9 62.7 %ffn.1 = (bf16[512,2176]{1,0:T(8,128)(2,1)}, bf16[512,2176]{1,0:T(8,128)(2,1)}, f32[128,128]{1,0:T(8,128)}, bf16[2048,5376]{1,0:T(8,128)(2,1)}, bf16[1024,384]{1...) custom-call(s32[1]{0:T(128)} %bitcast.35.refs_0_, bf16[336,1024]{1,0:T(8,128)(2,1)} %fusion.13.refs_1_, ...), custom_call_target="tpu_custom_call" | custom-call | flops 38000001024 | bytes 70000000 | tf_op jit(solution)/shard_map/ffn/pallas_call | solution.py:727
  289.8 4.5 collective-permute-done.36
  299.7 6.2 %collective-permute-done.39 = bf16[64,2176]{1,0:T(8,128)(2,1)S(1)} collective-permute-done((bf16[64,2176]{1,0:T(8,128)(2,1)S(1)}, bf16[64,2176]{1,0:T(8,128)(2,1)S(1)}, u32[]{:S(2)}, u32[]{:S(2)}) %collective-permute-start.39) | collective-permute-done | bytes 278560 | tf_op jit(solution)/shard_map/ppermute | solution.py:44
  305.9 3.4 collective-permute-done.37
  309.6 3.3 collective-permute-start.40
  313.0 11.4 %collective-permute-done.38.first_ref = bf16[128,2176]{1,0:T(8,128)(2,1)S(1)} collective-permute-done((bf16[128,2176]{1,0:T(8,128)(2,1)S(1)}, bf16[128,2176]{1,0:T(8,128)(2,1)S(1)}, u32[]{:S(2)}, u32[]{:S(2)}) %collective-permute-start.38) | collective-permute-done | bytes 557088 | tf_op jit(solution)/shard_map/ppermute | solution.py:44
  327.2 3.2 collective-permute-start.42
  346.3 4.0 collective-permute-done.43.refs_2_
  355.4 7.0 %mix_back.1 = (bf16[2304,128]{1,0:T(8,128)(2,1)}, bf16[4,256,256]{2,1,0:T(8,128)(2,1)}, bf16[4,256,256]{2,1,0:T(8,128)(2,1)}) custom-call(s32[8]{0:T(128)} %stack.95.place_ref, bf16[128,2048]{1,0:T(8,128)(2,1)} %copy-done.24, bf16[128,2048]{1,0:T(8,128)(2,1)} %collective-permute-done.42.refs_1_, bf16[64,2048]{1,0:T(8,128)(2,1)} %collective-permute-done.43.refs_2_, ...), custom_call_target="tpu_custom_call" | custom-call | flops 2200000000 | bytes 10000000 | tf_op jit(solution)/shard_map/mix_back/pallas_call | solution.py:347
  363.0 5.1 all-to-all-start.2
  370.3 17.3 %all-to-all-done.2 = bf16[16,144,128]{2,1,0:T(8,128)(2,1)S(1)} async-done(((bf16[16,144,128]{2,1,0:T(8,128)(2,1)}), bf16[16,144,128]{2,1,0:T(8,128)(2,1)S(1)}, u32[]{:S(2)}, u32[]{:S(2)}) %all-to-all-start.2) | async-done | bytes 589856 | tf_op jit(solution)/shard_map/all_to_all | solution.py:1025
  398.0 10.5 %attend_back.1 = (bf16[2048,384]{1,0:T(8,128)(2,1)S(1)}, f32[16,128]{1,0:T(8,128)S(1)}) custom-call(bf16[2048,384]{1,0:T(8,128)(2,1)} %bitcast.236, bf16[2304,128]{1,0:T(8,128)(2,1)S(1)} %bitcast.240, f32[2048,1]{1,0:T(8,128)S(1)} %copy-done.28, f32[1,2048]{1,0:T(1,128)S(1)} %fusion.117.seg_row_ref, f32[128,128]{1,0:T(8,128)S(1)} %copy-done.20, ...), custom_call_target="tpu_custom_call" | custom-call | flops 2684354560 | bytes 4194304 | tf_op jit(solution)/shard_map/attend_back/pallas_call | solution.py:243
  409.7 3.7 all-to-all-start.3
  418.7 4.5 collective-permute-start.57
  425.0 17.3 %collective-permute-done.56.refs_2_ = bf16[2,256,256]{2,1,0:T(8,128)(2,1)S(1)} collective-permute-done((bf16[2,256,256]{2,1,0:T(8,128)(2,1)S(1)}, bf16[2,256,256]{2,1,0:T(8,128)(2,1)S(1)}, u32[]{:S(2)}, u32[]{:S(2)}) %collective-permute-start.56) | collective-permute-done | bytes 262176 | tf_op jit(solution)/shard_map/ppermute | solution.py:44
  446.1 4.4 all-to-all-done.3
  452.3 3.8 all-to-all-start.4
  456.9 7.5 %qkv_weights.1 = (bf16[2048,384]{1,0:T(8,128)(2,1)}, bf16[1024,384]{1,0:T(8,128)(2,1)}) custom-call(bf16[1024,2048]{1,0:T(8,128)(2,1)} %get-tuple-element.192.normed_hbm, bf16[1024,256]{1,0:T(8,128)(2,1)} %copy-done.25, f32[1024,128]{1,0:T(8,128)} %copy-done.26, bf16[1024,128]{1,0:T(8,128)(2,1)} %copy-done.65), custom_call_target="tpu_custom_call" | custom-call | flops 1600000000 | bytes 8000000 | tf_op jit(solution)/shard_map/qkv_weights/pallas_call | solution.py:428
  464.4 3.7 convolution_convert_fusion.2
  468.5 7.5 %all-to-all-done.4 = bf16[16,128,256]{2,1,0:T(8,128)(2,1)S(1)} async-done(((bf16[16,128,256]{2,1,0:T(8,128)(2,1)}), bf16[16,128,256]{2,1,0:T(8,128)(2,1)S(1)}, u32[]{:S(2)}, u32[]{:S(2)}) %all-to-all-start.4) | async-done | bytes 1048608 | tf_op jit(solution)/shard_map/all_to_all | solution.py:1036
  477.8 3.6 convolution_convert_fusion.3
  481.4 4.4 all-to-all-start.5
  494.4 8.5 %collective-permute-done.62 = bf16[64,2048]{1,0:T(8,128)(2,1)} collective-permute-done((bf16[64,2048]{1,0:T(8,128)(2,1)}, bf16[64,2048]{1,0:T(8,128)(2,1)}, u32[]{:S(2)}, u32[]{:S(2)}) %collective-permute-start.62) | collective-permute-done | bytes 262176 | tf_op jit(solution)/shard_map/ppermute | solution.py:44
  507.2 3.3 all-to-all-done.5
  518.8 4.2 collective-permute-done.64
  523.1 3.4 collective-permute-done.63
  536.2 4.6 finish_dense.1
  (402 shorter events, 172.6 us)
Async XLA Ops:
  7.2 57.3 %all-gather.7.cloned.1.call-start = ((), (), s32[]{:S(2)}) async-start(), calls=%async_computation.7 | async-start | bytes 3899392 | tf_op jit(solution)/shard_map/all_gather | solution.py:896
  12.3 214.6 %all-gather.9.cloned.1.call-start = ((), (), s32[]{:S(2)}) async-start(), calls=%async_computation.8 | async-start | bytes 23396352 | tf_op jit(solution)/shard_map/all_gather | solution.py:926
  16.3 16.8 %collective-permute-start = (bf16[144,2048]{1,0:T(8,128)(2,1)S(1)}, bf16[144,2048]{1,0:T(8,128)(2,1)S(1)}, u32[]{:S(2)}, u32[]{:S(2)}) collective-permute-start(bf16[144,2048]{1,0:T(8,128)(2,1)S(1)} %fusion.31.refs_0_), channel_id=1, source_target_pairs={{0,6},{1,7},{2,0},{3,1},{4,2},{5,3},{6,4},{7,5},{8,14},{9,15},{10,... | collective-permute-start | bytes 1769480 | tf_op jit(solution)/shard_map/ppermute | solution.py:44
  20.5 16.4 %collective-permute-start.1 = (bf16[144,2048]{1,0:T(8,128)(2,1)S(1)}, bf16[144,2048]{1,0:T(8,128)(2,1)S(1)}, u32[]{:S(2)}, u32[]{:S(2)}) collective-permute-start(bf16[144,2048]{1,0:T(8,128)(2,1)S(1)} %fusion.31.refs_0_), channel_id=1, source_target_pairs={{0,2},{1,3},{2,4},{3,5},{4,6},{5,7},{6,0},{7,1},{8,10},{9,11},{10,... | collective-permute-start | bytes 1769480 | tf_op jit(solution)/shard_map/ppermute | solution.py:44
  33.1 12.1 %collective-permute-start.3 = (bf16[80,2048]{1,0:T(8,128)(2,1)S(1)}, bf16[80,2048]{1,0:T(8,128)(2,1)S(1)}, u32[]{:S(2)}, u32[]{:S(2)}) collective-permute-start(bf16[80,2048]{1,0:T(8,128)(2,1)S(1)} %slice.388), channel_id=1, source_target_pairs={{0,6},{1,7},{2,0},{3,1},{4,2},{5,3},{6,4},{7,5},{8,14},{9,15},{10,... | collective-permute-start | bytes 983048 | tf_op jit(solution)/shard_map/ppermute | solution.py:44
  37.0 15.5 %collective-permute-start.4 = (bf16[144,2048]{1,0:T(8,128)(2,1)S(1)}, bf16[144,2048]{1,0:T(8,128)(2,1)S(1)}, u32[]{:S(2)}, u32[]{:S(2)}) collective-permute-start(bf16[144,2048]{1,0:T(8,128)(2,1)S(1)} %fusion.31.refs_0_), channel_id=1, source_target_pairs={{0,1},{1,0},{2,3},{3,2},{4,5},{5,4},{6,7},{7,6},{8,9},{9,8},{10,11... | collective-permute-start | bytes 1769480 | tf_op jit(solution)/shard_map/ppermute | solution.py:48
  37.1 15.4 %collective-permute-start.5 = (bf16[144,2048]{1,0:T(8,128)(2,1)S(1)}, bf16[144,2048]{1,0:T(8,128)(2,1)S(1)}, u32[]{:S(2)}, u32[]{:S(2)}) collective-permute-start(bf16[144,2048]{1,0:T(8,128)(2,1)S(1)} %collective-permute-done.refs_1_), channel_id=1, source_target_pairs={{0,1},{1,0},{2,3},{3,2},{4,5},{5,4},{6,7},{7,6},{8,9},{9,8},{10,11... | collective-permute-start | bytes 1769480 | tf_op jit(solution)/shard_map/ppermute | solution.py:48
  37.6 14.8 %collective-permute-start.8 = (bf16[144,2048]{1,0:T(8,128)(2,1)S(1)}, bf16[144,2048]{1,0:T(8,128)(2,1)}, u32[]{:S(2)}, u32[]{:S(2)}) collective-permute-start(bf16[144,2048]{1,0:T(8,128)(2,1)S(1)} %collective-permute-done.1.refs_4_), channel_id=1, source_target_pairs={{0,1},{1,0},{2,3},{3,2},{4,5},{5,4},{6,7},{7,6},{8,9},{9,8},{10,11... | collective-permute-start | bytes 1769480 | tf_op jit(solution)/shard_map/ppermute | solution.py:48
  52.5 26.3 %collective-permute-start.9 = (bf16[128,2048]{1,0:T(8,128)(2,1)}, bf16[128,2048]{1,0:T(8,128)(2,1)}, u32[]{:S(2)}, u32[]{:S(2)}) collective-permute-start(bf16[128,2048]{1,0:T(8,128)(2,1)} %bitcast.refs_15_.cot_ref), channel_id=1, source_target_pairs={{0,2},{1,3},{2,4},{3,5},{4,6},{5,7},{6,0},{7,1},{8,10},{9,11},{10,... | collective-permute-start | bytes 1572872 | tf_op jit(solution)/shard_map/ppermute | solution.py:44
  52.6 26.3 %collective-permute-start.10 = (bf16[128,2048]{1,0:T(8,128)(2,1)}, bf16[128,2048]{1,0:T(8,128)(2,1)}, u32[]{:S(2)}, u32[]{:S(2)}) collective-permute-start(bf16[128,2048]{1,0:T(8,128)(2,1)} %bitcast.refs_15_.cot_ref), channel_id=1, source_target_pairs={{0,6},{1,7},{2,0},{3,1},{4,2},{5,3},{6,4},{7,5},{8,14},{9,15},{10,... | collective-permute-start | bytes 1572872 | tf_op jit(solution)/shard_map/ppermute | solution.py:44
  78.8 51.1 %all-to-all-start = ((bf16[16,128,384]{2,1,0:T(8,128)(2,1)}), bf16[16,128,384]{2,1,0:T(8,128)(2,1)S(1)}, u32[]{:S(2)}, u32[]{:S(2)}) async-start(bf16[16,128,384]{2,1,0:T(8,128)(2,1)} %bitcast.237), calls=%async_computation | async-start | bytes 3145728 | tf_op jit(solution)/shard_map/all_to_all | solution.py:962
  83.6 392.5 %reduce-scatter.2.cloned.1.call-start = ((), (), s32[]{:S(2)}) async-start(), calls=%async_computation.9 | async-start | bytes 23396352 | tf_op jit(solution)/shard_map/reduce_scatter | solution.py:1010
  89.7 15.4 %collective-permute-start.11 = (bf16[4,256,256]{2,1,0:T(8,128)(2,1)}, bf16[4,256,256]{2,1,0:T(8,128)(2,1)}, u32[]{:S(2)}, u32[]{:S(2)}) collective-permute-start(bf16[4,256,256]{2,1,0:T(8,128)(2,1)} %pad_maximum_fusion.6), channel_id=1, source_target_pairs={{0,1},{1,0},{2,3},{3,2},{4,5},{5,4},{6,7},{7,6},{8,9},{9,8},{10,11... | collective-permute-start | bytes 1572872 | tf_op jit(solution)/shard_map/ppermute | solution.py:48
  98.2 14.7 %collective-permute-start.15 = (bf16[64,2048]{1,0:T(8,128)(2,1)S(1)}, bf16[64,2048]{1,0:T(8,128)(2,1)}, u32[]{:S(2)}, u32[]{:S(2)}) collective-permute-start(bf16[64,2048]{1,0:T(8,128)(2,1)S(1)} %slice.315), channel_id=1, source_target_pairs={{0,2},{1,3},{2,4},{3,5},{4,6},{5,7},{6,0},{7,1},{8,10},{9,11},{10,... | collective-permute-start | bytes 786440 | tf_op jit(solution)/shard_map/ppermute | solution.py:44
  100.8 12.2 %collective-permute-start.16 = (bf16[64,2048]{1,0:T(8,128)(2,1)S(1)}, bf16[64,2048]{1,0:T(8,128)(2,1)}, u32[]{:S(2)}, u32[]{:S(2)}) collective-permute-start(bf16[64,2048]{1,0:T(8,128)(2,1)S(1)} %slice.316), channel_id=1, source_target_pairs={{0,6},{1,7},{2,0},{3,1},{4,2},{5,3},{6,4},{7,5},{8,14},{9,15},{10,... | collective-permute-start | bytes 786440 | tf_op jit(solution)/shard_map/ppermute | solution.py:44
  108.6 12.7 %collective-permute-start.13 = (bf16[2,256,256]{2,1,0:T(8,128)(2,1)S(1)}, bf16[2,256,256]{2,1,0:T(8,128)(2,1)S(1)}, u32[]{:S(2)}, u32[]{:S(2)}) collective-permute-start(bf16[2,256,256]{2,1,0:T(8,128)(2,1)S(1)} %get-tuple-element.330), channel_id=1, source_target_pairs={{0,4},{1,5},{2,6},{3,7},{4,0},{5,1},{6,2},{7,3},{8,12},{9,13},{10,... | collective-permute-start | bytes 786440 | tf_op jit(solution)/shard_map/ppermute | solution.py:44
  111.5 12.4 %collective-permute-start.14 = (bf16[2,256,256]{2,1,0:T(8,128)(2,1)S(1)}, bf16[2,256,256]{2,1,0:T(8,128)(2,1)S(1)}, u32[]{:S(2)}, u32[]{:S(2)}) collective-permute-start(bf16[2,256,256]{2,1,0:T(8,128)(2,1)S(1)} %get-tuple-element.328), channel_id=1, source_target_pairs={{0,6},{1,7},{2,0},{3,1},{4,2},{5,3},{6,4},{7,5},{8,14},{9,15},{10,... | collective-permute-start | bytes 786440 | tf_op jit(solution)/shard_map/ppermute | solution.py:44
  112.9 17.0 %collective-permute-start.18 = (bf16[128,2048]{1,0:T(8,128)(2,1)}, bf16[128,2048]{1,0:T(8,128)(2,1)}, u32[]{:S(2)}, u32[]{:S(2)}) collective-permute-start(bf16[128,2048]{1,0:T(8,128)(2,1)} %collective-permute-done.10.refs_16_), channel_id=1, source_target_pairs={{0,1},{1,0},{2,3},{3,2},{4,5},{5,4},{6,7},{7,6},{8,9},{9,8},{10,11... | collective-permute-start | bytes 1572872 | tf_op jit(solution)/shard_map/ppermute | solution.py:48
  113.0 16.9 %collective-permute-start.21 = (bf16[128,2048]{1,0:T(8,128)(2,1)}, bf16[128,2048]{1,0:T(8,128)(2,1)}, u32[]{:S(2)}, u32[]{:S(2)}) collective-permute-start(bf16[128,2048]{1,0:T(8,128)(2,1)} %collective-permute-done.9.refs_19_), channel_id=1, source_target_pairs={{0,1},{1,0},{2,3},{3,2},{4,5},{5,4},{6,7},{7,6},{8,9},{9,8},{10,11... | collective-permute-start | bytes 1572872 | tf_op jit(solution)/shard_map/ppermute | solution.py:48
  116.7 13.1 %collective-permute-start.17 = (bf16[128,2048]{1,0:T(8,128)(2,1)}, bf16[128,2048]{1,0:T(8,128)(2,1)}, u32[]{:S(2)}, u32[]{:S(2)}) collective-permute-start(bf16[128,2048]{1,0:T(8,128)(2,1)} %bitcast.refs_15_.cot_ref), channel_id=1, source_target_pairs={{0,1},{1,0},{2,3},{3,2},{4,5},{5,4},{6,7},{7,6},{8,9},{9,8},{10,11... | collective-permute-start | bytes 1572872 | tf_op jit(solution)/shard_map/ppermute | solution.py:48
  179.2 13.5 %collective-permute-start.26 = (bf16[128,2048]{1,0:T(8,128)(2,1)S(1)}, bf16[128,2048]{1,0:T(8,128)(2,1)S(1)}, u32[]{:S(2)}, u32[]{:S(2)}) collective-permute-start(bf16[128,2048]{1,0:T(8,128)(2,1)S(1)} %pad_maximum_fusion.8), channel_id=1, source_target_pairs={{0,6},{1,7},{2,0},{3,1},{4,2},{5,3},{6,4},{7,5},{8,14},{9,15},{10,... | collective-permute-start | bytes 1572872 | tf_op jit(solution)/shard_map/ppermute | solution.py:44
  182.2 13.9 %collective-permute-start.24 = (bf16[128,2048]{1,0:T(8,128)(2,1)S(1)}, bf16[128,2048]{1,0:T(8,128)(2,1)S(1)}, u32[]{:S(2)}, u32[]{:S(2)}) collective-permute-start(bf16[128,2048]{1,0:T(8,128)(2,1)S(1)} %pad_maximum_fusion.7), channel_id=1, source_target_pairs={{0,2},{1,3},{2,4},{3,5},{4,6},{5,7},{6,0},{7,1},{8,10},{9,11},{10,... | collective-permute-start | bytes 1572872 | tf_op jit(solution)/shard_map/ppermute | solution.py:44
  196.8 13.1 %collective-permute-start.28 = (bf16[128,2048]{1,0:T(8,128)(2,1)S(1)}, bf16[128,2048]{1,0:T(8,128)(2,1)S(1)}, u32[]{:S(2)}, u32[]{:S(2)}) collective-permute-start(bf16[128,2048]{1,0:T(8,128)(2,1)S(1)} %multiply_convert_fusion.refs_5_), channel_id=1, source_target_pairs={{0,2},{1,3},{2,4},{3,5},{4,6},{5,7},{6,0},{7,1},{8,10},{9,11},{10,... | collective-permute-start | bytes 1572872 | tf_op jit(solution)/shard_map/ppermute | solution.py:44
  196.8 13.1 %collective-permute-start.27 = (bf16[128,2048]{1,0:T(8,128)(2,1)S(1)}, bf16[128,2048]{1,0:T(8,128)(2,1)S(1)}, u32[]{:S(2)}, u32[]{:S(2)}) collective-permute-start(bf16[128,2048]{1,0:T(8,128)(2,1)S(1)} %multiply_convert_fusion.refs_5_), channel_id=1, source_target_pairs={{0,6},{1,7},{2,0},{3,1},{4,2},{5,3},{6,4},{7,5},{8,14},{9,15},{10,... | collective-permute-start | bytes 1572872 | tf_op jit(solution)/shard_map/ppermute | solution.py:44
  200.1 19.9 %collective-permute-start.31 = (bf16[128,2048]{1,0:T(8,128)(2,1)S(1)}, bf16[128,2048]{1,0:T(8,128)(2,1)S(1)}, u32[]{:S(2)}, u32[]{:S(2)}) collective-permute-start(bf16[128,2048]{1,0:T(8,128)(2,1)S(1)} %multiply_convert_fusion.refs_5_), channel_id=1, source_target_pairs={{0,1},{1,0},{2,3},{3,2},{4,5},{5,4},{6,7},{7,6},{8,9},{9,8},{10,11... | collective-permute-start | bytes 1572872 | tf_op jit(solution)/shard_map/ppermute | solution.py:48
  309.5 14.9 %collective-permute-start.38 = (bf16[128,2176]{1,0:T(8,128)(2,1)S(1)}, bf16[128,2176]{1,0:T(8,128)(2,1)S(1)}, u32[]{:S(2)}, u32[]{:S(2)}) collective-permute-start(bf16[128,2176]{1,0:T(8,128)(2,1)S(1)} %pad_maximum_fusion.3), channel_id=1, source_target_pairs={{0,2},{1,3},{2,4},{3,5},{4,6},{5,7},{6,0},{7,1},{8,10},{9,11},{10,... | collective-permute-start | bytes 1671176 | tf_op jit(solution)/shard_map/ppermute | solution.py:44
  309.6 14.8 %collective-permute-start.40 = (bf16[128,2176]{1,0:T(8,128)(2,1)S(1)}, bf16[128,2176]{1,0:T(8,128)(2,1)S(1)}, u32[]{:S(2)}, u32[]{:S(2)}) collective-permute-start(bf16[128,2176]{1,0:T(8,128)(2,1)S(1)} %pad_maximum_fusion.4), channel_id=1, source_target_pairs={{0,6},{1,7},{2,0},{3,1},{4,2},{5,3},{6,4},{7,5},{8,14},{9,15},{10,... | collective-permute-start | bytes 1671176 | tf_op jit(solution)/shard_map/ppermute | solution.py:44
  327.1 13.5 %collective-permute-start.41 = (bf16[128,2048]{1,0:T(8,128)(2,1)S(1)}, bf16[128,2048]{1,0:T(8,128)(2,1)}, u32[]{:S(2)}, u32[]{:S(2)}) collective-permute-start(bf16[128,2048]{1,0:T(8,128)(2,1)S(1)} %get-tuple-element.166.refs_0_), channel_id=1, source_target_pairs={{0,2},{1,3},{2,4},{3,5},{4,6},{5,7},{6,0},{7,1},{8,10},{9,11},{10,... | collective-permute-start | bytes 1572872 | tf_op jit(solution)/shard_map/ppermute | solution.py:44
  327.2 13.5 %collective-permute-start.42 = (bf16[128,2048]{1,0:T(8,128)(2,1)S(1)}, bf16[128,2048]{1,0:T(8,128)(2,1)}, u32[]{:S(2)}, u32[]{:S(2)}) collective-permute-start(bf16[128,2048]{1,0:T(8,128)(2,1)S(1)} %get-tuple-element.166.refs_0_), channel_id=1, source_target_pairs={{0,6},{1,7},{2,0},{3,1},{4,2},{5,3},{6,4},{7,5},{8,14},{9,15},{10,... | collective-permute-start | bytes 1572872 | tf_op jit(solution)/shard_map/ppermute | solution.py:44
  330.5 24.1 %collective-permute-start.45 = (bf16[128,2048]{1,0:T(8,128)(2,1)S(1)}, bf16[128,2048]{1,0:T(8,128)(2,1)}, u32[]{:S(2)}, u32[]{:S(2)}) collective-permute-start(bf16[128,2048]{1,0:T(8,128)(2,1)S(1)} %get-tuple-element.166.refs_0_), channel_id=1, source_target_pairs={{0,1},{1,0},{2,3},{3,2},{4,5},{5,4},{6,7},{7,6},{8,9},{9,8},{10,11... | collective-permute-start | bytes 1572872 | tf_op jit(solution)/shard_map/ppermute | solution.py:48
  362.4 25.2 %collective-permute-start.50 = (bf16[512,2048]{1,0:T(8,128)(2,1)}, bf16[512,2048]{1,0:T(8,128)(2,1)}, u32[]{:S(2)}, u32[]{:S(2)}) collective-permute-start(bf16[512,2048]{1,0:T(8,128)(2,1)} %add_convert_fusion.1), channel_id=1, source_target_pairs={{0,1},{1,0},{2,3},{3,2},{4,5},{5,4},{6,7},{7,6},{8,9},{9,8},{10,11... | collective-permute-start | bytes 6291464 | tf_op jit(solution)/shard_map/ppermute | solution.py:48
  363.0 24.6 %all-to-all-start.2 = ((bf16[16,144,128]{2,1,0:T(8,128)(2,1)}), bf16[16,144,128]{2,1,0:T(8,128)(2,1)S(1)}, u32[]{:S(2)}, u32[]{:S(2)}) async-start(bf16[16,144,128]{2,1,0:T(8,128)(2,1)} %bitcast.265), calls=%async_computation.2 | async-start | bytes 1179648 | tf_op jit(solution)/shard_map/all_to_all | solution.py:1025
  394.1 20.5 %collective-permute-start.52 = (bf16[64,2048]{1,0:T(8,128)(2,1)}, bf16[64,2048]{1,0:T(8,128)(2,1)}, u32[]{:S(2)}, u32[]{:S(2)}) collective-permute-start(bf16[64,2048]{1,0:T(8,128)(2,1)} %get-tuple-element.306), channel_id=1, source_target_pairs={{0,2},{1,3},{2,4},{3,5},{4,6},{5,7},{6,0},{7,1},{8,10},{9,11},{10,... | collective-permute-start | bytes 786440 | tf_op jit(solution)/shard_map/ppermute | solution.py:44
  395.8 18.7 %collective-permute-start.54 = (bf16[64,2048]{1,0:T(8,128)(2,1)}, bf16[64,2048]{1,0:T(8,128)(2,1)}, u32[]{:S(2)}, u32[]{:S(2)}) collective-permute-start(bf16[64,2048]{1,0:T(8,128)(2,1)} %get-tuple-element.307), channel_id=1, source_target_pairs={{0,6},{1,7},{2,0},{3,1},{4,2},{5,3},{6,4},{7,5},{8,14},{9,15},{10,... | collective-permute-start | bytes 786440 | tf_op jit(solution)/shard_map/ppermute | solution.py:44
  409.7 40.9 %all-to-all-start.3 = ((bf16[16,128,384]{2,1,0:T(8,128)(2,1)}), bf16[16,128,384]{2,1,0:T(8,128)(2,1)S(1)}, u32[]{:S(2)}, u32[]{:S(2)}) async-start(bf16[16,128,384]{2,1,0:T(8,128)(2,1)} %bitcast.238), calls=%async_computation.3 | async-start | bytes 3145728 | tf_op jit(solution)/shard_map/all_to_all | solution.py:1030
  416.1 27.7 %collective-permute-start.55 = (bf16[128,2048]{1,0:T(8,128)(2,1)S(1)}, bf16[128,2048]{1,0:T(8,128)(2,1)S(1)}, u32[]{:S(2)}, u32[]{:S(2)}) collective-permute-start(bf16[128,2048]{1,0:T(8,128)(2,1)S(1)} %pad_maximum_fusion.10), channel_id=1, source_target_pairs={{0,6},{1,7},{2,0},{3,1},{4,2},{5,3},{6,4},{7,5},{8,14},{9,15},{10,... | collective-permute-start | bytes 1572872 | tf_op jit(solution)/shard_map/ppermute | solution.py:44
  418.3 25.6 %collective-permute-start.53 = (bf16[128,2048]{1,0:T(8,128)(2,1)S(1)}, bf16[128,2048]{1,0:T(8,128)(2,1)S(1)}, u32[]{:S(2)}, u32[]{:S(2)}) collective-permute-start(bf16[128,2048]{1,0:T(8,128)(2,1)S(1)} %pad_maximum_fusion.9), channel_id=1, source_target_pairs={{0,2},{1,3},{2,4},{3,5},{4,6},{5,7},{6,0},{7,1},{8,10},{9,11},{10,... | collective-permute-start | bytes 1572872 | tf_op jit(solution)/shard_map/ppermute | solution.py:44
  418.4 23.8 %collective-permute-start.56 = (bf16[2,256,256]{2,1,0:T(8,128)(2,1)S(1)}, bf16[2,256,256]{2,1,0:T(8,128)(2,1)S(1)}, u32[]{:S(2)}, u32[]{:S(2)}) collective-permute-start(bf16[2,256,256]{2,1,0:T(8,128)(2,1)S(1)} %get-tuple-element.326), channel_id=1, source_target_pairs={{0,2},{1,3},{2,4},{3,5},{4,6},{5,7},{6,0},{7,1},{8,10},{9,11},{10,... | collective-permute-start | bytes 786440 | tf_op jit(solution)/shard_map/ppermute | solution.py:44
  418.7 23.6 %collective-permute-start.57 = (bf16[2,256,256]{2,1,0:T(8,128)(2,1)S(1)}, bf16[2,256,256]{2,1,0:T(8,128)(2,1)S(1)}, u32[]{:S(2)}, u32[]{:S(2)}) collective-permute-start(bf16[2,256,256]{2,1,0:T(8,128)(2,1)S(1)} %get-tuple-element.327), channel_id=1, source_target_pairs={{0,4},{1,5},{2,6},{3,7},{4,0},{5,1},{6,2},{7,3},{8,12},{9,13},{10,... | collective-permute-start | bytes 786440 | tf_op jit(solution)/shard_map/ppermute | solution.py:44
  423.2 19.1 %collective-permute-start.58 = (bf16[2,256,256]{2,1,0:T(8,128)(2,1)S(1)}, bf16[2,256,256]{2,1,0:T(8,128)(2,1)S(1)}, u32[]{:S(2)}, u32[]{:S(2)}) collective-permute-start(bf16[2,256,256]{2,1,0:T(8,128)(2,1)S(1)} %get-tuple-element.325), channel_id=1, source_target_pairs={{0,6},{1,7},{2,0},{3,1},{4,2},{5,3},{6,4},{7,5},{8,14},{9,15},{10,... | collective-permute-start | bytes 786440 | tf_op jit(solution)/shard_map/ppermute | solution.py:44
  452.3 23.8 %all-to-all-start.4 = ((bf16[16,128,256]{2,1,0:T(8,128)(2,1)}), bf16[16,128,256]{2,1,0:T(8,128)(2,1)S(1)}, u32[]{:S(2)}, u32[]{:S(2)}) async-start(bf16[16,128,256]{2,1,0:T(8,128)(2,1)} %bitcast.234), calls=%async_computation.4 | async-start | bytes 2097152 | tf_op jit(solution)/shard_map/all_to_all | solution.py:1036
  456.1 57.0 %all-gather.11.cloned.1.call-start = ((), (), s32[]{:S(2)}) async-start(), calls=%async_computation.10 | async-start | bytes 2654208 | tf_op jit(solution)/shard_map/all_gather | solution.py:1050
  468.0 17.9 %collective-permute-start.60 = (bf16[512,2048]{1,0:T(8,128)(2,1)}, bf16[512,2048]{1,0:T(8,128)(2,1)}, u32[]{:S(2)}, u32[]{:S(2)}) collective-permute-start(bf16[512,2048]{1,0:T(8,128)(2,1)} %convolution_convert_fusion.2), channel_id=1, source_target_pairs={{0,1},{1,0},{2,3},{3,2},{4,5},{5,4},{6,7},{7,6},{8,9},{9,8},{10,11... | collective-permute-start | bytes 6291464 | tf_op jit(solution)/shard_map/ppermute | solution.py:48
  481.4 29.2 %all-to-all-start.5 = ((bf16[16,128,384]{2,1,0:T(8,128)(2,1)}), bf16[16,128,384]{2,1,0:T(8,128)(2,1)}, u32[]{:S(2)}, u32[]{:S(2)}) async-start(bf16[16,128,384]{2,1,0:T(8,128)(2,1)} %bitcast.261), calls=%async_computation.5 | async-start | bytes 3145728 | tf_op jit(solution)/shard_map/all_to_all | solution.py:1041
  485.8 55.0 %all-gather.13.cloned.1.call-start = ((), (), s32[]{:S(2)}) async-start(), calls=%async_computation.11 | async-start | bytes 1769472 | tf_op jit(solution)/shard_map/all_gather | solution.py:1061
  491.9 11.0 %collective-permute-start.62 = (bf16[64,2048]{1,0:T(8,128)(2,1)}, bf16[64,2048]{1,0:T(8,128)(2,1)}, u32[]{:S(2)}, u32[]{:S(2)}) collective-permute-start(bf16[64,2048]{1,0:T(8,128)(2,1)} %get-tuple-element.303), channel_id=1, source_target_pairs={{0,6},{1,7},{2,0},{3,1},{4,2},{5,3},{6,4},{7,5},{8,14},{9,15},{10,... | collective-permute-start | bytes 786440 | tf_op jit(solution)/shard_map/ppermute | solution.py:44
  510.6 12.5 %collective-permute-start.64 = (bf16[128,2048]{1,0:T(8,128)(2,1)}, bf16[128,2048]{1,0:T(8,128)(2,1)S(1)}, u32[]{:S(2)}, u32[]{:S(2)}) collective-permute-start(bf16[128,2048]{1,0:T(8,128)(2,1)} %pad_maximum_fusion.12), channel_id=1, source_target_pairs={{0,6},{1,7},{2,0},{3,1},{4,2},{5,3},{6,4},{7,5},{8,14},{9,15},{10,... | collective-permute-start | bytes 1572872 | tf_op jit(solution)/shard_map/ppermute | solution.py:44
  512.8 13.6 %collective-permute-start.63 = (bf16[128,2048]{1,0:T(8,128)(2,1)}, bf16[128,2048]{1,0:T(8,128)(2,1)S(1)}, u32[]{:S(2)}, u32[]{:S(2)}) collective-permute-start(bf16[128,2048]{1,0:T(8,128)(2,1)} %pad_maximum_fusion.11), channel_id=1, source_target_pairs={{0,2},{1,3},{2,4},{3,5},{4,6},{5,7},{6,0},{7,1},{8,10},{9,11},{10,... | collective-permute-start | bytes 1572872 | tf_op jit(solution)/shard_map/ppermute | solution.py:44
  (96 other events, 672.4 us)
Sparse Core Ops, SparseCore 0:
  12.4 51.9 all-gather.6
  67.2 159.6 all-gather.8
  289.8 159.8 reduce-scatter.1
  477.9 24.5 all-gather.10
  516.1 22.0 all-gather.12

commit v3 on v2

--- a/solution.py
+++ b/solution.py
@@ -1023,12 +1023,12 @@
 
     sent_back, out_mine, out_other = mix_back(owners, back_pieces, w_out_own, mixed, small)
     grad_head = lax.all_to_all(sent_back, "fsdp", split_axis=0, concat_axis=0, tiled=True)
-    result_other, out_other, _ = together(result_other, out_other, sent_back)
-    result_got, out_got = swap_core(result_other), swap_core(out_other)
-    grad_head, result_got, out_got = together(grad_head, result_got, out_got)
     grads_head, small_sums = attend_back(qkv, grad_head, log_total, seg_row, seg_blocks, cos_all, sin_back)
     grads_qkv = lax.all_to_all(grads_head, "fsdp", split_axis=0, concat_axis=0, tiled=True)
-    out_grads = gather_out(source_owners(expert), exchange(out_mine, out_got))
+    result_other, result_mine, _ = together(result_other, result_mine, sent_back)
+    result_got = swap_core(result_other)
+    result_got, out_mine, out_other = together(result_got, out_mine, out_other)
+    out_grads = gather_out(source_owners(expert), exchange(out_mine, swap_core(out_other)))
     result_own, to_above, to_below = scatter_start(result_mine, result_got)
     result_own = scatter_end(result_own, move_z(to_above, 1), move_z(to_below, -1))
     layer_out = (middle + result_own).astype(low)
@@ -1037,17 +1037,19 @@
 
     grad_query, kv_mine, kv_other = collect(core[None], grads_qkv)
     attn_grads, grad_qkv = qkv_weights(normed_one, grad_query, kv_mine, swap_core(kv_other))
-    attn_grads, out_parts = together(attn_grads, out_parts)
-    attn_parts = lax.all_to_all(attn_grads, "fsdp", split_axis=0, concat_axis=0, tiled=True)
-
     grad_normed_other = mm_t(grad_qkv[half:], qkv_weight).astype(low)
     grad_normed_mine = mm_t(grad_qkv[:half], qkv_weight).astype(low)
+    ffn_sums, _ = together(ffn_sums, grads_qkv)
+    attn_grads, out_parts, grad_normed_other, grad_normed_mine, shared_sums = together(
+        attn_grads, out_parts, grad_normed_other, grad_normed_mine, ffn_sums[:, :base]
+    )
+    attn_parts = lax.all_to_all(attn_grads, "fsdp", split_axis=0, concat_axis=0, tiled=True)
+
     own_grad_one, to_above, to_below = scatter_start(grad_normed_mine, swap_core(grad_normed_other))
     attn_parts, to_above, to_below = together(attn_parts, to_above, to_below)
     own_grad_one = scatter_end(own_grad_one, move_z(to_above, 1), move_z(to_below, -1))
     grad_input = (grad_middle + norm_back(own_hidden, factor_one[:TOK], gain_one, own_grad_one)).astype(low)
-    ffn_sums, _ = together(ffn_sums, attn_grads)
-    shared_shards = lax.all_gather(ffn_sums[:, :base], "expert", axis=0)
+    shared_shards = lax.all_gather(shared_sums, "expert", axis=0)
     attn_parts, shared_shards = together(attn_parts, shared_shards)
     attn_sums = jnp.sum(attn_parts.reshape(FSDP, TOK, 3 * HD).astype(wide), axis=0)
     out_sums = jnp.sum(out_parts.reshape(FSDP, TOK, 256).astype(wide), axis=0)

time: 563 us -> 554 us (0.984)
  the two profiles are of different devices: /device:TPU:0 before, /device:TPU:1 now
where the time goes in v3:
time: 554 us; the launch traced here: 543 us
  waiting for transfers between devices  139 us (25%)
  starting transfers between devices  120 us (22%)
  Pallas kernels  115 us (21%)
  local copies, waits for them, and re-layouts  65 us (12%)
  other arithmetic  48.7 us (9%)
  blocking collectives  24.1 us (4%)
  matrix products  16.5 us (3%)
  between operations  15.7 us (3%)
    ppermute x38, waiting for transfers between devices, move_z(): return lax.ppermute(block, 'expert', shift_pairs(step))  110 us
    pallas_call x1, Pallas kernels, ffn(): pl.pallas_call(ffn_kernel, out_shape=tuple([jax.ShapeDtypeStruct(shape, l...  62.9 us
    ppermute x38, starting transfers between devices, move_z(): return lax.ppermute(block, 'expert', shift_pairs(step))  53.8 us
    ppermute x27, starting transfers between devices, swap_core(): return lax.ppermute(block, 'expert', core_pairs)  41.3 us
    unnamed x139, local copies, waits for them, and re-layouts  30 us
    all_to_all x1, blocking collectives, per_device(): lax.all_to_all(mixed_head, 'fsdp', split_axis=0, concat_axis=0, tiled=True)  24.1 us
    dot_general x10, matrix products, product(): lax.dot_general(left, right, (contract, ((), ())), preferred_element_type...  16.5 us
  transfers between devices with their start and end apart: 75, of which 29 were waited for; matrix products, arithmetic and copies ran while one was open for 18% of the time, Pallas kernels for 9%

profile of v3, /device:TPU:1, one launch (start us, length us, event | category | flops | bytes accessed | tf_op | source)
XLA Modules:
  0.0 543.5 jit_solution(8146719584614777546)
XLA Ops:
  16.3 4.7 collective-permute-start
  20.9 12.0 %collective-permute-done.refs_1_ = bf16[144,2048]{1,0:T(8,128)(2,1)S(1)} collective-permute-done((bf16[144,2048]{1,0:T(8,128)(2,1)S(1)}, bf16[144,2048]{1,0:T(8,128)(2,1)S(1)}, u32[]{:S(2)}, u32[]{:S(2)}) %collective-permute-start) | collective-permute-done | bytes 589856 | tf_op jit(solution)/shard_map/ppermute | solution.py:44
  33.0 3.5 collective-permute-start.3
  39.1 4.8 collective-permute-done.2.refs_2_
  46.7 5.7 %multiply_sine_fusion = (f32[2048,64]{1,0:T(8,128)}, f32[2048,64]{1,0:T(8,128)}, f32[2048,64]{1,0:T(8,128)}) fusion(f32[64]{0:T(128)S(1)} %multiply_power_fusion, f32[2048]{0:T(1024)S(1)} %iota_convert_fusion), kind=kLoop, calls=%fused_computation.24 | loop fusion | flops 262144 | bytes 1581312 | tf_op jit(solution)/shard_map/sin | solution.py:942
  56.5 4.3 pad_maximum_fusion.1
  60.8 4.0 all-gather.7.cloned.1.call-done.refs_10_
  67.8 8.6 %project.1 = (bf16[1024,2048]{1,0:T(8,128)(2,1)}, bf16[2048,384]{1,0:T(8,128)(2,1)S(1)}, f32[1024,1]{1,0:T(8,128)S(1)}, f32[16,2048]{1,0:T(8,128)S(1)}, bf16[128,2048]{1,0:T(8,128)(2,1)S(1)}) custom-call(bf16[144,2048]{1,0:T(8,128)(2,1)S(1)} %fusion.31.refs_0_, bf16[144,2048]{1,0:T(8,128)(2,1)S(1)} %collective-permute-done.refs_1_, ...), custom_call_target="tpu_custom_call" | custom-call | flops 2200000000 | bytes 16000000 | tf_op jit(solution)/shard_map/project/pallas_call | solution.py:305
  79.2 4.9 all-to-all-start
  85.9 3.2 fusion.102
  118.1 3.1 collective-permute-done.13.refs_3_
  132.3 6.6 %attend.1 = (bf16[2048,128]{1,0:T(8,128)(2,1)S(1)}, f32[2048,1]{1,0:T(8,128)S(1)}) custom-call(bf16[2048,384]{1,0:T(8,128)(2,1)S(1)} %bitcast.233, f32[1,2048]{1,0:T(1,128)S(1)} %fusion.117.seg_row_ref, f32[128,128]{1,0:T(8,128)S(1)} %copy-done.20), custom_call_target="tpu_custom_call" | custom-call | flops 1073741824 | bytes 2097152 | tf_op jit(solution)/shard_map/attend/pallas_call | solution.py:226
  138.9 24.1 %all_to_all.68 = bf16[16,128,128]{2,1,0:T(8,128)(2,1)S(1)} all-to-all(bf16[16,128,128]{2,1,0:T(8,128)(2,1)S(1)} %bitcast.239), channel_id=1, replica_groups=mesh['fsdp'=16,'expert'=8] {'fsdp'}, dimensions={0} | all-to-all | bytes 1048576 | tf_op jit(solution)/shard_map/all_to_all | solution.py:991
  166.5 2.8 collective-permute-done.22
  173.1 6.2 %collective-permute-done.23 = bf16[64,2048]{1,0:T(8,128)(2,1)S(1)} collective-permute-done((bf16[64,2048]{1,0:T(8,128)(2,1)S(1)}, bf16[64,2048]{1,0:T(8,128)(2,1)S(1)}, u32[]{:S(2)}, u32[]{:S(2)}) %collective-permute-start.23) | collective-permute-done | bytes 262176 | tf_op jit(solution)/shard_map/ppermute | solution.py:44
  182.0 9.9 %collective-permute-done.26 = bf16[128,2048]{1,0:T(8,128)(2,1)S(1)} collective-permute-done((bf16[128,2048]{1,0:T(8,128)(2,1)S(1)}, bf16[128,2048]{1,0:T(8,128)(2,1)S(1)}, u32[]{:S(2)}, u32[]{:S(2)}) %collective-permute-start.26) | collective-permute-done | bytes 524320 | tf_op jit(solution)/shard_map/ppermute | solution.py:44
  192.0 3.1 collective-permute-done.24
  198.4 3.1 collective-permute-start.31
  201.5 6.5 %collective-permute-done.28.refs_9_ = bf16[128,2048]{1,0:T(8,128)(2,1)S(1)} collective-permute-done((bf16[128,2048]{1,0:T(8,128)(2,1)S(1)}, bf16[128,2048]{1,0:T(8,128)(2,1)S(1)}, u32[]{:S(2)}, u32[]{:S(2)}) %collective-permute-start.28) | collective-permute-done | bytes 524320 | tf_op jit(solution)/shard_map/ppermute | solution.py:44
  208.0 3.4 collective-permute-start.32
  211.5 2.9 collective-permute-start.30
  214.8 4.1 collective-permute-start.33
  223.0 4.6 all-gather.9.cloned.1.call-done.refs_25_
  227.7 62.9 %ffn.1 = (bf16[512,2176]{1,0:T(8,128)(2,1)}, bf16[512,2176]{1,0:T(8,128)(2,1)}, f32[128,128]{1,0:T(8,128)}, bf16[2048,5376]{1,0:T(8,128)(2,1)}, bf16[1024,384]{1...) custom-call(s32[1]{0:T(128)} %bitcast.35.refs_0_, bf16[336,1024]{1,0:T(8,128)(2,1)} %fusion.13.refs_1_, ...), custom_call_target="tpu_custom_call" | custom-call | flops 38000001024 | bytes 70000000 | tf_op jit(solution)/shard_map/ffn/pallas_call | solution.py:727
  291.3 4.2 collective-permute-done.36
  300.6 5.7 %collective-permute-done.39 = bf16[64,2176]{1,0:T(8,128)(2,1)S(1)} collective-permute-done((bf16[64,2176]{1,0:T(8,128)(2,1)S(1)}, bf16[64,2176]{1,0:T(8,128)(2,1)S(1)}, u32[]{:S(2)}, u32[]{:S(2)}) %collective-permute-start.39) | collective-permute-done | bytes 278560 | tf_op jit(solution)/shard_map/ppermute | solution.py:44
  306.3 3.2 collective-permute-done.37
  312.6 11.1 %collective-permute-done.38.first_ref = bf16[128,2176]{1,0:T(8,128)(2,1)S(1)} collective-permute-done((bf16[128,2176]{1,0:T(8,128)(2,1)S(1)}, bf16[128,2176]{1,0:T(8,128)(2,1)S(1)}, u32[]{:S(2)}, u32[]{:S(2)}) %collective-permute-start.38) | collective-permute-done | bytes 557088 | tf_op jit(solution)/shard_map/ppermute | solution.py:44
  323.7 2.8 back_two.1
  356.9 7.1 %mix_back.1 = (bf16[2304,128]{1,0:T(8,128)(2,1)}, bf16[4,256,256]{2,1,0:T(8,128)(2,1)}, bf16[4,256,256]{2,1,0:T(8,128)(2,1)}) custom-call(s32[8]{0:T(128)} %stack.95.place_ref, bf16[128,2048]{1,0:T(8,128)(2,1)} %copy-done.25, bf16[128,2048]{1,0:T(8,128)(2,1)} %collective-permute-done.42.refs_1_, bf16[64,2048]{1,0:T(8,128)(2,1)} %collective-permute-done.43.refs_2_, ...), custom_call_target="tpu_custom_call" | custom-call | flops 2200000000 | bytes 10000000 | tf_op jit(solution)/shard_map/mix_back/pallas_call | solution.py:347
  364.1 4.8 all-to-all-start.2
  368.9 3.3 convert_add_fusion.2
  378.9 8.3 %all-to-all-done.2 = bf16[16,144,128]{2,1,0:T(8,128)(2,1)S(1)} async-done(((bf16[16,144,128]{2,1,0:T(8,128)(2,1)}), bf16[16,144,128]{2,1,0:T(8,128)(2,1)S(1)}, u32[]{:S(2)}, u32[]{:S(2)}) %all-to-all-start.2) | async-done | bytes 589856 | tf_op jit(solution)/shard_map/all_to_all | solution.py:1025
  389.8 10.5 %attend_back.1 = (bf16[2048,384]{1,0:T(8,128)(2,1)S(1)}, f32[16,128]{1,0:T(8,128)S(1)}) custom-call(bf16[2048,384]{1,0:T(8,128)(2,1)} %bitcast.234, bf16[2304,128]{1,0:T(8,128)(2,1)S(1)} %bitcast.238, f32[2048,1]{1,0:T(8,128)S(1)} %copy-done.29, f32[1,2048]{1,0:T(1,128)S(1)} %fusion.117.seg_row_ref, f32[128,128]{1,0:T(8,128)S(1)} %copy-done.21, ...), custom_call_target="tpu_custom_call" | custom-call | flops 2684354560 | bytes 4194304 | tf_op jit(solution)/shard_map/attend_back/pallas_call | solution.py:243
  401.5 3.7 all-to-all-start.3
  409.9 3.2 collective-permute-start.54
  413.4 3.8 collective-permute-start.57
  418.3 20.5 %collective-permute-done.56.refs_2_ = bf16[2,256,256]{2,1,0:T(8,128)(2,1)S(1)} collective-permute-done((bf16[2,256,256]{2,1,0:T(8,128)(2,1)S(1)}, bf16[2,256,256]{2,1,0:T(8,128)(2,1)S(1)}, u32[]{:S(2)}, u32[]{:S(2)}) %collective-permute-start.56) | collective-permute-done | bytes 262176 | tf_op jit(solution)/shard_map/ppermute | solution.py:44
  446.1 6.3 %all-to-all-start.4 = ((bf16[16,128,256]{2,1,0:T(8,128)(2,1)}), bf16[16,128,256]{2,1,0:T(8,128)(2,1)S(1)}, u32[]{:S(2)}, u32[]{:S(2)}) async-start(bf16[16,128,256]{2,1,0:T(8,128)(2,1)} %bitcast.232), calls=%async_computation.4 | async-start | bytes 2097152 | tf_op jit(solution)/shard_map/all_to_all | solution.py:1036
  453.1 7.5 %qkv_weights.1 = (bf16[2048,384]{1,0:T(8,128)(2,1)}, bf16[1024,384]{1,0:T(8,128)(2,1)}) custom-call(bf16[1024,2048]{1,0:T(8,128)(2,1)} %get-tuple-element.195.normed_hbm, bf16[1024,256]{1,0:T(8,128)(2,1)} %copy-done.26, f32[1024,128]{1,0:T(8,128)} %copy-done.27, bf16[1024,128]{1,0:T(8,128)(2,1)} %copy-done.65), custom_call_target="tpu_custom_call" | custom-call | flops 1600000000 | bytes 8000000 | tf_op jit(solution)/shard_map/qkv_weights/pallas_call | solution.py:428
  460.6 3.8 convolution_convert_fusion.3
  471.4 4.6 all-to-all-start.5
  476.1 3.1 convert_add_fusion.1
  484.0 11.6 %collective-permute-done.62 = bf16[64,2048]{1,0:T(8,128)(2,1)} collective-permute-done((bf16[64,2048]{1,0:T(8,128)(2,1)}, bf16[64,2048]{1,0:T(8,128)(2,1)}, u32[]{:S(2)}, u32[]{:S(2)}) %collective-permute-start.62) | collective-permute-done | bytes 262176 | tf_op jit(solution)/shard_map/ppermute | solution.py:44
  506.6 2.8 fusion.spread_ref
  514.4 2.8 collective-permute-done.63
  524.7 4.6 finish_dense.1
  529.4 2.8 all-gather.13.cloned.1.call-done
  (397 shorter events, 187.0 us)
Async XLA Ops:
  7.2 57.6 %all-gather.7.cloned.1.call-start = ((), (), s32[]{:S(2)}) async-start(), calls=%async_computation.7 | async-start | bytes 3899392 | tf_op jit(solution)/shard_map/all_gather | solution.py:896
  12.3 215.3 %all-gather.9.cloned.1.call-start = ((), (), s32[]{:S(2)}) async-start(), calls=%async_computation.8 | async-start | bytes 23396352 | tf_op jit(solution)/shard_map/all_gather | solution.py:926
  16.3 16.7 %collective-permute-start = (bf16[144,2048]{1,0:T(8,128)(2,1)S(1)}, bf16[144,2048]{1,0:T(8,128)(2,1)S(1)}, u32[]{:S(2)}, u32[]{:S(2)}) collective-permute-start(bf16[144,2048]{1,0:T(8,128)(2,1)S(1)} %fusion.31.refs_0_), channel_id=1, source_target_pairs={{0,6},{1,7},{2,0},{3,1},{4,2},{5,3},{6,4},{7,5},{8,14},{9,15},{10,... | collective-permute-start | bytes 1769480 | tf_op jit(solution)/shard_map/ppermute | solution.py:44
  20.9 15.5 %collective-permute-start.1 = (bf16[144,2048]{1,0:T(8,128)(2,1)S(1)}, bf16[144,2048]{1,0:T(8,128)(2,1)S(1)}, u32[]{:S(2)}, u32[]{:S(2)}) collective-permute-start(bf16[144,2048]{1,0:T(8,128)(2,1)S(1)} %fusion.31.refs_0_), channel_id=1, source_target_pairs={{0,2},{1,3},{2,4},{3,5},{4,6},{5,7},{6,0},{7,1},{8,10},{9,11},{10,... | collective-permute-start | bytes 1769480 | tf_op jit(solution)/shard_map/ppermute | solution.py:44
  33.0 13.6 %collective-permute-start.3 = (bf16[80,2048]{1,0:T(8,128)(2,1)S(1)}, bf16[80,2048]{1,0:T(8,128)(2,1)S(1)}, u32[]{:S(2)}, u32[]{:S(2)}) collective-permute-start(bf16[80,2048]{1,0:T(8,128)(2,1)S(1)} %slice.388), channel_id=1, source_target_pairs={{0,6},{1,7},{2,0},{3,1},{4,2},{5,3},{6,4},{7,5},{8,14},{9,15},{10,... | collective-permute-start | bytes 983048 | tf_op jit(solution)/shard_map/ppermute | solution.py:44
  36.6 16.9 %collective-permute-start.4 = (bf16[144,2048]{1,0:T(8,128)(2,1)S(1)}, bf16[144,2048]{1,0:T(8,128)(2,1)S(1)}, u32[]{:S(2)}, u32[]{:S(2)}) collective-permute-start(bf16[144,2048]{1,0:T(8,128)(2,1)S(1)} %fusion.31.refs_0_), channel_id=1, source_target_pairs={{0,1},{1,0},{2,3},{3,2},{4,5},{5,4},{6,7},{7,6},{8,9},{9,8},{10,11... | collective-permute-start | bytes 1769480 | tf_op jit(solution)/shard_map/ppermute | solution.py:48
  38.5 15.0 %collective-permute-start.5 = (bf16[144,2048]{1,0:T(8,128)(2,1)S(1)}, bf16[144,2048]{1,0:T(8,128)(2,1)S(1)}, u32[]{:S(2)}, u32[]{:S(2)}) collective-permute-start(bf16[144,2048]{1,0:T(8,128)(2,1)S(1)} %collective-permute-done.refs_1_), channel_id=1, source_target_pairs={{0,1},{1,0},{2,3},{3,2},{4,5},{5,4},{6,7},{7,6},{8,9},{9,8},{10,11... | collective-permute-start | bytes 1769480 | tf_op jit(solution)/shard_map/ppermute | solution.py:48
  38.6 14.9 %collective-permute-start.8 = (bf16[144,2048]{1,0:T(8,128)(2,1)S(1)}, bf16[144,2048]{1,0:T(8,128)(2,1)}, u32[]{:S(2)}, u32[]{:S(2)}) collective-permute-start(bf16[144,2048]{1,0:T(8,128)(2,1)S(1)} %collective-permute-done.1.refs_4_), channel_id=1, source_target_pairs={{0,1},{1,0},{2,3},{3,2},{4,5},{5,4},{6,7},{7,6},{8,9},{9,8},{10,11... | collective-permute-start | bytes 1769480 | tf_op jit(solution)/shard_map/ppermute | solution.py:48
  53.5 25.7 %collective-permute-start.9 = (bf16[128,2048]{1,0:T(8,128)(2,1)}, bf16[128,2048]{1,0:T(8,128)(2,1)}, u32[]{:S(2)}, u32[]{:S(2)}) collective-permute-start(bf16[128,2048]{1,0:T(8,128)(2,1)} %bitcast.refs_15_.cot_ref), channel_id=1, source_target_pairs={{0,2},{1,3},{2,4},{3,5},{4,6},{5,7},{6,0},{7,1},{8,10},{9,11},{10,... | collective-permute-start | bytes 1572872 | tf_op jit(solution)/shard_map/ppermute | solution.py:44
  53.6 25.6 %collective-permute-start.10 = (bf16[128,2048]{1,0:T(8,128)(2,1)}, bf16[128,2048]{1,0:T(8,128)(2,1)}, u32[]{:S(2)}, u32[]{:S(2)}) collective-permute-start(bf16[128,2048]{1,0:T(8,128)(2,1)} %bitcast.refs_15_.cot_ref), channel_id=1, source_target_pairs={{0,6},{1,7},{2,0},{3,1},{4,2},{5,3},{6,4},{7,5},{8,14},{9,15},{10,... | collective-permute-start | bytes 1572872 | tf_op jit(solution)/shard_map/ppermute | solution.py:44
  79.2 52.2 %all-to-all-start = ((bf16[16,128,384]{2,1,0:T(8,128)(2,1)}), bf16[16,128,384]{2,1,0:T(8,128)(2,1)S(1)}, u32[]{:S(2)}, u32[]{:S(2)}) async-start(bf16[16,128,384]{2,1,0:T(8,128)(2,1)} %bitcast.235), calls=%async_computation | async-start | bytes 3145728 | tf_op jit(solution)/shard_map/all_to_all | solution.py:962
  84.0 383.0 %reduce-scatter.2.cloned.1.call-start = ((), (), s32[]{:S(2)}) async-start(), calls=%async_computation.9 | async-start | bytes 23396352 | tf_op jit(solution)/shard_map/reduce_scatter | solution.py:1010
  90.2 15.8 %collective-permute-start.11 = (bf16[4,256,256]{2,1,0:T(8,128)(2,1)}, bf16[4,256,256]{2,1,0:T(8,128)(2,1)}, u32[]{:S(2)}, u32[]{:S(2)}) collective-permute-start(bf16[4,256,256]{2,1,0:T(8,128)(2,1)} %pad_maximum_fusion.6), channel_id=1, source_target_pairs={{0,1},{1,0},{2,3},{3,2},{4,5},{5,4},{6,7},{7,6},{8,9},{9,8},{10,11... | collective-permute-start | bytes 1572872 | tf_op jit(solution)/shard_map/ppermute | solution.py:48
  99.6 13.3 %collective-permute-start.15 = (bf16[64,2048]{1,0:T(8,128)(2,1)S(1)}, bf16[64,2048]{1,0:T(8,128)(2,1)}, u32[]{:S(2)}, u32[]{:S(2)}) collective-permute-start(bf16[64,2048]{1,0:T(8,128)(2,1)S(1)} %slice.315), channel_id=1, source_target_pairs={{0,2},{1,3},{2,4},{3,5},{4,6},{5,7},{6,0},{7,1},{8,10},{9,11},{10,... | collective-permute-start | bytes 786440 | tf_op jit(solution)/shard_map/ppermute | solution.py:44
  101.9 12.5 %collective-permute-start.16 = (bf16[64,2048]{1,0:T(8,128)(2,1)S(1)}, bf16[64,2048]{1,0:T(8,128)(2,1)}, u32[]{:S(2)}, u32[]{:S(2)}) collective-permute-start(bf16[64,2048]{1,0:T(8,128)(2,1)S(1)} %slice.316), channel_id=1, source_target_pairs={{0,6},{1,7},{2,0},{3,1},{4,2},{5,3},{6,4},{7,5},{8,14},{9,15},{10,... | collective-permute-start | bytes 786440 | tf_op jit(solution)/shard_map/ppermute | solution.py:44
  109.1 12.1 %collective-permute-start.13 = (bf16[2,256,256]{2,1,0:T(8,128)(2,1)S(1)}, bf16[2,256,256]{2,1,0:T(8,128)(2,1)S(1)}, u32[]{:S(2)}, u32[]{:S(2)}) collective-permute-start(bf16[2,256,256]{2,1,0:T(8,128)(2,1)S(1)} %get-tuple-element.336), channel_id=1, source_target_pairs={{0,4},{1,5},{2,6},{3,7},{4,0},{5,1},{6,2},{7,3},{8,12},{9,13},{10,... | collective-permute-start | bytes 786440 | tf_op jit(solution)/shard_map/ppermute | solution.py:44
  112.9 18.4 %collective-permute-start.18 = (bf16[128,2048]{1,0:T(8,128)(2,1)}, bf16[128,2048]{1,0:T(8,128)(2,1)}, u32[]{:S(2)}, u32[]{:S(2)}) collective-permute-start(bf16[128,2048]{1,0:T(8,128)(2,1)} %collective-permute-done.10.refs_16_), channel_id=1, source_target_pairs={{0,1},{1,0},{2,3},{3,2},{4,5},{5,4},{6,7},{7,6},{8,9},{9,8},{10,11... | collective-permute-start | bytes 1572872 | tf_op jit(solution)/shard_map/ppermute | solution.py:48
  114.4 17.0 %collective-permute-start.21 = (bf16[128,2048]{1,0:T(8,128)(2,1)}, bf16[128,2048]{1,0:T(8,128)(2,1)}, u32[]{:S(2)}, u32[]{:S(2)}) collective-permute-start(bf16[128,2048]{1,0:T(8,128)(2,1)} %collective-permute-done.9.refs_19_), channel_id=1, source_target_pairs={{0,1},{1,0},{2,3},{3,2},{4,5},{5,4},{6,7},{7,6},{8,9},{9,8},{10,11... | collective-permute-start | bytes 1572872 | tf_op jit(solution)/shard_map/ppermute | solution.py:48
  115.9 15.4 %collective-permute-start.17 = (bf16[128,2048]{1,0:T(8,128)(2,1)}, bf16[128,2048]{1,0:T(8,128)(2,1)}, u32[]{:S(2)}, u32[]{:S(2)}) collective-permute-start(bf16[128,2048]{1,0:T(8,128)(2,1)} %bitcast.refs_15_.cot_ref), channel_id=1, source_target_pairs={{0,1},{1,0},{2,3},{3,2},{4,5},{5,4},{6,7},{7,6},{8,9},{9,8},{10,11... | collective-permute-start | bytes 1572872 | tf_op jit(solution)/shard_map/ppermute | solution.py:48
  179.5 12.5 %collective-permute-start.26 = (bf16[128,2048]{1,0:T(8,128)(2,1)S(1)}, bf16[128,2048]{1,0:T(8,128)(2,1)S(1)}, u32[]{:S(2)}, u32[]{:S(2)}) collective-permute-start(bf16[128,2048]{1,0:T(8,128)(2,1)S(1)} %pad_maximum_fusion.8), channel_id=1, source_target_pairs={{0,6},{1,7},{2,0},{3,1},{4,2},{5,3},{6,4},{7,5},{8,14},{9,15},{10,... | collective-permute-start | bytes 1572872 | tf_op jit(solution)/shard_map/ppermute | solution.py:44
  181.9 13.1 %collective-permute-start.24 = (bf16[128,2048]{1,0:T(8,128)(2,1)S(1)}, bf16[128,2048]{1,0:T(8,128)(2,1)S(1)}, u32[]{:S(2)}, u32[]{:S(2)}) collective-permute-start(bf16[128,2048]{1,0:T(8,128)(2,1)S(1)} %pad_maximum_fusion.7), channel_id=1, source_target_pairs={{0,2},{1,3},{2,4},{3,5},{4,6},{5,7},{6,0},{7,1},{8,10},{9,11},{10,... | collective-permute-start | bytes 1572872 | tf_op jit(solution)/shard_map/ppermute | solution.py:44
  195.6 12.3 %collective-permute-start.28 = (bf16[128,2048]{1,0:T(8,128)(2,1)S(1)}, bf16[128,2048]{1,0:T(8,128)(2,1)S(1)}, u32[]{:S(2)}, u32[]{:S(2)}) collective-permute-start(bf16[128,2048]{1,0:T(8,128)(2,1)S(1)} %multiply_convert_fusion.refs_5_), channel_id=1, source_target_pairs={{0,2},{1,3},{2,4},{3,5},{4,6},{5,7},{6,0},{7,1},{8,10},{9,11},{10,... | collective-permute-start | bytes 1572872 | tf_op jit(solution)/shard_map/ppermute | solution.py:44
  195.7 12.3 %collective-permute-start.27 = (bf16[128,2048]{1,0:T(8,128)(2,1)S(1)}, bf16[128,2048]{1,0:T(8,128)(2,1)S(1)}, u32[]{:S(2)}, u32[]{:S(2)}) collective-permute-start(bf16[128,2048]{1,0:T(8,128)(2,1)S(1)} %multiply_convert_fusion.refs_5_), channel_id=1, source_target_pairs={{0,6},{1,7},{2,0},{3,1},{4,2},{5,3},{6,4},{7,5},{8,14},{9,15},{10,... | collective-permute-start | bytes 1572872 | tf_op jit(solution)/shard_map/ppermute | solution.py:44
  198.4 22.9 %collective-permute-start.31 = (bf16[128,2048]{1,0:T(8,128)(2,1)S(1)}, bf16[128,2048]{1,0:T(8,128)(2,1)S(1)}, u32[]{:S(2)}, u32[]{:S(2)}) collective-permute-start(bf16[128,2048]{1,0:T(8,128)(2,1)S(1)} %multiply_convert_fusion.refs_5_), channel_id=1, source_target_pairs={{0,1},{1,0},{2,3},{3,2},{4,5},{5,4},{6,7},{7,6},{8,9},{9,8},{10,11... | collective-permute-start | bytes 1572872 | tf_op jit(solution)/shard_map/ppermute | solution.py:48
  208.0 13.3 %collective-permute-start.32 = (bf16[128,2048]{1,0:T(8,128)(2,1)S(1)}, bf16[128,2048]{1,0:T(8,128)(2,1)S(1)}, u32[]{:S(2)}, u32[]{:S(2)}) collective-permute-start(bf16[128,2048]{1,0:T(8,128)(2,1)S(1)} %collective-permute-done.27.refs_6_), channel_id=1, source_target_pairs={{0,1},{1,0},{2,3},{3,2},{4,5},{5,4},{6,7},{7,6},{8,9},{9,8},{10,11... | collective-permute-start | bytes 1572872 | tf_op jit(solution)/shard_map/ppermute | solution.py:48
  309.7 14.1 %collective-permute-start.38 = (bf16[128,2176]{1,0:T(8,128)(2,1)S(1)}, bf16[128,2176]{1,0:T(8,128)(2,1)S(1)}, u32[]{:S(2)}, u32[]{:S(2)}) collective-permute-start(bf16[128,2176]{1,0:T(8,128)(2,1)S(1)} %pad_maximum_fusion.3), channel_id=1, source_target_pairs={{0,2},{1,3},{2,4},{3,5},{4,6},{5,7},{6,0},{7,1},{8,10},{9,11},{10,... | collective-permute-start | bytes 1671176 | tf_op jit(solution)/shard_map/ppermute | solution.py:44
  309.8 14.0 %collective-permute-start.40 = (bf16[128,2176]{1,0:T(8,128)(2,1)S(1)}, bf16[128,2176]{1,0:T(8,128)(2,1)S(1)}, u32[]{:S(2)}, u32[]{:S(2)}) collective-permute-start(bf16[128,2176]{1,0:T(8,128)(2,1)S(1)} %pad_maximum_fusion.4), channel_id=1, source_target_pairs={{0,6},{1,7},{2,0},{3,1},{4,2},{5,3},{6,4},{7,5},{8,14},{9,15},{10,... | collective-permute-start | bytes 1671176 | tf_op jit(solution)/shard_map/ppermute | solution.py:44
  326.5 14.2 %collective-permute-start.41 = (bf16[128,2048]{1,0:T(8,128)(2,1)S(1)}, bf16[128,2048]{1,0:T(8,128)(2,1)}, u32[]{:S(2)}, u32[]{:S(2)}) collective-permute-start(bf16[128,2048]{1,0:T(8,128)(2,1)S(1)} %get-tuple-element.169.refs_0_), channel_id=1, source_target_pairs={{0,2},{1,3},{2,4},{3,5},{4,6},{5,7},{6,0},{7,1},{8,10},{9,11},{10,... | collective-permute-start | bytes 1572872 | tf_op jit(solution)/shard_map/ppermute | solution.py:44
  326.6 14.1 %collective-permute-start.42 = (bf16[128,2048]{1,0:T(8,128)(2,1)S(1)}, bf16[128,2048]{1,0:T(8,128)(2,1)}, u32[]{:S(2)}, u32[]{:S(2)}) collective-permute-start(bf16[128,2048]{1,0:T(8,128)(2,1)S(1)} %get-tuple-element.169.refs_0_), channel_id=1, source_target_pairs={{0,6},{1,7},{2,0},{3,1},{4,2},{5,3},{6,4},{7,5},{8,14},{9,15},{10,... | collective-permute-start | bytes 1572872 | tf_op jit(solution)/shard_map/ppermute | solution.py:44
  329.3 26.9 %collective-permute-start.45 = (bf16[128,2048]{1,0:T(8,128)(2,1)S(1)}, bf16[128,2048]{1,0:T(8,128)(2,1)}, u32[]{:S(2)}, u32[]{:S(2)}) collective-permute-start(bf16[128,2048]{1,0:T(8,128)(2,1)S(1)} %get-tuple-element.169.refs_0_), channel_id=1, source_target_pairs={{0,1},{1,0},{2,3},{3,2},{4,5},{5,4},{6,7},{7,6},{8,9},{9,8},{10,11... | collective-permute-start | bytes 1572872 | tf_op jit(solution)/shard_map/ppermute | solution.py:48
  342.8 13.4 %collective-permute-start.46 = (bf16[128,2048]{1,0:T(8,128)(2,1)}, bf16[128,2048]{1,0:T(8,128)(2,1)S(1)}, u32[]{:S(2)}, u32[]{:S(2)}) collective-permute-start(bf16[128,2048]{1,0:T(8,128)(2,1)} %collective-permute-done.42.refs_1_), channel_id=1, source_target_pairs={{0,1},{1,0},{2,3},{3,2},{4,5},{5,4},{6,7},{7,6},{8,9},{9,8},{10,11... | collective-permute-start | bytes 1572872 | tf_op jit(solution)/shard_map/ppermute | solution.py:48
  364.1 23.2 %all-to-all-start.2 = ((bf16[16,144,128]{2,1,0:T(8,128)(2,1)}), bf16[16,144,128]{2,1,0:T(8,128)(2,1)S(1)}, u32[]{:S(2)}, u32[]{:S(2)}) async-start(bf16[16,144,128]{2,1,0:T(8,128)(2,1)} %bitcast.263), calls=%async_computation.2 | async-start | bytes 1179648 | tf_op jit(solution)/shard_map/all_to_all | solution.py:1025
  375.2 33.1 %collective-permute-start.51 = (bf16[64,2048]{1,0:T(8,128)(2,1)}, bf16[64,2048]{1,0:T(8,128)(2,1)}, u32[]{:S(2)}, u32[]{:S(2)}) collective-permute-start(bf16[64,2048]{1,0:T(8,128)(2,1)} %get-tuple-element.312), channel_id=1, source_target_pairs={{0,2},{1,3},{2,4},{3,5},{4,6},{5,7},{6,0},{7,1},{8,10},{9,11},{10,... | collective-permute-start | bytes 786440 | tf_op jit(solution)/shard_map/ppermute | solution.py:44
  376.7 31.6 %collective-permute-start.53 = (bf16[64,2048]{1,0:T(8,128)(2,1)}, bf16[64,2048]{1,0:T(8,128)(2,1)}, u32[]{:S(2)}, u32[]{:S(2)}) collective-permute-start(bf16[64,2048]{1,0:T(8,128)(2,1)} %get-tuple-element.313), channel_id=1, source_target_pairs={{0,6},{1,7},{2,0},{3,1},{4,2},{5,3},{6,4},{7,5},{8,14},{9,15},{10,... | collective-permute-start | bytes 786440 | tf_op jit(solution)/shard_map/ppermute | solution.py:44
  401.5 41.2 %all-to-all-start.3 = ((bf16[16,128,384]{2,1,0:T(8,128)(2,1)}), bf16[16,128,384]{2,1,0:T(8,128)(2,1)S(1)}, u32[]{:S(2)}, u32[]{:S(2)}) async-start(bf16[16,128,384]{2,1,0:T(8,128)(2,1)} %bitcast.236), calls=%async_computation.3 | async-start | bytes 3145728 | tf_op jit(solution)/shard_map/all_to_all | solution.py:1027
  409.9 30.5 %collective-permute-start.54 = (bf16[128,2048]{1,0:T(8,128)(2,1)S(1)}, bf16[128,2048]{1,0:T(8,128)(2,1)S(1)}, u32[]{:S(2)}, u32[]{:S(2)}) collective-permute-start(bf16[128,2048]{1,0:T(8,128)(2,1)S(1)} %pad_maximum_fusion.10), channel_id=1, source_target_pairs={{0,6},{1,7},{2,0},{3,1},{4,2},{5,3},{6,4},{7,5},{8,14},{9,15},{10,... | collective-permute-start | bytes 1572872 | tf_op jit(solution)/shard_map/ppermute | solution.py:44
  413.1 27.3 %collective-permute-start.52 = (bf16[128,2048]{1,0:T(8,128)(2,1)S(1)}, bf16[128,2048]{1,0:T(8,128)(2,1)S(1)}, u32[]{:S(2)}, u32[]{:S(2)}) collective-permute-start(bf16[128,2048]{1,0:T(8,128)(2,1)S(1)} %pad_maximum_fusion.9), channel_id=1, source_target_pairs={{0,2},{1,3},{2,4},{3,5},{4,6},{5,7},{6,0},{7,1},{8,10},{9,11},{10,... | collective-permute-start | bytes 1572872 | tf_op jit(solution)/shard_map/ppermute | solution.py:44
  413.3 25.5 %collective-permute-start.56 = (bf16[2,256,256]{2,1,0:T(8,128)(2,1)S(1)}, bf16[2,256,256]{2,1,0:T(8,128)(2,1)S(1)}, u32[]{:S(2)}, u32[]{:S(2)}) collective-permute-start(bf16[2,256,256]{2,1,0:T(8,128)(2,1)S(1)} %get-tuple-element.332), channel_id=1, source_target_pairs={{0,2},{1,3},{2,4},{3,5},{4,6},{5,7},{6,0},{7,1},{8,10},{9,11},{10,... | collective-permute-start | bytes 786440 | tf_op jit(solution)/shard_map/ppermute | solution.py:44
  413.4 25.4 %collective-permute-start.57 = (bf16[2,256,256]{2,1,0:T(8,128)(2,1)S(1)}, bf16[2,256,256]{2,1,0:T(8,128)(2,1)S(1)}, u32[]{:S(2)}, u32[]{:S(2)}) collective-permute-start(bf16[2,256,256]{2,1,0:T(8,128)(2,1)S(1)} %get-tuple-element.333), channel_id=1, source_target_pairs={{0,4},{1,5},{2,6},{3,7},{4,0},{5,1},{6,2},{7,3},{8,12},{9,13},{10,... | collective-permute-start | bytes 786440 | tf_op jit(solution)/shard_map/ppermute | solution.py:44
  417.2 21.6 %collective-permute-start.58 = (bf16[2,256,256]{2,1,0:T(8,128)(2,1)S(1)}, bf16[2,256,256]{2,1,0:T(8,128)(2,1)S(1)}, u32[]{:S(2)}, u32[]{:S(2)}) collective-permute-start(bf16[2,256,256]{2,1,0:T(8,128)(2,1)S(1)} %get-tuple-element.331), channel_id=1, source_target_pairs={{0,6},{1,7},{2,0},{3,1},{4,2},{5,3},{6,4},{7,5},{8,14},{9,15},{10,... | collective-permute-start | bytes 786440 | tf_op jit(solution)/shard_map/ppermute | solution.py:44
  446.1 23.9 %all-to-all-start.4 = ((bf16[16,128,256]{2,1,0:T(8,128)(2,1)}), bf16[16,128,256]{2,1,0:T(8,128)(2,1)S(1)}, u32[]{:S(2)}, u32[]{:S(2)}) async-start(bf16[16,128,256]{2,1,0:T(8,128)(2,1)} %bitcast.232), calls=%async_computation.4 | async-start | bytes 2097152 | tf_op jit(solution)/shard_map/all_to_all | solution.py:1036
  452.4 51.4 %all-gather.11.cloned.1.call-start = ((), (), s32[]{:S(2)}) async-start(), calls=%async_computation.10 | async-start | bytes 2654208 | tf_op jit(solution)/shard_map/all_gather | solution.py:1052
  471.4 30.5 %all-to-all-start.5 = ((bf16[16,128,384]{2,1,0:T(8,128)(2,1)}), bf16[16,128,384]{2,1,0:T(8,128)(2,1)}, u32[]{:S(2)}, u32[]{:S(2)}) async-start(bf16[16,128,384]{2,1,0:T(8,128)(2,1)} %bitcast.259), calls=%async_computation.6 | async-start | bytes 3145728 | tf_op jit(solution)/shard_map/all_to_all | solution.py:1046
  476.0 56.2 %all-gather.13.cloned.1.call-start = ((), (), s32[]{:S(2)}) async-start(), calls=%async_computation.11 | async-start | bytes 1769472 | tf_op jit(solution)/shard_map/all_gather | solution.py:1063
  482.1 13.5 %collective-permute-start.62 = (bf16[64,2048]{1,0:T(8,128)(2,1)}, bf16[64,2048]{1,0:T(8,128)(2,1)}, u32[]{:S(2)}, u32[]{:S(2)}) collective-permute-start(bf16[64,2048]{1,0:T(8,128)(2,1)} %get-tuple-element.309), channel_id=1, source_target_pairs={{0,6},{1,7},{2,0},{3,1},{4,2},{5,3},{6,4},{7,5},{8,14},{9,15},{10,... | collective-permute-start | bytes 786440 | tf_op jit(solution)/shard_map/ppermute | solution.py:44
  483.7 14.1 %collective-permute-start.61 = (bf16[64,2048]{1,0:T(8,128)(2,1)}, bf16[64,2048]{1,0:T(8,128)(2,1)}, u32[]{:S(2)}, u32[]{:S(2)}) collective-permute-start(bf16[64,2048]{1,0:T(8,128)(2,1)} %get-tuple-element.311), channel_id=1, source_target_pairs={{0,2},{1,3},{2,4},{3,5},{4,6},{5,7},{6,0},{7,1},{8,10},{9,11},{10,... | collective-permute-start | bytes 786440 | tf_op jit(solution)/shard_map/ppermute | solution.py:44
  501.9 12.5 %collective-permute-start.64 = (bf16[128,2048]{1,0:T(8,128)(2,1)}, bf16[128,2048]{1,0:T(8,128)(2,1)S(1)}, u32[]{:S(2)}, u32[]{:S(2)}) collective-permute-start(bf16[128,2048]{1,0:T(8,128)(2,1)} %pad_maximum_fusion.12), channel_id=1, source_target_pairs={{0,6},{1,7},{2,0},{3,1},{4,2},{5,3},{6,4},{7,5},{8,14},{9,15},{10,... | collective-permute-start | bytes 1572872 | tf_op jit(solution)/shard_map/ppermute | solution.py:44
  503.5 13.6 %collective-permute-start.63 = (bf16[128,2048]{1,0:T(8,128)(2,1)}, bf16[128,2048]{1,0:T(8,128)(2,1)S(1)}, u32[]{:S(2)}, u32[]{:S(2)}) collective-permute-start(bf16[128,2048]{1,0:T(8,128)(2,1)} %pad_maximum_fusion.11), channel_id=1, source_target_pairs={{0,2},{1,3},{2,4},{3,5},{4,6},{5,7},{6,0},{7,1},{8,10},{9,11},{10,... | collective-permute-start | bytes 1572872 | tf_op jit(solution)/shard_map/ppermute | solution.py:44
  (94 other events, 671.0 us)
Sparse Core Ops, SparseCore 0:
  12.4 52.3 all-gather.6
  67.5 160.0 all-gather.8
  290.7 159.1 reduce-scatter.1
  471.5 27.8 all-gather.10
  506.8 25.3 all-gather.12

commit v4 on v3

--- a/solution.py
+++ b/solution.py
@@ -323,9 +323,9 @@
 TALL = TOK + 16
 
 
-def mix_back_kernel(place_ref, *refs):
-    pieces, weight_ref, mixed_ref, small_ref = refs[:10], refs[10], refs[11], refs[12]
-    sent_ref, mine_ref, other_ref, grad_ref, sems = refs[13:]
+def mix_back_kernel(*refs):
+    pieces, weight_ref, small_ref = refs[:10], refs[10], refs[11]
+    sent_ref, grad_ref, sems = refs[12:]
     for index in range(FSDP):
         sent_ref[pl.ds(index * TALL + TOK, 16), :] = small_ref[:, index * TOK : (index + 1) * TOK]
     for copy in load_pieces(pieces, grad_ref, None, sems):
@@ -336,24 +336,39 @@
             for head in range(2):
                 place = pl.ds((index * 4 + 2 * part + head) * TALL, TOK)
                 sent_ref[place, :] = grad[part * TOK : (part + 1) * TOK, head * HD : (head + 1) * HD]
+
+
+def mix_back(pieces, weight, small):
+    return pl.pallas_call(
+        mix_back_kernel,
+        out_shape=(jax.ShapeDtypeStruct((FSDP * TALL, HD), low), jax.ShapeDtypeStruct((ALL, D), low)),
+        in_specs=[anywhere] * 10 + [vmem] * 2,
+        out_specs=(vmem, vmem),
+        scratch_shapes=[pltpu.SemaphoreType.DMA((20,))],
+        compiler_params=params(60),
+        cost_estimate=cost(1.1e9, 10e6),
+        name="mix_back",
+    )(*pieces, weight, small)
+
+
+def out_weights_kernel(place_ref, mixed_ref, grad_ref, mine_ref, other_ref):
     for index in range(EXPERTS):
         columns = pl.ds(pl.multiple_of(place_ref[index] * 256, 256), 256)
         target = mine_ref if index < 4 else other_ref
         target[index % 4] = t_mm(mixed_ref[...], grad_ref[:, columns]).astype(low)
 
 
-def mix_back(owners, pieces, weight, mixed, small):
+def out_weights(owners, mixed, grad):
     blocks = jax.ShapeDtypeStruct((4, 256, 256), low)
     return pl.pallas_call(
-        mix_back_kernel,
-        out_shape=(jax.ShapeDtypeStruct((FSDP * TALL, HD), low), blocks, blocks),
-        in_specs=[smem] + [anywhere] * 10 + [vmem] * 3,
-        out_specs=(vmem, vmem, vmem),
-        scratch_shapes=[pltpu.VMEM((ALL, D), low), pltpu.SemaphoreType.DMA((20,))],
-        compiler_params=params(60),
-        cost_estimate=cost(2.2e9, 10e6),
-        name="mix_back",
-    )(owners, *pieces, weight, mixed, small)
+        out_weights_kernel,
+        out_shape=(blocks, blocks),
+        in_specs=[smem, vmem, vmem],
+        out_specs=(vmem, vmem),
+        compiler_params=params(32),
+        cost_estimate=cost(1.1e9, 6e6),
+        name="out_weights",
+    )(owners, mixed, grad)
 
 
 def collect_kernel(core_ref, grads_ref, query_ref, mine_ref, other_ref):
@@ -1021,18 +1036,19 @@
     below, above, result_other, result_mine, small = together(below, above, result_other, result_mine, small)
     back_pieces = other_pieces(back_block, below, above)
 
-    sent_back, out_mine, out_other = mix_back(owners, back_pieces, w_out_own, mixed, small)
+    sent_back, grad_attn = mix_back(back_pieces, w_out_own, small)
     grad_head = lax.all_to_all(sent_back, "fsdp", split_axis=0, concat_axis=0, tiled=True)
     grads_head, small_sums = attend_back(qkv, grad_head, log_total, seg_row, seg_blocks, cos_all, sin_back)
     grads_qkv = lax.all_to_all(grads_head, "fsdp", split_axis=0, concat_axis=0, tiled=True)
     result_other, result_mine, _ = together(result_other, result_mine, sent_back)
     result_got = swap_core(result_other)
-    result_got, out_mine, out_other = together(result_got, out_mine, out_other)
+    result_got, grad_attn = together(result_got, grad_attn)
+    out_mine, out_other = out_weights(owners, mixed, grad_attn)
     out_grads = gather_out(source_owners(expert), exchange(out_mine, swap_core(out_other)))
     result_own, to_above, to_below = scatter_start(result_mine, result_got)
-    result_own = scatter_end(result_own, move_z(to_above, 1), move_z(to_below, -1))
-    layer_out = (middle + result_own).astype(low)
-    grads_qkv, layer_out, out_grads = together(grads_qkv, layer_out, out_grads)
+    from_below, from_above = move_z(to_above, 1), move_z(to_below, -1)
+    grads_qkv, from_below, from_above, out_grads = together(grads_qkv, from_below, from_above, out_grads)
+    layer_out = (middle + scatter_end(result_own, from_below, from_above)).astype(low)
     out_parts = lax.all_to_all(out_grads, "fsdp", split_axis=0, concat_axis=0, tiled=True)
 
     grad_query, kv_mine, kv_other = collect(core[None], grads_qkv)

time: 554 us -> 565 us (1.020)
  the two profiles are of different devices: /device:TPU:1 before, /device:TPU:0 now
where the time goes in v4:
time: 565 us; the launch traced here: 554 us
  waiting for transfers between devices  179 us (32%)
  Pallas kernels  116 us (21%)
  starting transfers between devices  92.4 us (16%)
  local copies, waits for them, and re-layouts  59.4 us (11%)
  other arithmetic  50.6 us (9%)
  blocking collectives  25 us (4%)
  matrix products  16.5 us (3%)
  between operations  15.8 us (3%)
    ppermute x38, waiting for transfers between devices, move_z(): return lax.ppermute(block, 'expert', shift_pairs(step))  130 us
    ppermute x38, starting transfers between devices, move_z(): return lax.ppermute(block, 'expert', shift_pairs(step))  62.7 us
    pallas_call x1, Pallas kernels, ffn(): pl.pallas_call(ffn_kernel, out_shape=tuple([jax.ShapeDtypeStruct(shape, l...  62.6 us
    unnamed x167, local copies, waits for them, and re-layouts  27.7 us
    all_to_all x1, blocking collectives, per_device(): lax.all_to_all(mixed_head, 'fsdp', split_axis=0, concat_axis=0, tiled=True)  25 us
    all_to_all x1, waiting for transfers between devices, per_device(): lax.all_to_all(sent_back, 'fsdp', split_axis=0, concat_axis=0, tiled=True)  18 us
    dot_general x10, matrix products, product(): lax.dot_general(left, right, (contract, ((), ())), preferred_element_type...  16.5 us
  transfers between devices with their start and end apart: 75, of which 30 were waited for; matrix products, arithmetic and copies ran while one was open for 17% of the time, Pallas kernels for 9%

profile of v4, /device:TPU:0, one launch (start us, length us, event | category | flops | bytes accessed | tf_op | source)
XLA Modules:
  0.0 554.4 jit_solution(9191486194219812012)
XLA Ops:
  16.3 4.2 collective-permute-start
  20.5 12.6 %collective-permute-done.refs_1_ = bf16[144,2048]{1,0:T(8,128)(2,1)S(1)} collective-permute-done((bf16[144,2048]{1,0:T(8,128)(2,1)S(1)}, bf16[144,2048]{1,0:T(8,128)(2,1)S(1)}, u32[]{:S(2)}, u32[]{:S(2)}) %collective-permute-start) | collective-permute-done | bytes 589856 | tf_op jit(solution)/shard_map/ppermute | solution.py:44
  33.8 3.7 collective-permute-start.3
  37.5 5.7 %multiply_sine_fusion = (f32[2048,64]{1,0:T(8,128)}, f32[2048,64]{1,0:T(8,128)}, f32[2048,64]{1,0:T(8,128)}) fusion(f32[64]{0:T(128)S(1)} %multiply_power_fusion, f32[2048]{0:T(1024)S(1)} %iota_convert_fusion), kind=kLoop, calls=%fused_computation.24 | loop fusion | flops 262144 | bytes 1581312 | tf_op jit(solution)/shard_map/sin | solution.py:957
  45.9 6.4 %collective-permute-done.2.refs_2_ = bf16[64,2048]{1,0:T(8,128)(2,1)} collective-permute-done((bf16[64,2048]{1,0:T(8,128)(2,1)}, bf16[64,2048]{1,0:T(8,128)(2,1)}, u32[]{:S(2)}, u32[]{:S(2)}) %collective-permute-start.2) | collective-permute-done | bytes 262176 | tf_op jit(solution)/shard_map/ppermute | solution.py:44
  52.3 4.2 pad_maximum_fusion.1
  59.3 5.1 all-gather.7.cloned.1.call-done.refs_10_
  64.5 3.6 fusion.103
  74.3 8.7 %project.1 = (bf16[1024,2048]{1,0:T(8,128)(2,1)}, bf16[2048,384]{1,0:T(8,128)(2,1)S(1)}, f32[1024,1]{1,0:T(8,128)S(1)}, f32[16,2048]{1,0:T(8,128)S(1)}, bf16[128,2048]{1,0:T(8,128)(2,1)S(1)}) custom-call(bf16[144,2048]{1,0:T(8,128)(2,1)S(1)} %fusion.31.refs_0_, bf16[144,2048]{1,0:T(8,128)(2,1)S(1)} %collective-permute-done.refs_1_, ...), custom_call_target="tpu_custom_call" | custom-call | flops 2200000000 | bytes 16000000 | tf_op jit(solution)/shard_map/project/pallas_call | solution.py:305
  86.4 4.7 all-to-all-start
  115.4 6.8 %collective-permute-done.13.refs_3_ = bf16[2,256,256]{2,1,0:T(8,128)(2,1)S(1)} collective-permute-done((bf16[2,256,256]{2,1,0:T(8,128)(2,1)S(1)}, bf16[2,256,256]{2,1,0:T(8,128)(2,1)S(1)}, u32[]{:S(2)}, u32[]{:S(2)}) %collective-permute-start.13) | collective-permute-done | bytes 262176 | tf_op jit(solution)/shard_map/ppermute | solution.py:44
  129.8 6.6 %attend.1 = (bf16[2048,128]{1,0:T(8,128)(2,1)S(1)}, f32[2048,1]{1,0:T(8,128)S(1)}) custom-call(bf16[2048,384]{1,0:T(8,128)(2,1)S(1)} %bitcast.235, f32[1,2048]{1,0:T(1,128)S(1)} %fusion.118.seg_row_ref, f32[128,128]{1,0:T(8,128)S(1)} %copy-done.25), custom_call_target="tpu_custom_call" | custom-call | flops 1073741824 | bytes 2097152 | tf_op jit(solution)/shard_map/attend/pallas_call | solution.py:226
  136.4 25.0 %all_to_all.68 = bf16[16,128,128]{2,1,0:T(8,128)(2,1)S(1)} all-to-all(bf16[16,128,128]{2,1,0:T(8,128)(2,1)S(1)} %bitcast.241), channel_id=1, replica_groups=mesh['fsdp'=16,'expert'=8] {'fsdp'}, dimensions={0} | all-to-all | bytes 1048576 | tf_op jit(solution)/shard_map/all_to_all | solution.py:1006
  163.5 3.1 collective-permute-done.22
  171.1 6.3 %collective-permute-done.23 = bf16[64,2048]{1,0:T(8,128)(2,1)S(1)} collective-permute-done((bf16[64,2048]{1,0:T(8,128)(2,1)S(1)}, bf16[64,2048]{1,0:T(8,128)(2,1)S(1)}, u32[]{:S(2)}, u32[]{:S(2)}) %collective-permute-start.23) | collective-permute-done | bytes 262176 | tf_op jit(solution)/shard_map/ppermute | solution.py:44
  181.1 11.1 %collective-permute-done.24 = bf16[128,2048]{1,0:T(8,128)(2,1)S(1)} collective-permute-done((bf16[128,2048]{1,0:T(8,128)(2,1)S(1)}, bf16[128,2048]{1,0:T(8,128)(2,1)S(1)}, u32[]{:S(2)}, u32[]{:S(2)}) %collective-permute-start.24) | collective-permute-done | bytes 524320 | tf_op jit(solution)/shard_map/ppermute | solution.py:44
  196.1 10.4 %collective-permute-done.28.refs_9_ = bf16[128,2048]{1,0:T(8,128)(2,1)S(1)} collective-permute-done((bf16[128,2048]{1,0:T(8,128)(2,1)S(1)}, bf16[128,2048]{1,0:T(8,128)(2,1)S(1)}, u32[]{:S(2)}, u32[]{:S(2)}) %collective-permute-start.28) | collective-permute-done | bytes 524320 | tf_op jit(solution)/shard_map/ppermute | solution.py:44
  206.6 3.3 collective-permute-start.30
  210.4 3.7 collective-permute-done.29.refs_7_
  217.1 9.8 %all-gather.9.cloned.1.call-done.refs_25_ = bf16[2048,5376]{1,0:T(8,128)(2,1)} async-done(((bf16[128,5376]{1,0:T(8,128)(2,1)}), bf16[2048,5376]{1,0:T(8,128)(2,1)}) %all-gather.9.cloned.1.call-update) | async-done | bytes 22020112 | tf_op jit(solution)/shard_map/all_gather | solution.py:941
  226.9 62.6 %ffn.1 = (bf16[512,2176]{1,0:T(8,128)(2,1)}, bf16[512,2176]{1,0:T(8,128)(2,1)}, f32[128,128]{1,0:T(8,128)}, bf16[2048,5376]{1,0:T(8,128)(2,1)}, bf16[1024,384]{1...) custom-call(s32[1]{0:T(128)} %bitcast.40.refs_0_, bf16[336,1024]{1,0:T(8,128)(2,1)} %fusion.13.refs_1_, ...), custom_call_target="tpu_custom_call" | custom-call | flops 38000001024 | bytes 70000000 | tf_op jit(solution)/shard_map/ffn/pallas_call | solution.py:742
  289.7 4.5 collective-permute-done.36
  299.9 6.7 %collective-permute-done.37 = bf16[64,2176]{1,0:T(8,128)(2,1)S(1)} collective-permute-done((bf16[64,2176]{1,0:T(8,128)(2,1)S(1)}, bf16[64,2176]{1,0:T(8,128)(2,1)S(1)}, u32[]{:S(2)}, u32[]{:S(2)}) %collective-permute-start.37) | collective-permute-done | bytes 278560 | tf_op jit(solution)/shard_map/ppermute | solution.py:44
  310.1 11.0 %collective-permute-done.40.second_ref = bf16[128,2176]{1,0:T(8,128)(2,1)S(1)} collective-permute-done((bf16[128,2176]{1,0:T(8,128)(2,1)S(1)}, bf16[128,2176]{1,0:T(8,128)(2,1)S(1)}, u32[]{:S(2)}, u32[]{:S(2)}) %collective-permute-start.40) | collective-permute-done | bytes 557088 | tf_op jit(solution)/shard_map/ppermute | solution.py:44
  321.1 3.5 collective-permute-done.38.first_ref
  327.4 3.2 collective-permute-start.42
  340.7 3.3 collective-permute-start.44
  344.5 4.8 collective-permute-done.43.refs_2_
  352.9 5.9 %mix_back.1 = (bf16[2304,128]{1,0:T(8,128)(2,1)}, bf16[1024,2048]{1,0:T(8,128)(2,1)}) custom-call(bf16[128,2048]{1,0:T(8,128)(2,1)} %copy-done.16, bf16[128,2048]{1,0:T(8,128)(2,1)} %copy-done.51, bf16[64,2048]{1,0:T(8,128)(2,1)} %copy-done.65, bf16[64,2048]{1,0:T(8,128)(2,1)} %copy-done.66, bf16[128,2048]{1,0:T(8,128)(2,1)} %copy-done.50, ...), custom_call_target="tpu_custom_call" | custom-call | flops 1100000000 | bytes 10000000 | tf_op jit(solution)/shard_map/mix_back/pallas_call | solution.py:342
  359.1 5.7 %all-to-all-start.2 = ((bf16[16,144,128]{2,1,0:T(8,128)(2,1)}), bf16[16,144,128]{2,1,0:T(8,128)(2,1)S(1)}, u32[]{:S(2)}, u32[]{:S(2)}) async-start(bf16[16,144,128]{2,1,0:T(8,128)(2,1)} %bitcast.265), calls=%async_computation.2 | async-start | bytes 1179648 | tf_op jit(solution)/shard_map/all_to_all | solution.py:1040
  366.3 18.0 %all-to-all-done.2 = bf16[16,144,128]{2,1,0:T(8,128)(2,1)S(1)} async-done(((bf16[16,144,128]{2,1,0:T(8,128)(2,1)}), bf16[16,144,128]{2,1,0:T(8,128)(2,1)S(1)}, u32[]{:S(2)}, u32[]{:S(2)}) %all-to-all-start.2) | async-done | bytes 589856 | tf_op jit(solution)/shard_map/all_to_all | solution.py:1040
  386.8 10.6 %attend_back.1 = (bf16[2048,384]{1,0:T(8,128)(2,1)S(1)}, f32[16,128]{1,0:T(8,128)S(1)}) custom-call(bf16[2048,384]{1,0:T(8,128)(2,1)} %bitcast.236, bf16[2304,128]{1,0:T(8,128)(2,1)S(1)} %bitcast.240, f32[2048,1]{1,0:T(8,128)S(1)} %copy-done.32, f32[1,2048]{1,0:T(1,128)S(1)} %fusion.118.seg_row_ref, f32[128,128]{1,0:T(8,128)S(1)} %copy-done.25, ...), custom_call_target="tpu_custom_call" | custom-call | flops 2684354560 | bytes 4194304 | tf_op jit(solution)/shard_map/attend_back/pallas_call | solution.py:243
  398.6 3.7 all-to-all-start.3
  405.8 3.4 collective-permute-start.53
  411.3 3.1 collective-permute-done.51
  415.3 3.1 collective-permute-start.54
  419.5 4.7 collective-permute-start.57
  424.2 19.3 %collective-permute-done.56.refs_2_ = bf16[2,256,256]{2,1,0:T(8,128)(2,1)S(1)} collective-permute-done((bf16[2,256,256]{2,1,0:T(8,128)(2,1)S(1)}, bf16[2,256,256]{2,1,0:T(8,128)(2,1)S(1)}, u32[]{:S(2)}, u32[]{:S(2)}) %collective-permute-start.56) | collective-permute-done | bytes 262176 | tf_op jit(solution)/shard_map/ppermute | solution.py:44
  447.5 6.5 %all-to-all-start.4 = ((bf16[16,128,256]{2,1,0:T(8,128)(2,1)}), bf16[16,128,256]{2,1,0:T(8,128)(2,1)}, u32[]{:S(2)}, u32[]{:S(2)}) async-start(bf16[16,128,256]{2,1,0:T(8,128)(2,1)} %bitcast.233), calls=%async_computation.4 | async-start | bytes 2097152 | tf_op jit(solution)/shard_map/all_to_all | solution.py:1052
  454.8 7.5 %qkv_weights.1 = (bf16[2048,384]{1,0:T(8,128)(2,1)}, bf16[1024,384]{1,0:T(8,128)(2,1)}) custom-call(bf16[1024,2048]{1,0:T(8,128)(2,1)} %get-tuple-element.197.normed_hbm, bf16[1024,256]{1,0:T(8,128)(2,1)} %copy-done.29, f32[1024,128]{1,0:T(8,128)} %copy-done.30, bf16[1024,128]{1,0:T(8,128)(2,1)} %copy-done.79), custom_call_target="tpu_custom_call" | custom-call | flops 1600000000 | bytes 8000000 | tf_op jit(solution)/shard_map/qkv_weights/pallas_call | solution.py:443
  462.3 3.7 convolution_convert_fusion.2
  472.8 4.8 all-to-all-start.5
  477.7 3.2 convert_add_fusion.1
  484.2 3.4 collective-permute-start.62
  489.1 9.5 %collective-permute-done.61 = bf16[64,2048]{1,0:T(8,128)(2,1)} collective-permute-done((bf16[64,2048]{1,0:T(8,128)(2,1)}, bf16[64,2048]{1,0:T(8,128)(2,1)}, u32[]{:S(2)}, u32[]{:S(2)}) %collective-permute-start.61) | collective-permute-done | bytes 262176 | tf_op jit(solution)/shard_map/ppermute | solution.py:44
  510.2 3.2 collective-permute-start.64
  520.4 10.5 %collective-permute-done.63 = bf16[128,2048]{1,0:T(8,128)(2,1)S(1)} collective-permute-done((bf16[128,2048]{1,0:T(8,128)(2,1)S(1)}, bf16[128,2048]{1,0:T(8,128)(2,1)S(1)}, u32[]{:S(2)}, u32[]{:S(2)}) %collective-permute-start.63) | collective-permute-done | bytes 524320 | tf_op jit(solution)/shard_map/ppermute | solution.py:44
  538.5 4.6 finish_dense.1
  (426 shorter events, 159.5 us)
Async XLA Ops:
  7.2 57.3 %all-gather.7.cloned.1.call-start = ((), (), s32[]{:S(2)}) async-start(), calls=%async_computation.7 | async-start | bytes 3899392 | tf_op jit(solution)/shard_map/all_gather | solution.py:911
  12.3 214.6 %all-gather.9.cloned.1.call-start = ((), (), s32[]{:S(2)}) async-start(), calls=%async_computation.8 | async-start | bytes 23396352 | tf_op jit(solution)/shard_map/all_gather | solution.py:941
  16.3 16.8 %collective-permute-start = (bf16[144,2048]{1,0:T(8,128)(2,1)S(1)}, bf16[144,2048]{1,0:T(8,128)(2,1)S(1)}, u32[]{:S(2)}, u32[]{:S(2)}) collective-permute-start(bf16[144,2048]{1,0:T(8,128)(2,1)S(1)} %fusion.31.refs_0_), channel_id=1, source_target_pairs={{0,6},{1,7},{2,0},{3,1},{4,2},{5,3},{6,4},{7,5},{8,14},{9,15},{10,... | collective-permute-start | bytes 1769480 | tf_op jit(solution)/shard_map/ppermute | solution.py:44
  20.5 22.7 %collective-permute-start.1 = (bf16[144,2048]{1,0:T(8,128)(2,1)S(1)}, bf16[144,2048]{1,0:T(8,128)(2,1)S(1)}, u32[]{:S(2)}, u32[]{:S(2)}) collective-permute-start(bf16[144,2048]{1,0:T(8,128)(2,1)S(1)} %fusion.31.refs_0_), channel_id=1, source_target_pairs={{0,2},{1,3},{2,4},{3,5},{4,6},{5,7},{6,0},{7,1},{8,10},{9,11},{10,... | collective-permute-start | bytes 1769480 | tf_op jit(solution)/shard_map/ppermute | solution.py:44
  20.5 36.0 %collective-permute-start.4 = (bf16[144,2048]{1,0:T(8,128)(2,1)S(1)}, bf16[144,2048]{1,0:T(8,128)(2,1)S(1)}, u32[]{:S(2)}, u32[]{:S(2)}) collective-permute-start(bf16[144,2048]{1,0:T(8,128)(2,1)S(1)} %fusion.31.refs_0_), channel_id=1, source_target_pairs={{0,1},{1,0},{2,3},{3,2},{4,5},{5,4},{6,7},{7,6},{8,9},{9,8},{10,11... | collective-permute-start | bytes 1769480 | tf_op jit(solution)/shard_map/ppermute | solution.py:48
  33.8 11.7 %collective-permute-start.3 = (bf16[80,2048]{1,0:T(8,128)(2,1)}, bf16[80,2048]{1,0:T(8,128)(2,1)S(1)}, u32[]{:S(2)}, u32[]{:S(2)}) collective-permute-start(bf16[80,2048]{1,0:T(8,128)(2,1)} %slice.388), channel_id=1, source_target_pairs={{0,6},{1,7},{2,0},{3,1},{4,2},{5,3},{6,4},{7,5},{8,14},{9,15},{10,... | collective-permute-start | bytes 983048 | tf_op jit(solution)/shard_map/ppermute | solution.py:44
  43.9 13.3 %collective-permute-start.5 = (bf16[144,2048]{1,0:T(8,128)(2,1)S(1)}, bf16[144,2048]{1,0:T(8,128)(2,1)S(1)}, u32[]{:S(2)}, u32[]{:S(2)}) collective-permute-start(bf16[144,2048]{1,0:T(8,128)(2,1)S(1)} %collective-permute-done.refs_1_), channel_id=1, source_target_pairs={{0,1},{1,0},{2,3},{3,2},{4,5},{5,4},{6,7},{7,6},{8,9},{9,8},{10,11... | collective-permute-start | bytes 1769480 | tf_op jit(solution)/shard_map/ppermute | solution.py:48
  43.9 13.3 %collective-permute-start.8 = (bf16[144,2048]{1,0:T(8,128)(2,1)S(1)}, bf16[144,2048]{1,0:T(8,128)(2,1)}, u32[]{:S(2)}, u32[]{:S(2)}) collective-permute-start(bf16[144,2048]{1,0:T(8,128)(2,1)S(1)} %collective-permute-done.1.refs_4_), channel_id=1, source_target_pairs={{0,1},{1,0},{2,3},{3,2},{4,5},{5,4},{6,7},{7,6},{8,9},{9,8},{10,11... | collective-permute-start | bytes 1769480 | tf_op jit(solution)/shard_map/ppermute | solution.py:48
  45.5 11.7 %collective-permute-start.7 = (bf16[80,2048]{1,0:T(8,128)(2,1)S(1)}, bf16[80,2048]{1,0:T(8,128)(2,1)}, u32[]{:S(2)}, u32[]{:S(2)}) collective-permute-start(bf16[80,2048]{1,0:T(8,128)(2,1)S(1)} %collective-permute-done.3.refs_3_), channel_id=1, source_target_pairs={{0,1},{1,0},{2,3},{3,2},{4,5},{5,4},{6,7},{7,6},{8,9},{9,8},{10,11... | collective-permute-start | bytes 983048 | tf_op jit(solution)/shard_map/ppermute | solution.py:48
  57.2 25.8 %collective-permute-start.10 = (bf16[128,2048]{1,0:T(8,128)(2,1)}, bf16[128,2048]{1,0:T(8,128)(2,1)}, u32[]{:S(2)}, u32[]{:S(2)}) collective-permute-start(bf16[128,2048]{1,0:T(8,128)(2,1)} %bitcast.1.refs_15_.cot_ref), channel_id=1, source_target_pairs={{0,6},{1,7},{2,0},{3,1},{4,2},{5,3},{6,4},{7,5},{8,14},{9,15},{10,... | collective-permute-start | bytes 1572872 | tf_op jit(solution)/shard_map/ppermute | solution.py:44
  57.3 25.7 %collective-permute-start.9 = (bf16[128,2048]{1,0:T(8,128)(2,1)}, bf16[128,2048]{1,0:T(8,128)(2,1)}, u32[]{:S(2)}, u32[]{:S(2)}) collective-permute-start(bf16[128,2048]{1,0:T(8,128)(2,1)} %bitcast.1.refs_15_.cot_ref), channel_id=1, source_target_pairs={{0,2},{1,3},{2,4},{3,5},{4,6},{5,7},{6,0},{7,1},{8,10},{9,11},{10,... | collective-permute-start | bytes 1572872 | tf_op jit(solution)/shard_map/ppermute | solution.py:44
  85.0 19.3 %collective-permute-start.11 = (bf16[4,256,256]{2,1,0:T(8,128)(2,1)}, bf16[4,256,256]{2,1,0:T(8,128)(2,1)}, u32[]{:S(2)}, u32[]{:S(2)}) collective-permute-start(bf16[4,256,256]{2,1,0:T(8,128)(2,1)} %pad_maximum_fusion.6), channel_id=1, source_target_pairs={{0,1},{1,0},{2,3},{3,2},{4,5},{5,4},{6,7},{7,6},{8,9},{9,8},{10,11... | collective-permute-start | bytes 1572872 | tf_op jit(solution)/shard_map/ppermute | solution.py:48
  86.4 42.5 %all-to-all-start = ((bf16[16,128,384]{2,1,0:T(8,128)(2,1)}), bf16[16,128,384]{2,1,0:T(8,128)(2,1)S(1)}, u32[]{:S(2)}, u32[]{:S(2)}) async-start(bf16[16,128,384]{2,1,0:T(8,128)(2,1)} %bitcast.237), calls=%async_computation | async-start | bytes 3145728 | tf_op jit(solution)/shard_map/all_to_all | solution.py:977
  91.0 377.7 %reduce-scatter.2.cloned.1.call-start = ((), (), s32[]{:S(2)}) async-start(), calls=%async_computation.9 | async-start | bytes 23396352 | tf_op jit(solution)/shard_map/reduce_scatter | solution.py:1025
  99.9 12.3 %collective-permute-start.15 = (bf16[64,2048]{1,0:T(8,128)(2,1)S(1)}, bf16[64,2048]{1,0:T(8,128)(2,1)}, u32[]{:S(2)}, u32[]{:S(2)}) collective-permute-start(bf16[64,2048]{1,0:T(8,128)(2,1)S(1)} %slice.315), channel_id=1, source_target_pairs={{0,2},{1,3},{2,4},{3,5},{4,6},{5,7},{6,0},{7,1},{8,10},{9,11},{10,... | collective-permute-start | bytes 786440 | tf_op jit(solution)/shard_map/ppermute | solution.py:44
  105.5 9.9 %collective-permute-start.12 = (bf16[2,256,256]{2,1,0:T(8,128)(2,1)S(1)}, bf16[2,256,256]{2,1,0:T(8,128)(2,1)S(1)}, u32[]{:S(2)}, u32[]{:S(2)}) collective-permute-start(bf16[2,256,256]{2,1,0:T(8,128)(2,1)S(1)} %get-tuple-element.337), channel_id=1, source_target_pairs={{0,2},{1,3},{2,4},{3,5},{4,6},{5,7},{6,0},{7,1},{8,10},{9,11},{10,... | collective-permute-start | bytes 786440 | tf_op jit(solution)/shard_map/ppermute | solution.py:44
  107.8 14.3 %collective-permute-start.13 = (bf16[2,256,256]{2,1,0:T(8,128)(2,1)S(1)}, bf16[2,256,256]{2,1,0:T(8,128)(2,1)S(1)}, u32[]{:S(2)}, u32[]{:S(2)}) collective-permute-start(bf16[2,256,256]{2,1,0:T(8,128)(2,1)S(1)} %get-tuple-element.338), channel_id=1, source_target_pairs={{0,4},{1,5},{2,6},{3,7},{4,0},{5,1},{6,2},{7,3},{8,12},{9,13},{10,... | collective-permute-start | bytes 786440 | tf_op jit(solution)/shard_map/ppermute | solution.py:44
  110.8 12.1 %collective-permute-start.14 = (bf16[2,256,256]{2,1,0:T(8,128)(2,1)S(1)}, bf16[2,256,256]{2,1,0:T(8,128)(2,1)S(1)}, u32[]{:S(2)}, u32[]{:S(2)}) collective-permute-start(bf16[2,256,256]{2,1,0:T(8,128)(2,1)S(1)} %get-tuple-element.336), channel_id=1, source_target_pairs={{0,6},{1,7},{2,0},{3,1},{4,2},{5,3},{6,4},{7,5},{8,14},{9,15},{10,... | collective-permute-start | bytes 786440 | tf_op jit(solution)/shard_map/ppermute | solution.py:44
  112.2 16.7 %collective-permute-start.18 = (bf16[128,2048]{1,0:T(8,128)(2,1)}, bf16[128,2048]{1,0:T(8,128)(2,1)}, u32[]{:S(2)}, u32[]{:S(2)}) collective-permute-start(bf16[128,2048]{1,0:T(8,128)(2,1)} %collective-permute-done.10.refs_16_), channel_id=1, source_target_pairs={{0,1},{1,0},{2,3},{3,2},{4,5},{5,4},{6,7},{7,6},{8,9},{9,8},{10,11... | collective-permute-start | bytes 1572872 | tf_op jit(solution)/shard_map/ppermute | solution.py:48
  112.3 16.6 %collective-permute-start.21 = (bf16[128,2048]{1,0:T(8,128)(2,1)}, bf16[128,2048]{1,0:T(8,128)(2,1)}, u32[]{:S(2)}, u32[]{:S(2)}) collective-permute-start(bf16[128,2048]{1,0:T(8,128)(2,1)} %collective-permute-done.9.refs_19_), channel_id=1, source_target_pairs={{0,1},{1,0},{2,3},{3,2},{4,5},{5,4},{6,7},{7,6},{8,9},{9,8},{10,11... | collective-permute-start | bytes 1572872 | tf_op jit(solution)/shard_map/ppermute | solution.py:48
  115.4 13.5 %collective-permute-start.17 = (bf16[128,2048]{1,0:T(8,128)(2,1)}, bf16[128,2048]{1,0:T(8,128)(2,1)}, u32[]{:S(2)}, u32[]{:S(2)}) collective-permute-start(bf16[128,2048]{1,0:T(8,128)(2,1)} %bitcast.1.refs_15_.cot_ref), channel_id=1, source_target_pairs={{0,1},{1,0},{2,3},{3,2},{4,5},{5,4},{6,7},{7,6},{8,9},{9,8},{10,11... | collective-permute-start | bytes 1572872 | tf_op jit(solution)/shard_map/ppermute | solution.py:48
  177.6 14.5 %collective-permute-start.24 = (bf16[128,2048]{1,0:T(8,128)(2,1)S(1)}, bf16[128,2048]{1,0:T(8,128)(2,1)S(1)}, u32[]{:S(2)}, u32[]{:S(2)}) collective-permute-start(bf16[128,2048]{1,0:T(8,128)(2,1)S(1)} %pad_maximum_fusion.7), channel_id=1, source_target_pairs={{0,2},{1,3},{2,4},{3,5},{4,6},{5,7},{6,0},{7,1},{8,10},{9,11},{10,... | collective-permute-start | bytes 1572872 | tf_op jit(solution)/shard_map/ppermute | solution.py:44
  178.6 13.6 %collective-permute-start.26 = (bf16[128,2048]{1,0:T(8,128)(2,1)S(1)}, bf16[128,2048]{1,0:T(8,128)(2,1)S(1)}, u32[]{:S(2)}, u32[]{:S(2)}) collective-permute-start(bf16[128,2048]{1,0:T(8,128)(2,1)S(1)} %pad_maximum_fusion.8), channel_id=1, source_target_pairs={{0,6},{1,7},{2,0},{3,1},{4,2},{5,3},{6,4},{7,5},{8,14},{9,15},{10,... | collective-permute-start | bytes 1572872 | tf_op jit(solution)/shard_map/ppermute | solution.py:44
  192.7 13.7 %collective-permute-start.28 = (bf16[128,2048]{1,0:T(8,128)(2,1)S(1)}, bf16[128,2048]{1,0:T(8,128)(2,1)S(1)}, u32[]{:S(2)}, u32[]{:S(2)}) collective-permute-start(bf16[128,2048]{1,0:T(8,128)(2,1)S(1)} %multiply_convert_fusion.refs_5_), channel_id=1, source_target_pairs={{0,2},{1,3},{2,4},{3,5},{4,6},{5,7},{6,0},{7,1},{8,10},{9,11},{10,... | collective-permute-start | bytes 1572872 | tf_op jit(solution)/shard_map/ppermute | solution.py:44
  193.8 12.8 %collective-permute-start.27 = (bf16[128,2048]{1,0:T(8,128)(2,1)S(1)}, bf16[128,2048]{1,0:T(8,128)(2,1)S(1)}, u32[]{:S(2)}, u32[]{:S(2)}) collective-permute-start(bf16[128,2048]{1,0:T(8,128)(2,1)S(1)} %multiply_convert_fusion.refs_5_), channel_id=1, source_target_pairs={{0,6},{1,7},{2,0},{3,1},{4,2},{5,3},{6,4},{7,5},{8,14},{9,15},{10,... | collective-permute-start | bytes 1572872 | tf_op jit(solution)/shard_map/ppermute | solution.py:44
  196.1 19.0 %collective-permute-start.31 = (bf16[128,2048]{1,0:T(8,128)(2,1)S(1)}, bf16[128,2048]{1,0:T(8,128)(2,1)S(1)}, u32[]{:S(2)}, u32[]{:S(2)}) collective-permute-start(bf16[128,2048]{1,0:T(8,128)(2,1)S(1)} %multiply_convert_fusion.refs_5_), channel_id=1, source_target_pairs={{0,1},{1,0},{2,3},{3,2},{4,5},{5,4},{6,7},{7,6},{8,9},{9,8},{10,11... | collective-permute-start | bytes 1572872 | tf_op jit(solution)/shard_map/ppermute | solution.py:48
  296.6 10.0 %collective-permute-start.37 = (bf16[64,2176]{1,0:T(8,128)(2,1)S(1)}, bf16[64,2176]{1,0:T(8,128)(2,1)S(1)}, u32[]{:S(2)}, u32[]{:S(2)}) collective-permute-start(bf16[64,2176]{1,0:T(8,128)(2,1)S(1)} %get-tuple-element.309), channel_id=1, source_target_pairs={{0,2},{1,3},{2,4},{3,5},{4,6},{5,7},{6,0},{7,1},{8,10},{9,11},{10,... | collective-permute-start | bytes 835592 | tf_op jit(solution)/shard_map/ppermute | solution.py:44
  306.8 14.3 %collective-permute-start.40 = (bf16[128,2176]{1,0:T(8,128)(2,1)S(1)}, bf16[128,2176]{1,0:T(8,128)(2,1)S(1)}, u32[]{:S(2)}, u32[]{:S(2)}) collective-permute-start(bf16[128,2176]{1,0:T(8,128)(2,1)S(1)} %pad_maximum_fusion.4), channel_id=1, source_target_pairs={{0,6},{1,7},{2,0},{3,1},{4,2},{5,3},{6,4},{7,5},{8,14},{9,15},{10,... | collective-permute-start | bytes 1671176 | tf_op jit(solution)/shard_map/ppermute | solution.py:44
  309.9 14.7 %collective-permute-start.38 = (bf16[128,2176]{1,0:T(8,128)(2,1)S(1)}, bf16[128,2176]{1,0:T(8,128)(2,1)S(1)}, u32[]{:S(2)}, u32[]{:S(2)}) collective-permute-start(bf16[128,2176]{1,0:T(8,128)(2,1)S(1)} %pad_maximum_fusion.3), channel_id=1, source_target_pairs={{0,2},{1,3},{2,4},{3,5},{4,6},{5,7},{6,0},{7,1},{8,10},{9,11},{10,... | collective-permute-start | bytes 1671176 | tf_op jit(solution)/shard_map/ppermute | solution.py:44
  327.3 13.2 %collective-permute-start.41 = (bf16[128,2048]{1,0:T(8,128)(2,1)S(1)}, bf16[128,2048]{1,0:T(8,128)(2,1)S(1)}, u32[]{:S(2)}, u32[]{:S(2)}) collective-permute-start(bf16[128,2048]{1,0:T(8,128)(2,1)S(1)} %get-tuple-element.170.refs_0_), channel_id=1, source_target_pairs={{0,2},{1,3},{2,4},{3,5},{4,6},{5,7},{6,0},{7,1},{8,10},{9,11},{10,... | collective-permute-start | bytes 1572872 | tf_op jit(solution)/shard_map/ppermute | solution.py:44
  327.4 13.2 %collective-permute-start.42 = (bf16[128,2048]{1,0:T(8,128)(2,1)S(1)}, bf16[128,2048]{1,0:T(8,128)(2,1)S(1)}, u32[]{:S(2)}, u32[]{:S(2)}) collective-permute-start(bf16[128,2048]{1,0:T(8,128)(2,1)S(1)} %get-tuple-element.170.refs_0_), channel_id=1, source_target_pairs={{0,6},{1,7},{2,0},{3,1},{4,2},{5,3},{6,4},{7,5},{8,14},{9,15},{10,... | collective-permute-start | bytes 1572872 | tf_op jit(solution)/shard_map/ppermute | solution.py:44
  330.6 19.2 %collective-permute-start.45 = (bf16[128,2048]{1,0:T(8,128)(2,1)S(1)}, bf16[128,2048]{1,0:T(8,128)(2,1)S(1)}, u32[]{:S(2)}, u32[]{:S(2)}) collective-permute-start(bf16[128,2048]{1,0:T(8,128)(2,1)S(1)} %get-tuple-element.170.refs_0_), channel_id=1, source_target_pairs={{0,1},{1,0},{2,3},{3,2},{4,5},{5,4},{6,7},{7,6},{8,9},{9,8},{10,11... | collective-permute-start | bytes 1572872 | tf_op jit(solution)/shard_map/ppermute | solution.py:48
  358.9 43.4 %collective-permute-start.50 = (bf16[512,2048]{1,0:T(8,128)(2,1)}, bf16[512,2048]{1,0:T(8,128)(2,1)}, u32[]{:S(2)}, u32[]{:S(2)}) collective-permute-start(bf16[512,2048]{1,0:T(8,128)(2,1)} %add_convert_fusion.1), channel_id=1, source_target_pairs={{0,1},{1,0},{2,3},{3,2},{4,5},{5,4},{6,7},{7,6},{8,9},{9,8},{10,11... | collective-permute-start | bytes 6291464 | tf_op jit(solution)/shard_map/ppermute | solution.py:48
  359.1 25.3 %all-to-all-start.2 = ((bf16[16,144,128]{2,1,0:T(8,128)(2,1)}), bf16[16,144,128]{2,1,0:T(8,128)(2,1)S(1)}, u32[]{:S(2)}, u32[]{:S(2)}) async-start(bf16[16,144,128]{2,1,0:T(8,128)(2,1)} %bitcast.265), calls=%async_computation.2 | async-start | bytes 1179648 | tf_op jit(solution)/shard_map/all_to_all | solution.py:1040
  398.6 46.5 %all-to-all-start.3 = ((bf16[16,128,384]{2,1,0:T(8,128)(2,1)}), bf16[16,128,384]{2,1,0:T(8,128)(2,1)S(1)}, u32[]{:S(2)}, u32[]{:S(2)}) async-start(bf16[16,128,384]{2,1,0:T(8,128)(2,1)} %bitcast.238), calls=%async_computation.3 | async-start | bytes 3145728 | tf_op jit(solution)/shard_map/all_to_all | solution.py:1042
  415.3 29.8 %collective-permute-start.54 = (bf16[128,2048]{1,0:T(8,128)(2,1)}, bf16[128,2048]{1,0:T(8,128)(2,1)}, u32[]{:S(2)}, u32[]{:S(2)}) collective-permute-start(bf16[128,2048]{1,0:T(8,128)(2,1)} %pad_maximum_fusion.10), channel_id=1, source_target_pairs={{0,6},{1,7},{2,0},{3,1},{4,2},{5,3},{6,4},{7,5},{8,14},{9,15},{10,... | collective-permute-start | bytes 1572872 | tf_op jit(solution)/shard_map/ppermute | solution.py:44
  419.3 25.8 %collective-permute-start.52 = (bf16[128,2048]{1,0:T(8,128)(2,1)}, bf16[128,2048]{1,0:T(8,128)(2,1)}, u32[]{:S(2)}, u32[]{:S(2)}) collective-permute-start(bf16[128,2048]{1,0:T(8,128)(2,1)} %pad_maximum_fusion.9), channel_id=1, source_target_pairs={{0,2},{1,3},{2,4},{3,5},{4,6},{5,7},{6,0},{7,1},{8,10},{9,11},{10,... | collective-permute-start | bytes 1572872 | tf_op jit(solution)/shard_map/ppermute | solution.py:44
  419.4 24.1 %collective-permute-start.56 = (bf16[2,256,256]{2,1,0:T(8,128)(2,1)S(1)}, bf16[2,256,256]{2,1,0:T(8,128)(2,1)S(1)}, u32[]{:S(2)}, u32[]{:S(2)}) collective-permute-start(bf16[2,256,256]{2,1,0:T(8,128)(2,1)S(1)} %get-tuple-element.334), channel_id=1, source_target_pairs={{0,2},{1,3},{2,4},{3,5},{4,6},{5,7},{6,0},{7,1},{8,10},{9,11},{10,... | collective-permute-start | bytes 786440 | tf_op jit(solution)/shard_map/ppermute | solution.py:44
  419.5 24.0 %collective-permute-start.57 = (bf16[2,256,256]{2,1,0:T(8,128)(2,1)S(1)}, bf16[2,256,256]{2,1,0:T(8,128)(2,1)S(1)}, u32[]{:S(2)}, u32[]{:S(2)}) collective-permute-start(bf16[2,256,256]{2,1,0:T(8,128)(2,1)S(1)} %get-tuple-element.335), channel_id=1, source_target_pairs={{0,4},{1,5},{2,6},{3,7},{4,0},{5,1},{6,2},{7,3},{8,12},{9,13},{10,... | collective-permute-start | bytes 786440 | tf_op jit(solution)/shard_map/ppermute | solution.py:44
  424.2 19.3 %collective-permute-start.58 = (bf16[2,256,256]{2,1,0:T(8,128)(2,1)S(1)}, bf16[2,256,256]{2,1,0:T(8,128)(2,1)S(1)}, u32[]{:S(2)}, u32[]{:S(2)}) collective-permute-start(bf16[2,256,256]{2,1,0:T(8,128)(2,1)S(1)} %get-tuple-element.333), channel_id=1, source_target_pairs={{0,6},{1,7},{2,0},{3,1},{4,2},{5,3},{6,4},{7,5},{8,14},{9,15},{10,... | collective-permute-start | bytes 786440 | tf_op jit(solution)/shard_map/ppermute | solution.py:44
  447.5 25.3 %all-to-all-start.4 = ((bf16[16,128,256]{2,1,0:T(8,128)(2,1)}), bf16[16,128,256]{2,1,0:T(8,128)(2,1)}, u32[]{:S(2)}, u32[]{:S(2)}) async-start(bf16[16,128,256]{2,1,0:T(8,128)(2,1)} %bitcast.233), calls=%async_computation.4 | async-start | bytes 2097152 | tf_op jit(solution)/shard_map/all_to_all | solution.py:1052
  454.1 50.3 %all-gather.11.cloned.1.call-start = ((), (), s32[]{:S(2)}) async-start(), calls=%async_computation.10 | async-start | bytes 2654208 | tf_op jit(solution)/shard_map/all_gather | solution.py:1068
  472.8 31.5 %all-to-all-start.5 = ((bf16[16,128,384]{2,1,0:T(8,128)(2,1)}), bf16[16,128,384]{2,1,0:T(8,128)(2,1)}, u32[]{:S(2)}, u32[]{:S(2)}) async-start(bf16[16,128,384]{2,1,0:T(8,128)(2,1)} %bitcast.261), calls=%async_computation.6 | async-start | bytes 3145728 | tf_op jit(solution)/shard_map/all_to_all | solution.py:1062
  477.6 65.5 %all-gather.13.cloned.1.call-start = ((), (), s32[]{:S(2)}) async-start(), calls=%async_computation.11 | async-start | bytes 1769472 | tf_op jit(solution)/shard_map/all_gather | solution.py:1079
  484.2 14.5 %collective-permute-start.61 = (bf16[64,2048]{1,0:T(8,128)(2,1)}, bf16[64,2048]{1,0:T(8,128)(2,1)}, u32[]{:S(2)}, u32[]{:S(2)}) collective-permute-start(bf16[64,2048]{1,0:T(8,128)(2,1)} %get-tuple-element.313), channel_id=1, source_target_pairs={{0,2},{1,3},{2,4},{3,5},{4,6},{5,7},{6,0},{7,1},{8,10},{9,11},{10,... | collective-permute-start | bytes 786440 | tf_op jit(solution)/shard_map/ppermute | solution.py:44
  484.2 14.5 %collective-permute-start.62 = (bf16[64,2048]{1,0:T(8,128)(2,1)}, bf16[64,2048]{1,0:T(8,128)(2,1)}, u32[]{:S(2)}, u32[]{:S(2)}) collective-permute-start(bf16[64,2048]{1,0:T(8,128)(2,1)} %get-tuple-element.311), channel_id=1, source_target_pairs={{0,6},{1,7},{2,0},{3,1},{4,2},{5,3},{6,4},{7,5},{8,14},{9,15},{10,... | collective-permute-start | bytes 786440 | tf_op jit(solution)/shard_map/ppermute | solution.py:44
  510.1 20.8 %collective-permute-start.63 = (bf16[128,2048]{1,0:T(8,128)(2,1)S(1)}, bf16[128,2048]{1,0:T(8,128)(2,1)S(1)}, u32[]{:S(2)}, u32[]{:S(2)}) collective-permute-start(bf16[128,2048]{1,0:T(8,128)(2,1)S(1)} %copy-done.58), channel_id=1, source_target_pairs={{0,2},{1,3},{2,4},{3,5},{4,6},{5,7},{6,0},{7,1},{8,10},{9,11},{10,... | collective-permute-start | bytes 1572872 | tf_op jit(solution)/shard_map/ppermute | solution.py:44
  510.2 20.7 %collective-permute-start.64 = (bf16[128,2048]{1,0:T(8,128)(2,1)S(1)}, bf16[128,2048]{1,0:T(8,128)(2,1)S(1)}, u32[]{:S(2)}, u32[]{:S(2)}) collective-permute-start(bf16[128,2048]{1,0:T(8,128)(2,1)S(1)} %copy-done.57), channel_id=1, source_target_pairs={{0,6},{1,7},{2,0},{3,1},{4,2},{5,3},{6,4},{7,5},{8,14},{9,15},{10,... | collective-permute-start | bytes 1572872 | tf_op jit(solution)/shard_map/ppermute | solution.py:44
  (108 other events, 730.8 us)
Sparse Core Ops, SparseCore 0:
  12.4 51.9 all-gather.6
  67.2 159.6 all-gather.8
  289.7 156.3 reduce-scatter.1
  472.9 26.6 all-gather.10
  507.3 24.9 all-gather.12
